TPU v7x, 32 devices: a whole 2x2x4 slice. The times are simulated.
32 devices in a mesh: wide: 8 (over z, y), narrow: 4 (over x, core).
Axes of the slice: x: 2, y: 2, z: 4, core: 2. Of those that a mesh axis runs over, the one named last changes fastest.
Arguments:
- word_states: float32 [32, 512, 768], P(('wide', 'narrow')), may hold values from -6 to 6
- entity_states: float32 [32, 128, 768], P(('wide', 'narrow')), may hold values from -6 to 6
- seq_counts: int32 [32, 2], P(('wide', 'narrow')), may hold values from 0 to 512, as said below
- attention_weight: float32 [7, 768, 768], P(None, 'narrow', 'wide')
- expand_weight: float32 [768, 3072], P('narrow', 'wide')
- reduce_weight: float32 [3072, 768], P('narrow', 'wide')
- norm_params: float32 [4, 768], replicated
- moment_attention: float32 [7, 768, 768], P(None, 'narrow', 'wide')
- moment_expand: float32 [768, 3072], P('narrow', 'wide')
- moment_reduce: float32 [3072, 768], P('narrow', 'wide')
- moment_norms: float32 [4, 768], replicated
- square_attention: float32 [7, 768, 768], P(None, 'narrow', 'wide')
- square_expand: float32 [768, 3072], P('narrow', 'wide')
- square_reduce: float32 [3072, 768], P('narrow', 'wide')
- square_norms: float32 [4, 768], replicated
- word_cotangent: float32 [32, 512, 768], P(('wide', 'narrow')), may hold values from -6 to 6
- entity_cotangent: float32 [32, 128, 768], P(('wide', 'narrow')), may hold values from -6 to 6
Outputs:
- word_output: float32 [32, 512, 768], P(('wide', 'narrow'))
- entity_output: float32 [32, 128, 768], P(('wide', 'narrow'))
- word_grad: float32 [32, 512, 768], P(('wide', 'narrow'))
- entity_grad: float32 [32, 128, 768], P(('wide', 'narrow'))
- new_attention: float32 [7, 768, 768], P(None, 'narrow', 'wide')
- new_expand: float32 [768, 3072], P('narrow', 'wide')
- new_reduce: float32 [3072, 768], P('narrow', 'wide')
- new_norms: float32 [4, 768], replicated
- moment_attention_new: float32 [7, 768, 768], P(None, 'narrow', 'wide')
- moment_expand_new: float32 [768, 3072], P('narrow', 'wide')
- moment_reduce_new: float32 [3072, 768], P('narrow', 'wide')
- moment_norms_new: float32 [4, 768], replicated
- square_attention_new: float32 [7, 768, 768], P(None, 'narrow', 'wide')
- square_expand_new: float32 [768, 3072], P('narrow', 'wide')
- square_reduce_new: float32 [3072, 768], P('narrow', 'wide')
- square_norms_new: float32 [4, 768], replicated
- trust_stats: float32 [13, 3], replicated
Inputs may be any that keep to these rules, and one draw needn't show every extreme that they name: seq_counts[s, 0] is 256 to 512 and seq_counts[s, 1] is 0 to 128; some sequence has exactly 512 live words and some exactly 128 live entities.
All inputs are finite; a program needn't handle non-finite values.
Results may differ from a plain program's by a relative error of at most 0.024.
The roundings to bfloat16 on the way count: a program that leaves them out, or rounds other values in their place, can miss the bound.
Values may be sent and summed in bfloat16 or wider, within the bound.
No kernel may reach another device: no remote copies, remote signals or barrier semaphores. Data moves between devices by JAX's collectives and lax.ppermute only.
A program may use at most 192 MiB of HBM per device.

v0:
```python
import jax
import jax.numpy as jnp
from jax import lax
from jax.sharding import PartitionSpec as P

D = 768
HEADS = 12
HEAD = 64
WORDS = 512
ENTS = 128
STEP = 7


eps_norm = 1e-05
adam_eps = 1e-06
matrix_decay = 0.01
learn_rate = 0.5
masked_score = -1e30


def layer_norm(value, gain, shift):
    center = value - jnp.mean(value, axis=-1, keepdims=True)
    spread = jnp.mean(center * center, axis=-1, keepdims=True)
    return center * lax.rsqrt(spread + eps_norm) * gain + shift


def gelu_exact(value):
    return jax.nn.gelu(value, approximate=False)


def split_heads(value):
    return value.reshape(value.shape[0], HEADS, HEAD)


def head_scores(query, key):
    return jnp.einsum(
        "qhd,khd->hqk", split_heads(query), split_heads(key), preferred_element_type=jnp.float32
    )


def dense(left, right):
    return jnp.dot(left, right, preferred_element_type=jnp.float32)


def dense_left(left, right):
    return lax.dot_general(
        left, right, (((0,), (0,)), ((), ())), preferred_element_type=jnp.float32
    )


def dense_right(left, right):
    return lax.dot_general(
        left, right, (((1,), (1,)), ((), ())), preferred_element_type=jnp.float32
    )


def key_live(counts):
    return jnp.concatenate(
        [
            jnp.arange(WORDS, dtype=jnp.int32) < counts[0],
            jnp.arange(ENTS, dtype=jnp.int32) < counts[1],
        ]
    )


def full_scores(word_query, entity_query, keys, counts):
    key_words = keys[:WORDS]
    key_entities = keys[WORDS:]
    upper = jnp.concatenate(
        [head_scores(word_query[0], key_words), head_scores(word_query[1], key_entities)], 2
    )
    lower = jnp.concatenate(
        [head_scores(entity_query[0], key_words), head_scores(entity_query[1], key_entities)], 2
    )
    scores = jnp.concatenate([upper, lower], 1) * HEAD ** (-0.5)
    return jnp.where(key_live(counts)[None, None, :], scores, masked_score)


def forward_one(weights, norms, word_rows, entity_rows, counts):
    attention, expand, shrink = weights
    bf16 = jnp.bfloat16
    hidden = jnp.concatenate([word_rows, entity_rows], 0)
    hidden_low = hidden.astype(bf16)
    keys = dense(hidden_low, attention[4]).astype(bf16)
    values = dense(hidden_low, attention[5]).astype(bf16)
    word_query = jnp.einsum(
        "ld,kde->kle", hidden_low[:WORDS], attention[0:2], preferred_element_type=jnp.float32
    ).astype(bf16)
    entity_query = jnp.einsum(
        "ld,kde->kle", hidden_low[WORDS:], attention[2:4], preferred_element_type=jnp.float32
    ).astype(bf16)
    scores = full_scores(word_query, entity_query, keys, counts)
    top = jnp.max(scores, axis=2, keepdims=True)
    expd = jnp.exp(scores - top)
    total = jnp.sum(expd, axis=2, keepdims=True)
    probs_low = (expd / total).astype(bf16)
    log_total = top + jnp.log(total)
    context = jnp.einsum(
        "hqk,khd->qhd", probs_low, split_heads(values), preferred_element_type=jnp.float32
    )
    context = context.reshape(-1, D).astype(bf16)
    first_sum = hidden + dense(context, attention[6])
    middle = layer_norm(first_sum, norms[0], norms[1])
    middle_low = middle.astype(bf16)
    inner = dense(middle_low, expand)
    activated = gelu_exact(inner).astype(bf16)
    second_sum = middle + dense(activated, shrink)
    result = layer_norm(second_sum, norms[2], norms[3])
    kept = (
        hidden_low,
        word_query,
        entity_query,
        keys,
        values,
        log_total,
        context,
        first_sum,
        middle_low,
        inner,
        activated,
        second_sum,
    )
    return (result, kept)


def backward_one(weights, norms, kept, counts, cotangent):
    attention, expand, shrink = weights
    bf16 = jnp.bfloat16
    scale = HEAD ** (-0.5)
    (
        hidden_low,
        word_query,
        entity_query,
        keys,
        values,
        log_total,
        context,
        first_sum,
        middle_low,
        inner,
        activated,
        second_sum,
    ) = kept
    unused, pull_second = jax.vjp(layer_norm, second_sum, norms[2], norms[3])
    d_second, d_gain_two, d_shift_two = pull_second(cotangent)
    d_ffn_low = d_second.astype(bf16)
    grad_shrink = dense_left(activated, d_ffn_low)
    unused, pull_gelu = jax.vjp(gelu_exact, inner)
    d_inner_low = pull_gelu(dense_right(d_ffn_low, shrink))[0].astype(bf16)
    grad_expand = dense_left(middle_low, d_inner_low)
    d_middle = d_second + dense_right(d_inner_low, expand)
    unused, pull_first = jax.vjp(layer_norm, first_sum, norms[0], norms[1])
    d_first, d_gain_one, d_shift_one = pull_first(d_middle)
    d_out_low = d_first.astype(bf16)
    grad_out = dense_left(context, d_out_low)
    d_context = dense_right(d_out_low, attention[6]).astype(bf16)
    probs = jnp.exp(full_scores(word_query, entity_query, keys, counts) - log_total)
    probs_low = probs.astype(bf16)
    d_probs = head_scores(d_context, values)
    d_values = jnp.einsum(
        "hqk,qhd->khd", probs_low, split_heads(d_context), preferred_element_type=jnp.float32
    )
    d_values = d_values.reshape(-1, D).astype(bf16)
    row_inner = jnp.sum(probs * d_probs, axis=2, keepdims=True)
    d_scores = (probs * (d_probs - row_inner)).astype(bf16)
    key_words = split_heads(keys[:WORDS])
    key_entities = split_heads(keys[WORDS:])

    def back_query(block, key_part):
        return (
            (
                jnp.einsum("hqk,khd->qhd", block, key_part, preferred_element_type=jnp.float32)
                * scale
            )
            .reshape(-1, D)
            .astype(bf16)
        )

    def back_key(block, query):
        return jnp.einsum(
            "hqk,qhd->khd", block, split_heads(query), preferred_element_type=jnp.float32
        )

    upper = d_scores[:, :WORDS]
    lower = d_scores[:, WORDS:]
    dq_word_word = back_query(upper[:, :, :WORDS], key_words)
    dq_word_entity = back_query(upper[:, :, WORDS:], key_entities)
    dq_entity_word = back_query(lower[:, :, :WORDS], key_words)
    dq_entity_entity = back_query(lower[:, :, WORDS:], key_entities)
    dk_words = back_key(upper[:, :, :WORDS], word_query[0]) + back_key(
        lower[:, :, :WORDS], entity_query[0]
    )
    dk_entities = back_key(upper[:, :, WORDS:], word_query[1]) + back_key(
        lower[:, :, WORDS:], entity_query[1]
    )
    d_keys = (jnp.concatenate([dk_words, dk_entities], 0) * scale).reshape(-1, D).astype(bf16)
    word_low = hidden_low[:WORDS]
    entity_low = hidden_low[WORDS:]
    grad_attention = jnp.stack(
        [
            dense_left(word_low, dq_word_word),
            dense_left(word_low, dq_word_entity),
            dense_left(entity_low, dq_entity_word),
            dense_left(entity_low, dq_entity_entity),
            dense_left(hidden_low, d_keys),
            dense_left(hidden_low, d_values),
            grad_out,
        ]
    )
    d_word_low = dense_right(dq_word_word, attention[0]) + dense_right(dq_word_entity, attention[1])
    d_entity_low = dense_right(dq_entity_word, attention[2]) + dense_right(
        dq_entity_entity, attention[3]
    )
    d_hidden = (
        d_first
        + jnp.concatenate([d_word_low, d_entity_low], 0)
        + dense_right(d_keys, attention[4])
        + dense_right(d_values, attention[5])
    )
    grad_norms = jnp.stack([d_gain_one, d_shift_one, d_gain_two, d_shift_two])
    return (d_hidden, (grad_attention, grad_expand, grad_shrink, grad_norms))


def adapt(weight, grad, first, second, decay):
    first = 0.5 * first + 0.5 * grad
    second = 0.5 * second + 0.5 * grad * grad
    fix_first = 1.0 - 0.5**STEP
    fix_second = 1.0 - 0.5**STEP
    update = first / fix_first / (jnp.sqrt(second / fix_second) + adam_eps) + decay * weight
    return (first, second, update)


def shards(
    word_states,
    entity_states,
    seq_counts,
    attention_weight,
    expand_weight,
    reduce_weight,
    norm_params,
    moment_attention,
    moment_expand,
    moment_reduce,
    moment_norms,
    square_attention,
    square_expand,
    square_reduce,
    square_norms,
    word_cotangent,
    entity_cotangent,
):
    bf16 = jnp.bfloat16
    narrow_parts = (
        lax.all_gather(attention_weight.astype(bf16), "wide", axis=2, tiled=True),
        lax.all_gather(expand_weight.astype(bf16), "wide", axis=1, tiled=True),
        lax.all_gather(reduce_weight.astype(bf16), "wide", axis=1, tiled=True),
    )
    weight_local = jnp.concatenate(
        [
            jnp.sum(attention_weight * attention_weight, axis=(1, 2)),
            jnp.sum(expand_weight * expand_weight)[None],
            jnp.sum(reduce_weight * reduce_weight)[None],
        ]
    )
    weight_total = lax.psum(weight_local, ("wide", "narrow"))
    forward_weights = (
        lax.all_gather(narrow_parts[0], "narrow", axis=1, tiled=True),
        lax.all_gather(narrow_parts[1], "narrow", axis=0, tiled=True),
        lax.all_gather(narrow_parts[2], "narrow", axis=0, tiled=True),
    )

    def forward_step(carry, items):
        result, kept = forward_one(forward_weights, norm_params, items[0], items[1], items[2])
        return (carry, (result, kept))

    unused, (results, kept_all) = lax.scan(
        forward_step, jnp.zeros((), jnp.float32), (word_states, entity_states, seq_counts)
    )
    word_output = results[:, :WORDS]
    entity_output = results[:, WORDS:]
    back_weights = (
        lax.all_gather(narrow_parts[0], "narrow", axis=1, tiled=True),
        lax.all_gather(narrow_parts[1], "narrow", axis=0, tiled=True),
        lax.all_gather(narrow_parts[2], "narrow", axis=0, tiled=True),
    )
    cotangent = jnp.concatenate([word_cotangent, entity_cotangent], 1)
    width = back_weights[1].shape[0]
    hidden_units = back_weights[1].shape[1]
    zeros = (
        jnp.zeros((7, width, width), jnp.float32),
        jnp.zeros((width, hidden_units), jnp.float32),
        jnp.zeros((hidden_units, width), jnp.float32),
        jnp.zeros((4, width), jnp.float32),
    )

    def backward_step(totals, items):
        d_hidden, grads = backward_one(back_weights, norm_params, items[0], items[1], items[2])
        return (jax.tree.map(jnp.add, totals, grads), d_hidden)

    local_grads, d_hidden_all = lax.scan(backward_step, zeros, (kept_all, seq_counts, cotangent))
    word_grad = d_hidden_all[:, :WORDS]
    entity_grad = d_hidden_all[:, WORDS:]
    halfway = (
        lax.psum_scatter(
            local_grads[0].astype(jnp.bfloat16), "wide", scatter_dimension=2, tiled=True
        ).astype(jnp.float32),
        lax.psum_scatter(
            local_grads[1].astype(jnp.bfloat16), "wide", scatter_dimension=1, tiled=True
        ).astype(jnp.float32),
        lax.psum_scatter(
            local_grads[2].astype(jnp.bfloat16), "wide", scatter_dimension=1, tiled=True
        ).astype(jnp.float32),
    )
    grads = (
        lax.psum_scatter(
            halfway[0].astype(jnp.bfloat16), "narrow", scatter_dimension=1, tiled=True
        ).astype(jnp.float32),
        lax.psum_scatter(
            halfway[1].astype(jnp.bfloat16), "narrow", scatter_dimension=0, tiled=True
        ).astype(jnp.float32),
        lax.psum_scatter(
            halfway[2].astype(jnp.bfloat16), "narrow", scatter_dimension=0, tiled=True
        ).astype(jnp.float32),
    )
    att_first, att_second, att_update = adapt(
        attention_weight, grads[0], moment_attention, square_attention, matrix_decay
    )
    exp_first, exp_second, exp_update = adapt(
        expand_weight, grads[1], moment_expand, square_expand, matrix_decay
    )
    red_first, red_second, red_update = adapt(
        reduce_weight, grads[2], moment_reduce, square_reduce, matrix_decay
    )
    update_local = jnp.concatenate(
        [
            jnp.sum(att_update * att_update, axis=(1, 2)),
            jnp.sum(exp_update * exp_update)[None],
            jnp.sum(red_update * red_update)[None],
        ]
    )
    norm_grads = lax.psum(local_grads[3], ("wide", "narrow"))
    update_total = lax.psum(update_local, ("wide", "narrow"))
    nrm_first, nrm_second, nrm_update = adapt(
        norm_params, norm_grads, moment_norms, square_norms, 0.0
    )
    weight_norm = jnp.sqrt(
        jnp.concatenate([weight_total, jnp.sum(norm_params * norm_params, axis=1)])
    )
    update_norm = jnp.sqrt(
        jnp.concatenate([update_total, jnp.sum(nrm_update * nrm_update, axis=1)])
    )
    trust = weight_norm / update_norm
    new_attention = attention_weight - learn_rate * trust[0:7, None, None] * att_update
    new_expand = expand_weight - learn_rate * trust[7] * exp_update
    new_reduce = reduce_weight - learn_rate * trust[8] * red_update
    new_norms = norm_params - learn_rate * trust[9:13, None] * nrm_update
    trust_stats = jnp.stack([jnp.log(weight_norm), jnp.log(update_norm), jnp.log(trust)], 1)
    return (
        word_output,
        entity_output,
        word_grad,
        entity_grad,
        new_attention,
        new_expand,
        new_reduce,
        new_norms,
        att_first,
        exp_first,
        red_first,
        nrm_first,
        att_second,
        exp_second,
        red_second,
        nrm_second,
        trust_stats,
    )


def solution(mesh):
    return jax.shard_map(
        shards,
        mesh=mesh,
        in_specs=(
            P(("wide", "narrow"), None, None),
            P(("wide", "narrow"), None, None),
            P(("wide", "narrow"), None),
            P(None, "narrow", "wide"),
            P("narrow", "wide"),
            P("narrow", "wide"),
            P(),
            P(None, "narrow", "wide"),
            P("narrow", "wide"),
            P("narrow", "wide"),
            P(),
            P(None, "narrow", "wide"),
            P("narrow", "wide"),
            P("narrow", "wide"),
            P(),
            P(("wide", "narrow"), None, None),
            P(("wide", "narrow"), None, None),
        ),
        out_specs=(
            P(("wide", "narrow"), None, None),
            P(("wide", "narrow"), None, None),
            P(("wide", "narrow"), None, None),
            P(("wide", "narrow"), None, None),
            P(None, "narrow", "wide"),
            P("narrow", "wide"),
            P("narrow", "wide"),
            P(),
            P(None, "narrow", "wide"),
            P("narrow", "wide"),
            P("narrow", "wide"),
            P(),
            P(None, "narrow", "wide"),
            P("narrow", "wide"),
            P("narrow", "wide"),
            P(),
            P(),
        ),
        check_vma=False,
    )
```

profile of v0, /device:TPU:0, one launch (start us, length us, event | category | flops | bytes accessed | tf_op | source)
XLA Modules:
  0.0 838.8 jit_solution(6601003515121584079)
XLA Ops:
  13.8 60.1 %all-gather.7.cloned.1.call-done = bf16[7,192,768]{1,0,2:T(8,128)(2,1)} async-done(((bf16[7,192,96]{1,0,2:T(8,128)(2,1)}), bf16[7,192,768]{1,0,2:T(8,128)(2,1)}) %all-gather.7.cloned.1.call-update) | async-done | bytes 2064400 | tf_op jit(solution)/shard_map/all_gather | solution.py:254
  74.0 4.8 copy.143
  78.8 37.4 %all-gather.11.cloned.1.call-done = bf16[192,3072]{1,0:T(8,128)(2,1)} async-done(((bf16[192,384]{1,0:T(8,128)(2,1)}), bf16[192,3072]{1,0:T(8,128)(2,1)}) %all-gather.11.cloned.1.call-update) | async-done | bytes 1179664 | tf_op jit(solution)/shard_map/all_gather | solution.py:255
  118.9 39.9 %all-gather.15.cloned.1.call-done = bf16[768,768]{0,1:T(8,128)(2,1)} async-done(((bf16[768,96]{0,1:T(8,128)(2,1)}), bf16[768,768]{0,1:T(8,128)(2,1)}) %all-gather.15.cloned.1.call-update) | async-done | bytes 1179664 | tf_op jit(solution)/shard_map/all_gather | solution.py:256
  159.0 57.7 %all-gather.9.cloned.1.call-done = bf16[7,768,768]{2,1,0:T(8,128)(2,1)} async-done(((bf16[7,192,768]{2,1,0:T(8,128)(2,1)}), bf16[7,768,768]{2,1,0:T(8,128)(2,1)}) %all-gather.9.cloned.1.call-update) | async-done | bytes 8257552 | tf_op jit(solution)/shard_map/all_gather | solution.py:267
  226.7 3.5 fusion.39
  241.5 10.5 %fusion.122 = (f32[12,640]{1,0:T(8,128)S(1)}, f32[12,640,640]{1,2,0:T(8,128)}) fusion(f32[12,128,128]{1,2,0:T(8,128)S(1)} %copy-done.22, f32[12,128,512]{1,2,0:T(8,128)S(1)} %fusion.132, f32[12,512,128]{1,2,0:T(8,128)S(1)} %fusion.131, f32[12,512,512]{1,2,0:T(8,128)S(1)} %fusion.130, pred[640]{0:T(1024)(128)(4,1)S(1)} %pad_add_fusion), kind=kLoop, calls=%fused_computation.203 | loop fusion | flops 29483520 | bytes 39352960 | tf_op jit(solution)/shard_map/while/body/eval_jaxpr/reduce_max | solution.py:93
  251.9 9.4 %fusion.3 = f32[12,640]{1,0:T(8,128)S(1)} fusion(f32[12,640,640]{1,2,0:T(8,128)} %get-tuple-element.237, f32[12,640]{1,0:T(8,128)S(1)} %get-tuple-element.236), kind=kLoop, calls=%fused_computation.9 | loop fusion | flops 9822720 | bytes 19722240 | tf_op jit(solution)/shard_map/while/body/eval_jaxpr/reduce_sum | solution.py:95
  261.4 10.6 %fusion.42 = bf16[12,64,640]{2,1,0:T(8,128)(2,1)S(1)} fusion(bf16[640,12,64]{0,2,1:T(8,128)(2,1)S(1)} %bitcast.208, f32[12,640,640]{1,2,0:T(8,128)} %get-tuple-element.237, f32[12,640]{1,0:T(8,128)S(1)} %fusion.3, f32[12,640]{1,0:T(8,128)S(1)} %get-tuple-element.236), kind=kOutput, calls=%fused_computation.81 | convolution fusion | flops 644382720 | bytes 21688320 | tf_op jit(solution)/shard_map/while/body/eval_jaxpr/hqk,khd->qhd/dot_general | solution.py:98
  272.0 2.7 fusion.128
  275.2 24.1 %multiply_convert_fusion.1 = (bf16[640,3072]{1,0:T(8,128)(2,1)}, f32[640,3072]{1,0:T(8,128)}, f32[640,3072]{1,0:T(8,128)}) fusion(bf16[768,3072]{1,0:T(8,128)(2,1)} %all-gather.13.cloned.1.call-done, f32[640,768]{1,0:T(8,128)S(1)} %get-tuple-element.254, f32[768]{0:T(1024)S(1)} %copy-done.60, f32[768]{0:T(1024)S(1)} %get-tuple-element.215, ...), kind=kOutput, calls=%fused_computation.18 | convolution fusion | flops 3150151680 | bytes 26356736 | tf_op jit(solution)/shard_map/while/body/eval_jaxpr/dot_general | solution.py:42
  299.3 7.1 fusion.129
  310.8 6.0 convolution_convert_fusion
  316.9 10.7 %add_convert_fusion = bf16[640,3072]{1,0:T(8,128)(2,1)S(1)} fusion(f32[640,3072]{1,0:T(8,128)} %get-tuple-element.235, f32[640,3072]{1,0:T(8,128)} %get-tuple-element.255, bf16[3072,768]{0,1:T(8,128)(2,1)} %all-gather.17.cloned.1.call-done, f32[640,768]{1,0:T(8,128)} %copy-done.25, f32[640]{0:T(1024)} %copy-done.64), kind=kOutput, calls=%fused_computation.17 | convolution fusion | flops 3048407040 | bytes 26348032 | tf_op jit(solution)/shard_map/while/body/eval_jaxpr/dot_general | solution.py:52
  329.5 6.2 convolution_convert_fusion.1
  335.8 6.7 copy.184
  342.5 9.3 %multiply_reduce_fusion.2 = (f32[768]{0:T(1024)}, f32[640]{0:T(1024)S(1)}, f32[768]{0:T(1024)}, f32[640,768]{1,0:T(8,128)S(1)}) fusion(f32[640,768]{1,0:T(8,128)} %copy-done.4, f32[640]{0:T(1024)S(1)} %copy-done.56, f32[640]{0:T(1024)S(1)} %broadcast_multiply_fusion.1, f32[768]{0:T(1024)S(1)} %get-tuple-element.215, bf16[640,3072]{1,0:T(8,128)(2,1)} %copy-done.70, ...), kind=kOutput, calls=%fused_computation.53 | convolution fusion | flops 3024811776 | bytes 14568448 | tf_op jit(solution)/shard_map/while/body/eval_jaxpr/dot_general | solution.py:52
  354.0 3.2 convolution_convert_fusion.9
  360.8 22.6 %multiply_convert_fusion = bf16[12,640,640]{1,2,0:T(8,128)(2,1)} fusion(f32[12,640,640]{1,2,0:T(8,128)} %get-tuple-element.237, f32[12,640]{1,0:T(8,128)} %log_add_fusion, bf16[640,12,64]{0,2,1:T(8,128)(2,1)} %bitcast.193, bf16[640,12,64]{0,2,1:T(8,128)(2,1)} %bitcast.207), kind=kOutput, calls=%fused_computation.3 | convolution fusion | flops 1287790720 | bytes 31488000 | tf_op jit(solution)/shard_map/while/body/eval_jaxpr/sub | solution.py:165
  391.0 4.3 multiply_convert_fusion.3
  407.7 10.1 %fusion.43 = bf16[12,64,640]{2,1,0:T(8,128)(2,1)S(1)} fusion(bf16[640,12,64]{0,2,1:T(8,128)(2,1)S(1)} %bitcast.194, f32[12,640,640]{1,2,0:T(8,128)} %get-tuple-element.237, f32[12,640]{1,0:T(8,128)S(1)} %copy-done.49), kind=kOutput, calls=%fused_computation.82 | convolution fusion | flops 639467520 | bytes 21657600 | tf_op jit(solution)/shard_map/while/body/eval_jaxpr/hqk,qhd->khd/dot_general | solution.py:160
  423.2 13.1 %copy.164 = bf16[7,768,768]{1,0,2:T(8,128)(2,1)} copy(bf16[7,768,768]{2,1,0:T(8,128)(2,1)} %fusion.53) | data formatting | bytes 16515072 | tf_op jit(solution)/shard_map/while/body/eval_jaxpr/stack | solution.py:199
  436.9 74.0 %reduce-scatter.21.cloned.1.call-done = bf16[384,768]{1,0:T(8,128)(2,1)} async-done(((bf16[3072,768]{1,0:T(8,128)(2,1)}), bf16[384,768]{1,0:T(8,128)(2,1)}) %reduce-scatter.21.cloned.1.call-update) | async-done | bytes 589840
  527.5 150.1 %reduce-scatter.11.cloned.1.call-done = bf16[7,768,96]{1,0,2:T(8,128)(2,1)} async-done(((bf16[7,768,768]{1,0,2:T(8,128)(2,1)}), bf16[7,768,96]{1,0,2:T(8,128)(2,1)}) %reduce-scatter.11.cloned.1.call-update) | async-done | bytes 1032208 | tf_op jit(solution)/shard_map/reduce_scatter | solution.py:304
  677.7 30.5 %copy.182 = bf16[7,768,96]{0,2,1:T(8,128)(2,1)} copy(bf16[7,768,96]{1,0,2:T(8,128)(2,1)} %reduce-scatter.11.cloned.1.call-done) | data formatting | bytes 2064384
  708.2 23.5 %reshape.379 = bf16[768,672]{1,0:T(8,128)(2,1)} reshape(bf16[768,96,7]{2,1,0:T(8,128)(2,1)} %bitcast.174) | data formatting | bytes 2064384
  738.3 2.7 fusion.28
  748.4 8.4 reduce-scatter.19.cloned.1.call-done
  756.8 12.1 %reshape.380 = bf16[192,96,7]{2,1,0:T(8,128)(2,1)} reshape(bf16[192,672]{1,0:T(8,128)(2,1)} %reduce-scatter.19.cloned.1.call-done) | data formatting | bytes 516096
  768.9 6.4 copy.183
  777.2 2.7 pad_maximum_fusion.3
  779.9 39.7 %all-reduce = (f32[9]{0:T(128)S(1)}, f32[4,768]{1,0:T(4,128)S(1)}, f32[9]{0:T(128)S(1)}) all-reduce(f32[9]{0:T(128)S(1)} %get-tuple-element.259, f32[4,768]{1,0:T(4,128)S(1)} %pad_maximum_fusion.1, f32[9]{0:T(128)S(1)} %get-tuple-element.260), channel_id=1, replica_groups=mesh['wide'=8,'narrow'=4] {'wide','narrow'}, use_global_device_ids=true, to_apply=%region_14.15 | all-reduce | flops 3090 | bytes 24720 | tf_op jit(solution)/shard_map/psum | solution.py:265
  (275 shorter events, 112.0 us)
Async XLA Ops:
  7.2 66.8 %all-gather.7.cloned.1.call-start = ((), (), s32[]{:S(2)}) async-start(), calls=%async_computation.6 | async-start | bytes 3538944 | tf_op jit(solution)/shard_map/all_gather | solution.py:254
  10.3 105.9 %all-gather.11.cloned.1.call-start = ((), (), s32[]{:S(2)}) async-start(), calls=%async_computation.8 | async-start | bytes 1327104 | tf_op jit(solution)/shard_map/all_gather | solution.py:255
  12.0 146.9 %all-gather.15.cloned.1.call-start = ((), (), s32[]{:S(2)}) async-start(), calls=%async_computation.10 | async-start | bytes 1327104 | tf_op jit(solution)/shard_map/all_gather | solution.py:256
  13.7 102.5 %copy-start.66 = (s32[1,2]{1,0:T(1,128)S(1)}, s32[1,2]{1,0:T(1,128)}, u32[]{:S(2)}) copy-start(s32[1,2]{1,0:T(1,128)} %param.19) | copy-start | bytes 28
  13.8 104.4 %copy-start.51 = (f32[4,768]{1,0:T(4,128)S(1)}, f32[4,768]{1,0:T(4,128)}, u32[]{:S(2)}) copy-start(f32[4,768]{1,0:T(4,128)} %param.23) | copy-start | bytes 36868
  13.8 105.1 %copy-start.33 = (f32[1,512,768]{2,1,0:T(8,128)S(1)}, f32[1,512,768]{2,1,0:T(8,128)}, u32[]{:S(2)}) copy-start(f32[1,512,768]{2,1,0:T(8,128)} %param.17) | copy-start | bytes 4718596
  13.8 105.1 %copy-start.42 = (f32[1,128,768]{2,1,0:T(8,128)S(1)}, f32[1,128,768]{2,1,0:T(8,128)}, u32[]{:S(2)}) copy-start(f32[1,128,768]{2,1,0:T(8,128)} %param.18) | copy-start | bytes 1179652
  13.8 202.9 %all-gather.9.cloned.1.call-start = ((), (), s32[]{:S(2)}) async-start(), calls=%async_computation.7 | async-start | bytes 10321920 | tf_op jit(solution)/shard_map/all_gather | solution.py:267
  78.8 196.4 %all-gather.13.cloned.1.call-start = ((), (), s32[]{:S(2)}) async-start(), calls=%async_computation.9 | async-start | bytes 5898240 | tf_op jit(solution)/shard_map/all_gather | solution.py:268
  116.2 183.0 %all-gather.17.cloned.1.call-start = ((), (), s32[]{:S(2)}) async-start(), calls=%async_computation.11 | async-start | bytes 5898240 | tf_op jit(solution)/shard_map/all_gather | solution.py:269
  118.9 107.8 %copy-start.26 = (bf16[640,768]{1,0:T(8,128)(2,1)}, bf16[640,768]{1,0:T(8,128)(2,1)S(1)}, u32[]{:S(2)}) copy-start(bf16[640,768]{1,0:T(8,128)(2,1)S(1)} %fusion.38) | copy-start | bytes 2949124
  158.9 277.4 %reduce-scatter.15.cloned.1.call-start = ((), (), s32[]{:S(2)}) async-start(), calls=%async_computation.14 | async-start | bytes 5308416 | tf_op jit(solution)/shard_map/reduce_scatter | solution.py:310
  225.5 12.2 %copy-start.28 = (bf16[1,128,768]{1,2,0:T(8,128)(2,1)}, bf16[1,128,768]{1,2,0:T(8,128)(2,1)S(1)}, u32[]{:S(2)}) copy-start(bf16[1,128,768]{1,2,0:T(8,128)(2,1)S(1)} %copy.149) | copy-start | bytes 589828
  274.7 24.5 %copy-start.4 = (f32[640,768]{1,0:T(8,128)}, f32[640,768]{1,0:T(8,128)S(1)}, u32[]{:S(2)}) copy-start(f32[640,768]{1,0:T(8,128)S(1)} %get-tuple-element.254) | copy-start | bytes 5898244
  275.1 24.1 %copy-start.55 = (f32[640]{0:T(1024)}, f32[640]{0:T(1024)S(1)}, u32[]{:S(2)}) copy-start(f32[640]{0:T(1024)S(1)} %fusion.104) | copy-start | bytes 7684
  316.8 194.1 %reduce-scatter.21.cloned.1.call-start = ((), (), s32[]{:S(2)}) async-start(), calls=%async_computation.17 | async-start | bytes 5308416
  316.8 12.7 %copy-start.5 = (f32[640,768]{1,0:T(8,128)S(1)}, f32[640,768]{1,0:T(8,128)}, u32[]{:S(2)}) copy-start(f32[640,768]{1,0:T(8,128)} %copy-done.4) | copy-start | bytes 5898244
  316.9 12.7 %copy-start.56 = (f32[640]{0:T(1024)S(1)}, f32[640]{0:T(1024)}, u32[]{:S(2)}) copy-start(f32[640]{0:T(1024)} %copy-done.55) | copy-start | bytes 7684
  316.9 12.7 %copy-start.61 = (f32[768]{0:T(1024)S(1)}, f32[768]{0:T(1024)}, u32[]{:S(2)}) copy-start(f32[768]{0:T(1024)} %get-tuple-element.214) | copy-start | bytes 9220
  342.5 335.2 %reduce-scatter.11.cloned.1.call-start = ((), (), s32[]{:S(2)}) async-start(), calls=%async_computation.12 | async-start | bytes 10616832 | tf_op jit(solution)/shard_map/reduce_scatter | solution.py:304
  385.0 15.6 %copy-start.30 = (bf16[12,64,128]{2,1,0:T(8,128)(2,1)}, bf16[12,64,128]{2,1,0:T(8,128)(2,1)S(1)}, u32[]{:S(2)}) copy-start(bf16[12,64,128]{2,1,0:T(8,128)(2,1)S(1)} %fusion.85) | copy-start | bytes 589828
  388.7 13.4 %slice-start = ((s8[9830400]{0:T(1024)(128)(4,1)}), s8[4194304]{0:T(1024)(128)(4,1)S(1)}, s32[]{:S(2)}) async-start(s8[9830400]{0:T(1024)(128)(4,1)} %bitcast.177), calls=%async_computation.18 | async-start | bytes 8388608
  391.0 11.1 %slice-start.1 = ((s8[9830400]{0:T(1024)(128)(4,1)}), s8[4194304]{0:T(1024)(128)(4,1)S(1)}, s32[]{:S(2)}) async-start(s8[9830400]{0:T(1024)(128)(4,1)} %bitcast.177), calls=%async_computation.19 | async-start | bytes 8388608
  436.3 307.0 %reduce-scatter.17.cloned.1.call-start = ((), (), s32[]{:S(2)}) async-start(), calls=%async_computation.15 | async-start | bytes 737280 | tf_op jit(solution)/shard_map/reduce_scatter | solution.py:321
  436.8 309.0 %reduce-scatter.13.cloned.1.call-start = ((), (), s32[]{:S(2)}) async-start(), calls=%async_computation.13 | async-start | bytes 737280 | tf_op jit(solution)/shard_map/reduce_scatter | solution.py:318
  513.0 243.8 %reduce-scatter.19.cloned.1.call-start = ((), (), s32[]{:S(2)}) async-start(), calls=%async_computation.16 | async-start | bytes 1474560
  708.2 23.6 %copy-start.31 = (bf16[12,64,128]{2,1,0:T(8,128)(2,1)S(1)}, bf16[12,64,128]{2,1,0:T(8,128)(2,1)}, u32[]{:S(2)}) copy-start(bf16[12,64,128]{2,1,0:T(8,128)(2,1)} %copy-done.30) | copy-start | bytes 589828
  748.4 26.8 %copy-start.11 = (f32[7,192,96]{1,0,2:T(8,128)S(1)}, f32[7,192,96]{1,0,2:T(8,128)}, u32[]{:S(2)}) copy-start(f32[7,192,96]{1,0,2:T(8,128)} %copy.167) | copy-start | bytes 1548292
  748.4 26.8 %copy-start.19 = (f32[7,192,96]{1,0,2:T(8,128)S(1)}, f32[7,192,96]{1,0,2:T(8,128)}, u32[]{:S(2)}) copy-start(f32[7,192,96]{1,0,2:T(8,128)} %copy.163) | copy-start | bytes 1548292
  768.8 50.8 %copy-start.52 = (f32[4,768]{1,0:T(4,128)S(1)}, f32[4,768]{1,0:T(4,128)}, u32[]{:S(2)}) copy-start(f32[4,768]{1,0:T(4,128)} %param.23) | copy-start | bytes 36868
  768.8 50.8 %copy-start.58 = (f32[4,768]{1,0:T(4,128)S(1)}, f32[4,768]{1,0:T(4,128)}, u32[]{:S(2)}) copy-start(f32[4,768]{1,0:T(4,128)} %param.27) | copy-start | bytes 36868
  768.8 50.8 %copy-start.59 = (f32[4,768]{1,0:T(4,128)S(1)}, f32[4,768]{1,0:T(4,128)}, u32[]{:S(2)}) copy-start(f32[4,768]{1,0:T(4,128)} %param.31) | copy-start | bytes 36868
  (55 other events, 267.3 us)
Sparse Core Ops, SparseCore 0:
  10.8 63.1 all-gather.6
  76.6 39.5 all-gather.10
  119.0 39.8 all-gather.14
  160.3 56.2 all-gather.8
  218.1 37.4 all-gather.12
  257.0 37.4 all-gather.16
  316.9 95.2 reduce-scatter.14
  415.9 94.9 reduce-scatter.20
  514.4 163.1 reduce-scatter.10
  680.0 21.1 reduce-scatter.16
  704.3 22.0 reduce-scatter.12
  731.9 24.8 reduce-scatter.18
where the time goes:
time: 844 us; the launch traced here: 839 us
  waiting for transfers between devices  428 us (51%)
  matrix products  171 us (20%)
  local copies, waits for them, and re-layouts  133 us (16%)
  other arithmetic  49.2 us (6%)
  blocking collectives  39.7 us (5%)
  between operations  16.8 us (2%)
    reduce_scatter x1, waiting for transfers between devices, shards(): lax.psum_scatter(local_grads[0].astype(jnp.bfloat16), 'wide', scatter_dim...  150 us
    unnamed x162, local copies, waits for them, and re-layouts  98.3 us
    unnamed x14, waiting for transfers between devices  83 us
    all_gather x1, waiting for transfers between devices, shards(): lax.all_gather(attention_weight.astype(bf16), 'wide', axis=2, tiled=True)  60.1 us
    all_gather x1, waiting for transfers between devices, shards(): lax.all_gather(narrow_parts[0], 'narrow', axis=1, tiled=True)  57.7 us
    all_gather x1, waiting for transfers between devices, shards(): lax.all_gather(reduce_weight.astype(bf16), 'wide', axis=1, tiled=True)  39.9 us
    psum x1, blocking collectives, shards(): weight_total = lax.psum(weight_local, ('wide', 'narrow'))  39.7 us
    dot_general x5, matrix products, dense(): return jnp.dot(left, right, preferred_element_type=jnp.float32)  38.2 us
  transfers between devices with their start and end apart: 12, of which 7 were waited for; matrix products, arithmetic and copies ran while one was open for 35% of the time, Pallas kernels for 0%

commit v1 on v0

v1 whole, which is shorter than its diff:
```python
import functools

import jax
import jax.numpy as jnp
from jax import lax
from jax.experimental import pallas as pl
from jax.experimental.pallas import tpu as pltpu
from jax.sharding import PartitionSpec as P

D = 768
FF = 3072
HEADS = 12
HEAD = 64
WORDS = 512
ENTS = 128
ROWS = WORDS + ENTS
STEP = 7

eps_norm = 1e-05
adam_eps = 1e-06
matrix_decay = 0.01
learn_rate = 0.5
masked_score = -1e30

f32 = jnp.float32
bf16 = jnp.bfloat16
NN = (((1,), (0,)), ((), ()))
NT = (((1,), (1,)), ((), ()))
TN = (((0,), (0,)), ((), ()))
VMEM = pl.BlockSpec(memory_space=pltpu.VMEM)
SMEM = pl.BlockSpec(memory_space=pltpu.SMEM)
ANY = pl.BlockSpec(memory_space=pl.ANY)
PARAMS = pltpu.CompilerParams(vmem_limit_bytes=60 * 2**20)


def dot(left, right, dims):
    return lax.dot_general(left, right, dims, preferred_element_type=f32)


def shape(dims, dtype):
    return jax.ShapeDtypeStruct(dims, dtype)


def cost(flops, moved):
    return pl.CostEstimate(flops=flops, bytes_accessed=moved, transcendentals=0)


def away_blocks():
    for core in range(2):
        for outer in range(2):
            for lead in range(2):
                for low in range(2):
                    for high in range(2):
                        yield core, outer, lead, low, high


def places(wide, narrow, second, block):
    core, outer, lead, low, high = block
    x_away, y_away = (outer, lead) if second else (lead, outer)
    w = wide ^ (high * 4 + low * 2 + y_away)
    n = narrow ^ (x_away * 2 + core)
    return w, n


def piece_of(bufs, block):
    core, outer, lead, low, high = block
    return bufs[core * 2 + outer].at[lead, low, high]


def coords():
    return lax.axis_index("wide"), lax.axis_index("narrow")


def start_attention(bufs, second, target, slots, sem):
    wide, narrow = coords()
    for block in away_blocks():
        w, n = places(wide, narrow, second, block)
        row = pl.multiple_of(w * 96 + (n % 2) * 48, 16)
        lane = pl.multiple_of((n // 2) * 384, 128)
        src = piece_of(bufs, block)
        pltpu.make_async_copy(src, target.at[slots, pl.ds(row, 48), pl.ds(lane, 384)], sem).start()


def drain(ref, sem):
    pltpu.make_async_copy(ref, ref, sem).wait()


def prep_kernel(att, exp, red, keep, send, exp_low, red_low, sums):
    narrow = lax.axis_index("narrow")
    core = narrow % 2
    total = []
    for i in range(7):
        value = att[i]
        total.append(jnp.sum(value * value))
        turned = value.T.astype(bf16)
        halves = turned.reshape(2, 48, 192)

        @pl.when(core == 0)
        def _():
            keep[i] = halves[0]
            send[i] = halves[1]

        @pl.when(core == 1)
        def _():
            keep[i] = halves[1]
            send[i] = halves[0]

    value = exp[...]
    total.append(jnp.sum(value * value))
    exp_low[...] = value.astype(bf16)
    value = red[...]
    total.append(jnp.sum(value * value))
    turned = value.T.astype(bf16)
    red_low[0] = turned[:, :384]
    red_low[1] = turned[:, 384:]
    for i in range(9):
        sums[i] = total[i]


def prep(att, exp, red):
    return pl.pallas_call(
        prep_kernel,
        in_specs=[VMEM] * 3,
        out_specs=[VMEM] * 4 + [SMEM],
        out_shape=[
            shape((7, 48, 192), bf16),
            shape((7, 48, 192), bf16),
            shape((192, 384), bf16),
            shape((2, 96, 384), bf16),
            shape((9,), f32),
        ],
        compiler_params=PARAMS,
        name="prep",
    )(att, exp, red)


def project_kv_kernel(fast, word, ent, *refs):
    if fast:
        first, second, refs = refs[:4], refs[4:8], refs[8:]
    else:
        whole, refs = refs[0], refs[1:]
    low, keys, values, target, sem = refs
    if fast:
        start_attention(first, False, target, pl.ds(0, 1), sem)
        start_attention(second, True, target, pl.ds(1, 1), sem)
    else:
        pltpu.make_async_copy(whole.at[pl.ds(4, 2)], target, sem).start()
    low[:WORDS] = word[...].astype(bf16)
    low[WORDS:] = ent[...].astype(bf16)
    drain(target, sem)
    keys[...] = dot(low[...], target[0], NT).astype(bf16)
    values[...] = dot(low[...], target[1], NT).astype(bf16)


def project_kv(fast, word, ent, pieces):
    return pl.pallas_call(
        functools.partial(project_kv_kernel, fast),
        in_specs=[VMEM, VMEM] + [ANY] * len(pieces),
        out_specs=[VMEM] * 4,
        out_shape=[shape((ROWS, D), bf16)] * 3 + [shape((2, D, D), bf16)],
        scratch_shapes=[pltpu.SemaphoreType.DMA],
        compiler_params=PARAMS,
        cost_estimate=cost(2 * ROWS * D * D * 2, 8000000),
        name="project_kv",
    )(word, ent, *pieces)


def project_q_kernel(fast, low, *refs):
    if fast:
        first, second, refs = refs[:4], refs[4:8], refs[8:]
    else:
        whole, refs = refs[0], refs[1:]
    to_words, to_ents, target, sem = refs
    if fast:
        start_attention(first, False, target, pl.ds(0, 2), sem)
        start_attention(second, True, target, pl.ds(2, 2), sem)
    else:
        for slot, k in enumerate((0, 2, 1, 3)):
            pltpu.make_async_copy(whole.at[k], target.at[slot], sem).start()
    drain(target, sem)
    scale = HEAD ** (-0.5)
    word = low[:WORDS]
    ent = low[WORDS:]
    to_words[:WORDS] = (dot(word, target[0], NT) * scale).astype(bf16)
    to_words[WORDS:] = (dot(ent, target[1], NT) * scale).astype(bf16)
    to_ents[:WORDS] = (dot(word, target[2], NT) * scale).astype(bf16)
    to_ents[WORDS:] = (dot(ent, target[3], NT) * scale).astype(bf16)


def project_q(fast, low, pieces):
    return pl.pallas_call(
        functools.partial(project_q_kernel, fast),
        in_specs=[VMEM] + [ANY] * len(pieces),
        out_specs=[VMEM] * 3,
        out_shape=[shape((ROWS, D), bf16)] * 2 + [shape((4, D, D), bf16)],
        scratch_shapes=[pltpu.SemaphoreType.DMA],
        compiler_params=PARAMS,
        cost_estimate=cost(2 * ROWS * D * D * 2, 8000000),
        name="project_q",
    )(low, *pieces)


def head_masks(counts):
    lane = lax.broadcasted_iota(jnp.int32, (ROWS, 128), 1)
    row = lax.broadcasted_iota(jnp.int32, (ROWS, 128), 0)
    edge = jnp.where(row < WORDS, counts[0], counts[1] + WORDS)
    bias = jnp.where(row < edge, 0.0, masked_score)
    out = []
    for h in range(2):
        own = jnp.where((lane < HEAD) if h == 0 else (lane >= HEAD), 1.0, 0.0).astype(bf16)
        mark = jnp.where(lane == (HEAD if h == 0 else 0), 1.0, 0.0)
        rest = (1.0 - mark).astype(bf16)
        tag = (bias * mark).astype(bf16)
        out.append((own, mark.astype(bf16), rest, tag))
    return out


def scores_of(masks, keys, to_words, to_ents):
    own, mark, rest, tag = masks
    tagged = keys * own + tag
    upper = dot(tagged[:WORDS], to_words * rest + mark, NT)
    lower = dot(tagged[WORDS:], to_ents * rest + mark, NT)
    return jnp.concatenate([upper, lower], 0)


def attend_kernel(counts, to_words, to_ents, keys, values, context, exact, lse):
    masks = head_masks(counts)
    outs = []
    for h in range(2):
        scores = scores_of(masks[h], keys[...], to_words[...], to_ents[...])
        top = jnp.max(scores, axis=0, keepdims=True)
        expd = jnp.exp(scores - top)
        total = jnp.sum(expd, axis=0, keepdims=True)
        lse[h : h + 1, :] = top + jnp.log(total)
        mixed = dot(values[:, h * HEAD : (h + 1) * HEAD], expd.astype(bf16), TN)
        outs.append(mixed * (1.0 / total))
    joined = jnp.concatenate(outs, 0).T
    exact[...] = joined
    context[...] = joined.astype(bf16)


def attend(counts, to_words, to_ents, keys, values):
    pair = pl.BlockSpec((ROWS, 128), lambda i: (0, i))
    stat = pl.BlockSpec((None, 2, ROWS), lambda i: (i, 0, 0))
    return pl.pallas_call(
        attend_kernel,
        grid=(HEADS // 2,),
        in_specs=[SMEM, pair, pair, pair, pair],
        out_specs=[pair, pair, stat],
        out_shape=[
            shape((ROWS, D), bf16),
            shape((ROWS, D), f32),
            shape((HEADS // 2, 2, ROWS), f32),
        ],
        compiler_params=PARAMS,
        cost_estimate=cost(8 * ROWS * ROWS * D, 12000000),
        name="attend",
    )(counts, to_words, to_ents, keys, values)


def normed(value):
    center = value - jnp.mean(value, axis=-1, keepdims=True)
    spread = jnp.mean(center * center, axis=-1, keepdims=True)
    inverse = lax.rsqrt(spread + eps_norm)
    return center * inverse, inverse


def normed_back(unit, inverse, cotangent):
    mean = jnp.mean(cotangent, axis=-1, keepdims=True)
    inner = jnp.mean(cotangent * unit, axis=-1, keepdims=True)
    return inverse * (cotangent - mean - unit * inner)


def column_sum(value):
    return jnp.sum(value, axis=0, keepdims=True)


def feed_kernel(fast, word, ent, context, norms, word_cot, ent_cot, *refs):
    if fast:
        bufs, refs = (refs[0:4], refs[4:8], refs[8:12], refs[12:16]), refs[16:]
    else:
        bufs, refs = refs[0:3], refs[3:]
    (
        word_out,
        ent_out,
        middle_low,
        activated,
        slope,
        d_second,
        d_ffn,
        unit_one,
        inverse_one,
        grads_two,
        out_all,
        exp_all,
        red_all,
        total,
        sem_out,
        sem_exp,
        sem_red,
        sem_save,
    ) = refs
    step = pl.program_id(0)

    @pl.when(step == 0)
    def _():
        if fast:
            start_feed(bufs, out_all, exp_all, red_all, sem_out, sem_exp, sem_red)
        else:
            pltpu.make_async_copy(bufs[0].at[6], out_all, sem_out).start()
            for j in range(4):
                cols = pl.ds(j * D, D)
                pltpu.make_async_copy(bufs[1].at[:, cols], exp_all.at[j], sem_exp.at[j]).start()
                pltpu.make_async_copy(bufs[2].at[:, cols], red_all.at[j], sem_red.at[j]).start()
        drain(out_all, sem_out)
        hidden = jnp.concatenate([word[...], ent[...]], 0)
        unit, inverse = normed(hidden + dot(context[...], out_all[...], NT))
        middle = unit * norms[0:1, :] + norms[1:2, :]
        unit_one[...] = unit
        inverse_one[...] = inverse
        middle_low[...] = middle.astype(bf16)
        total[...] = middle

    for j in range(4):

        @pl.when(step == j)
        def _():
            drain(exp_all.at[j], sem_exp.at[j])
            drain(red_all.at[j], sem_red.at[j])

    inner = dot(middle_low[...], exp_all[step], NN)
    share = 0.5 + 0.5 * lax.erf(inner * 0.7071067811865476)
    slope[...] = share + inner * jnp.exp(-0.5 * inner * inner) * 0.3989422804014327
    active = (inner * share).astype(bf16)
    activated[...] = active
    total[...] += dot(active, red_all[step], NT)

    @pl.when(step == 3)
    def _():
        unit, inverse = normed(total[...])
        result = unit * norms[2:3, :] + norms[3:4, :]
        word_out[...] = result[:WORDS]
        ent_out[...] = result[WORDS:]
        cot = jnp.concatenate([word_cot[...], ent_cot[...]], 0)
        grads_two[0:1, :] = column_sum(cot * unit)
        grads_two[1:2, :] = column_sum(cot)
        back = normed_back(unit, inverse, cot * norms[2:3, :])
        d_second[...] = back
        d_ffn[...] = back.astype(bf16)


def start_feed(bufs, out_all, exp_all, red_all, sem_out, sem_exp, sem_red):
    wide, narrow = coords()
    for block in away_blocks():
        w, n = places(wide, narrow, False, block)
        row = pl.multiple_of(w * 96 + (n % 2) * 48, 16)
        lane = pl.multiple_of((n // 2) * 384, 128)
        src = piece_of(bufs[0], block).at[pl.ds(96, 48)]
        pltpu.make_async_copy(src, out_all.at[pl.ds(row, 48), pl.ds(lane, 384)], sem_out).start()
    for half in range(2):
        for block in away_blocks():
            w, n = places(wide, narrow, False, block)
            src = piece_of(bufs[2 * half], block)
            if half == 0:
                src = src.at[pl.ds(0, 96)]
            row = pl.multiple_of(n * 192 + half * 96, 16)
            lane = pl.multiple_of((w % 2) * 384, 128)
            dst = exp_all.at[w // 2, pl.ds(row, 96), pl.ds(lane, 384)]
            pltpu.make_async_copy(src, dst, sem_exp.at[w // 2]).start()
        for block in away_blocks():
            w, n = places(wide, narrow, True, block)
            src = piece_of(bufs[2 * half + 1], block)
            row = pl.multiple_of(w * 96 + half * 48, 16)
            for part in range(2):
                dst = red_all.at[n, pl.ds(row, 48), pl.ds(part * 384, 384)]
                pltpu.make_async_copy(src.at[pl.ds(part * 48, 48)], dst, sem_red.at[n]).start()


def feed(fast, word, ent, context, norms, word_cot, ent_cot, pieces):
    column = pl.BlockSpec((ROWS, D), lambda i: (0, i))
    return pl.pallas_call(
        functools.partial(feed_kernel, fast),
        grid=(4,),
        in_specs=[VMEM] * 6 + [ANY] * len(pieces),
        out_specs=[VMEM] * 3 + [column, column] + [VMEM] * 8,
        out_shape=[
            shape((WORDS, D), f32),
            shape((ENTS, D), f32),
            shape((ROWS, D), bf16),
            shape((ROWS, FF), bf16),
            shape((ROWS, FF), f32),
            shape((ROWS, D), f32),
            shape((ROWS, D), bf16),
            shape((ROWS, D), f32),
            shape((ROWS, 1), f32),
            shape((2, D), f32),
            shape((D, D), bf16),
            shape((4, D, D), bf16),
            shape((4, D, D), bf16),
        ],
        scratch_shapes=[
            pltpu.VMEM((ROWS, D), f32),
            pltpu.SemaphoreType.DMA,
            pltpu.SemaphoreType.DMA((4,)),
            pltpu.SemaphoreType.DMA((4,)),
            pltpu.SemaphoreType.DMA,
        ],
        compiler_params=PARAMS,
        cost_estimate=cost(2 * ROWS * D * (D + 2 * FF), 40000000),
        name="feed",
    )(word, ent, context, norms, word_cot, ent_cot, *pieces)


def feed_back_kernel(
    d_ffn,
    red_all,
    exp_all,
    slope,
    d_second,
    unit_one,
    inverse_one,
    norms,
    out_all,
    exact,
    d_inner,
    d_first,
    d_out,
    d_context,
    row_inner,
    grads_one,
    total,
):
    step = pl.program_id(0)
    back = (dot(d_ffn[...], red_all[...], NN) * slope[...]).astype(bf16)
    d_inner[...] = back

    @pl.when(step == 0)
    def _():
        total[...] = d_second[...]

    total[...] += dot(back, exp_all[...], NT)

    @pl.when(step == 3)
    def _():
        d_middle = total[...]
        unit = unit_one[...]
        grads_one[0:1, :] = column_sum(d_middle * unit)
        grads_one[1:2, :] = column_sum(d_middle)
        first = normed_back(unit, inverse_one[...], d_middle * norms[0:1, :])
        d_first[...] = first
        d_out[...] = first.astype(bf16)
        context = dot(first.astype(bf16), out_all[...], NN).astype(bf16)
        d_context[...] = context
        product = context.astype(f32) * exact[...]
        head = lax.broadcasted_iota(jnp.int32, (16, D), 1) // HEAD
        pick = jnp.where(head == lax.broadcasted_iota(jnp.int32, (16, D), 0), 1.0, 0.0).astype(bf16)
        high = product.astype(bf16)
        low = (product - high.astype(f32)).astype(bf16)
        sums = dot(pick, high, NT) + dot(pick, low, NT)
        for i in range(HEADS // 2):
            row_inner[i] = sums[2 * i : 2 * i + 2]


def feed_back(d_ffn, red_all, exp_all, slope, d_second, unit_one, inverse_one, norms, out_all, exact):
    column = pl.BlockSpec((ROWS, D), lambda i: (0, i))
    part = pl.BlockSpec((None, D, D), lambda i: (i, 0, 0))
    return pl.pallas_call(
        feed_back_kernel,
        grid=(4,),
        in_specs=[VMEM, part, part, column] + [VMEM] * 6,
        out_specs=[column] + [VMEM] * 5,
        out_shape=[
            shape((ROWS, FF), bf16),
            shape((ROWS, D), f32),
            shape((ROWS, D), bf16),
            shape((ROWS, D), bf16),
            shape((HEADS // 2, 2, ROWS), f32),
            shape((2, D), f32),
        ],
        scratch_shapes=[pltpu.VMEM((ROWS, D), f32)],
        compiler_params=PARAMS,
        cost_estimate=cost(2 * ROWS * D * (D + 2 * FF), 30000000),
        name="feed_back",
    )(d_ffn, red_all, exp_all, slope, d_second, unit_one, inverse_one, norms, out_all, exact)


def attend_back_kernel(
    counts, to_words, to_ents, keys, values, d_context, lse, row_inner, d_to_words, d_to_ents, d_keys, d_values
):
    masks = head_masks(counts)
    scale = HEAD ** (-0.5)
    one, two, three, four = [], [], [], []
    for h in range(2):
        cols = slice(h * HEAD, (h + 1) * HEAD)
        scores = scores_of(masks[h], keys[...], to_words[...], to_ents[...])
        probs = jnp.exp(scores - lse[h : h + 1, :])
        d_probs = dot(values[...] * masks[h][0], d_context[...], NT)
        d_scores = (probs * (d_probs - row_inner[h : h + 1, :])).astype(bf16)
        one.append(dot(keys[:WORDS, cols], d_scores[:WORDS], TN))
        two.append(dot(keys[WORDS:, cols], d_scores[WORDS:], TN))
        three.append(
            jnp.concatenate(
                [
                    dot(d_scores[:WORDS], to_words[:, cols], NN),
                    dot(d_scores[WORDS:], to_ents[:, cols], NN),
                ],
                0,
            )
        )
        four.append(dot(probs.astype(bf16), d_context[:, cols], NN))
    d_to_words[...] = (jnp.concatenate(one, 0).T * scale).astype(bf16)
    d_to_ents[...] = (jnp.concatenate(two, 0).T * scale).astype(bf16)
    d_keys[...] = jnp.concatenate(three, 1).astype(bf16)
    d_values[...] = jnp.concatenate(four, 1).astype(bf16)


def attend_back(counts, to_words, to_ents, keys, values, d_context, lse, row_inner):
    pair = pl.BlockSpec((ROWS, 128), lambda i: (0, i))
    stat = pl.BlockSpec((None, 2, ROWS), lambda i: (i, 0, 0))
    return pl.pallas_call(
        attend_back_kernel,
        grid=(HEADS // 2,),
        in_specs=[SMEM] + [pair] * 5 + [stat] * 2,
        out_specs=[pair] * 4,
        out_shape=[shape((ROWS, D), bf16)] * 4,
        compiler_params=PARAMS,
        cost_estimate=cost(16 * ROWS * ROWS * D, 12000000),
        name="attend_back",
    )(counts, to_words, to_ents, keys, values, d_context, lse, row_inner)


def grad_red_kernel(d_ffn, activated, send, keep, whole):
    wide, narrow = coords()
    for core in range(2):
        out = keep if core == 0 else send
        for x in range(2):
            n = narrow ^ (x * 2 + core)
            lanes = pl.ds(pl.multiple_of(n * D, D), D)
            whole[...] = dot(d_ffn[...], activated[:, lanes], TN)
            for w in range(8):
                away = wide ^ w
                y, low, high = away % 2, (away // 2) % 2, away // 4
                out[0, x, y, low, high] = whole[w * 96 : w * 96 + 48].astype(bf16)
                out[1, y, x, low, high] = whole[w * 96 + 48 : w * 96 + 96].astype(bf16)


def grad_red(d_ffn, activated):
    block = shape((2, 2, 2, 2, 2, 48, D), bf16)
    return pl.pallas_call(
        grad_red_kernel,
        in_specs=[VMEM] * 2,
        out_specs=[VMEM] * 2,
        out_shape=[block, block],
        scratch_shapes=[pltpu.VMEM((D, D), f32)],
        compiler_params=PARAMS,
        cost_estimate=cost(2 * ROWS * D * FF, 10000000),
        name="grad_red",
    )(d_ffn, activated)


def grad_exp_kernel(middle_low, d_inner, d_out, context, send, keep, whole):
    wide, narrow = coords()
    for z in range(4):
        away_z = (wide // 2) ^ z
        low, high = away_z % 2, away_z // 2
        whole[...] = dot(middle_low[...], d_inner[:, z * D : (z + 1) * D], TN)
        for y in range(2):
            w = z * 2 + y
            away_y = (wide ^ w) % 2
            for x in range(2):
                for core in range(2):
                    out = keep if core == 0 else send
                    n = narrow ^ (x * 2 + core)
                    for half in range(2):
                        rows = pl.ds(pl.multiple_of(n * 192 + half * 96, 16), 96)
                        value = whole[rows, y * 384 : (y + 1) * 384].astype(bf16)
                        if half == 0:
                            out[0, x, away_y, low, high, :96] = value
                        else:
                            out[1, away_y, x, low, high, :96] = value
    whole[...] = dot(d_out[...], context[...], TN)
    store_attention(whole, send, keep, 96, (24, 24))


def store_attention(whole, send, keep, at, halves):
    wide, narrow = coords()
    for w in range(8):
        away = wide ^ w
        y, low, high = away % 2, (away // 2) % 2, away // 4
        for x in range(2):
            for core in range(2):
                out = keep if core == 0 else send
                n = narrow ^ (x * 2 + core)
                lanes = pl.ds(pl.multiple_of((n // 2) * 384, 128), 384)
                start = w * 96 + (n % 2) * 48
                for half in range(2):
                    if not halves[half]:
                        continue
                    skip = halves[0] if half else 0
                    rows = pl.ds(pl.multiple_of(start + skip, 8), halves[half])
                    value = whole[rows, lanes].astype(bf16)
                    if half == 0:
                        out[0, x, y, low, high, at : at + halves[0]] = value
                    else:
                        out[1, y, x, low, high, at : at + halves[1]] = value


def grad_exp(middle_low, d_inner, d_out, context):
    block = shape((2, 2, 2, 2, 2, 120, 384), bf16)
    return pl.pallas_call(
        grad_exp_kernel,
        in_specs=[VMEM] * 4,
        out_specs=[VMEM] * 2,
        out_shape=[block, block],
        scratch_shapes=[pltpu.VMEM((D, D), f32)],
        compiler_params=PARAMS,
        cost_estimate=cost(2 * ROWS * D * (FF + D), 12000000),
        name="grad_exp",
    )(middle_low, d_inner, d_out, context)


def grad_att_kernel(low, d_to_words, d_to_ents, d_keys, d_values, send, keep, whole):
    word = low[:WORDS]
    ent = low[WORDS:]
    work = (
        (d_keys, slice(0, ROWS), 0, 0),
        (d_to_words, slice(0, WORDS), 0, 48),
        (d_to_words, slice(WORDS, ROWS), 0, 96),
        (d_values, slice(0, ROWS), 1, 0),
        (d_to_ents, slice(0, WORDS), 1, 48),
        (d_to_ents, slice(WORDS, ROWS), 1, 96),
    )
    for ref, rows, half, at in work:
        whole[...] = dot(ref[rows, :], low[rows, :], TN)
        store_attention(whole, send, keep, at, (48, 0) if half == 0 else (0, 48))


def grad_att(low, d_to_words, d_to_ents, d_keys, d_values):
    block = shape((2, 2, 2, 2, 2, 144, 384), bf16)
    return pl.pallas_call(
        grad_att_kernel,
        in_specs=[VMEM] * 5,
        out_specs=[VMEM] * 2,
        out_shape=[block, block],
        scratch_shapes=[pltpu.VMEM((D, D), f32)],
        compiler_params=PARAMS,
        cost_estimate=cost(2 * ROWS * D * D * 4, 12000000),
        name="grad_att",
    )(low, d_to_words, d_to_ents, d_keys, d_values)


def grad_hidden_kernel(d_first, d_to_words, d_to_ents, d_keys, d_values, kv, q, word, ent):
    shared = d_first[...] + dot(d_keys[...], kv[0], NN) + dot(d_values[...], kv[1], NN)
    word[...] = (
        shared[:WORDS] + dot(d_to_words[:WORDS], q[0], NN) + dot(d_to_ents[:WORDS], q[2], NN)
    )
    ent[...] = (
        shared[WORDS:] + dot(d_to_words[WORDS:], q[1], NN) + dot(d_to_ents[WORDS:], q[3], NN)
    )


def grad_hidden(*args):
    return pl.pallas_call(
        grad_hidden_kernel,
        in_specs=[VMEM] * 7,
        out_specs=[VMEM] * 2,
        out_shape=[shape((WORDS, D), f32), shape((ENTS, D), f32)],
        compiler_params=PARAMS,
        cost_estimate=cost(2 * ROWS * D * D * 4, 16000000),
        name="grad_hidden",
    )(*args)


def flip(axis, bit, value):
    size = lax.axis_size(axis)
    return lax.ppermute(value, axis, [(i, i ^ bit) for i in range(size)])


def over(name, value):
    axis, bit = {
        "core": ("narrow", 1),
        "x": ("narrow", 2),
        "y": ("wide", 1),
        "low": ("wide", 2),
        "high": ("wide", 4),
    }[name]
    return flip(axis, bit, value)


def gather_pair(first, second):
    cut = first.shape[0]
    both = jnp.concatenate([first, second], 0)
    both = jnp.stack([both, over("high", both)], 0)
    got = over("low", both)
    left = jnp.stack([both[:, :cut], got[:, :cut]], 0)
    right = jnp.stack([both[:, cut:], got[:, cut:]], 0)
    left = jnp.stack([left, over("x", left)], 0)
    right = jnp.stack([right, over("y", right)], 0)
    left_far = over("y", left)
    right_far = over("x", right)
    left_core = over("core", left)
    right_core = over("core", right)
    return (
        (left, left_far, left_core, over("core", left_far)),
        (right, right_far, right_core, over("core", right_far)),
    )


def plus(kept, got, at):
    return (kept[at].astype(f32) + got[at].astype(f32)).astype(bf16)


def scatter_pair(send, keep):
    got = over("core", send)
    left = over("x", plus(keep, got, (0, 1)))
    right = over("y", plus(keep, got, (1, 1)))
    keep_left = plus(keep, got, (0, 0))
    keep_right = plus(keep, got, (1, 0))
    left_two = over("y", plus(keep_left, left, 1))
    right_two = over("x", plus(keep_right, right, 1))
    keep_left = plus(keep_left, left, 0)
    keep_right = plus(keep_right, right, 0)
    keep = jnp.stack([plus(keep_left, left_two, ()), plus(keep_right, right_two, ())], 1)
    got = over("low", keep[1])
    keep = (keep[0].astype(f32) + got.astype(f32)).astype(bf16)
    got = over("high", keep[:, 1])
    return keep[:, 0].astype(f32) + got.astype(f32)


def sum_all(value):
    size = lax.axis_size("wide") * lax.axis_size("narrow")
    spread = jnp.broadcast_to(value[None], (size,) + value.shape)
    got = lax.all_to_all(spread, ("wide", "narrow"), 0, 0, tiled=False)
    return jnp.sum(got, axis=0)


def adapt(weight, grad, first, second, decay):
    first = 0.5 * first + 0.5 * grad
    second = 0.5 * second + 0.5 * grad * grad
    fix_first = 1.0 - 0.5**STEP
    fix_second = 1.0 - 0.5**STEP
    update = first / fix_first / (jnp.sqrt(second / fix_second) + adam_eps) + decay * weight
    return (first, second, update)


def shards(
    fast,
    word_states,
    entity_states,
    seq_counts,
    attention_weight,
    expand_weight,
    reduce_weight,
    norm_params,
    moment_attention,
    moment_expand,
    moment_reduce,
    moment_norms,
    square_attention,
    square_expand,
    square_reduce,
    square_norms,
    word_cotangent,
    entity_cotangent,
):
    word, ent, counts = word_states[0], entity_states[0], seq_counts[0]
    core = lax.axis_index("narrow") % 2
    if fast:
        keep, send, exp_low, red_low, weight_local = prep(
            attention_weight, expand_weight, reduce_weight
        )
        got = over("core", send)
        rows = jnp.where(
            core == 0, jnp.concatenate([keep, got], 2), jnp.concatenate([got, keep], 2)
        )
        kv = gather_pair(rows[4], rows[5])
        query = gather_pair(
            jnp.concatenate([rows[0], rows[2]], 0), jnp.concatenate([rows[1], rows[3]], 0)
        )
        feed_one = gather_pair(
            jnp.concatenate([exp_low[:96], rows[6]], 0), red_low[:, :48].reshape(96, 384)
        )
        feed_two = gather_pair(exp_low[96:], red_low[:, 48:].reshape(96, 384))
        kv_pieces = [
            v.reshape(v.shape[:3] + (1, 48, 384)) for half in kv for v in half
        ]
        query_pieces = [
            v.reshape(v.shape[:3] + (2, 48, 384)) for half in query for v in half
        ]
        feed_pieces = [v for pair in (feed_one, feed_two) for half in pair for v in half]
    else:
        weight_local = jnp.concatenate(
            [
                jnp.sum(attention_weight * attention_weight, axis=(1, 2)),
                jnp.sum(expand_weight * expand_weight)[None],
                jnp.sum(reduce_weight * reduce_weight)[None],
            ]
        )
        turned = jnp.swapaxes(attention_weight.astype(bf16), 1, 2)
        turned = lax.all_gather(turned, "wide", axis=1, tiled=True)
        turned = lax.all_gather(turned, "narrow", axis=2, tiled=True)
        exp_all = lax.all_gather(expand_weight.astype(bf16), "wide", axis=1, tiled=True)
        exp_all = lax.all_gather(exp_all, "narrow", axis=0, tiled=True)
        red_all = lax.all_gather(reduce_weight.astype(bf16).T, "wide", axis=0, tiled=True)
        red_all = lax.all_gather(red_all, "narrow", axis=1, tiled=True)
        kv_pieces = query_pieces = [turned]
        feed_pieces = [turned, exp_all, red_all]

    low, keys, values, kv_all = project_kv(fast, word, ent, kv_pieces)
    to_words, to_ents, q_all = project_q(fast, low, query_pieces)
    context, exact, lse = attend(counts, to_words, to_ents, keys, values)
    (
        word_out,
        ent_out,
        middle_low,
        activated,
        slope,
        d_second,
        d_ffn,
        unit_one,
        inverse_one,
        grads_two,
        out_all,
        exp_all,
        red_all,
    ) = feed(
        fast, word, ent, context, norm_params, word_cotangent[0], entity_cotangent[0], feed_pieces
    )
    if fast:
        red_sum = scatter_pair(*grad_red(d_ffn, activated))
    d_inner, d_first, d_out, d_context, row_inner, grads_one = feed_back(
        d_ffn,
        red_all,
        exp_all,
        slope,
        d_second,
        unit_one,
        inverse_one,
        norm_params,
        out_all,
        exact,
    )
    if fast:
        exp_sum = scatter_pair(*grad_exp(middle_low, d_inner, d_out, context))
    d_to_words, d_to_ents, d_keys, d_values = attend_back(
        counts, to_words, to_ents, keys, values, d_context, lse, row_inner
    )
    if fast:
        att_sum = scatter_pair(*grad_att(low, d_to_words, d_to_ents, d_keys, d_values))
    word_grad, ent_grad = grad_hidden(
        d_first, d_to_words, d_to_ents, d_keys, d_values, kv_all, q_all
    )
    early = jnp.concatenate([grads_one, grads_two], 0)
    early = jnp.concatenate([early, jnp.pad(weight_local, (0, D - 9))[None]], 0)
    early = jnp.sum(lax.all_gather(early, ("wide", "narrow"), axis=0, tiled=False), axis=0)
    norm_grads = early[:4]
    weight_total = early[4, :9]

    if fast:
        out_rows = jnp.concatenate([exp_sum[0, 96:], exp_sum[1, 96:]], 0)
        rows = jnp.stack(
            [
                att_sum[0, 48:96],
                att_sum[1, 48:96],
                att_sum[0, 96:],
                att_sum[1, 96:],
                att_sum[0, :48],
                att_sum[1, :48],
                out_rows,
            ]
        ).astype(bf16)
        near, far = rows[:, :, :192], rows[:, :, 192:]
        got = over("core", jnp.where(core == 0, far, near))
        own = jnp.where(core == 0, near, far)
        turned = jnp.where(
            core == 0, jnp.concatenate([own, got], 1), jnp.concatenate([got, own], 1)
        )
        att_grad = jnp.swapaxes(turned.astype(f32), 1, 2)
        exp_grad = jnp.concatenate([exp_sum[0, :96], exp_sum[1, :96]], 0)
        red_grad = jnp.concatenate([red_sum[0], red_sum[1]], 0).T
    else:
        words, ents = low[:WORDS], low[WORDS:]
        turned = jnp.stack(
            [
                dot(d_to_words[:WORDS], words, TN),
                dot(d_to_ents[:WORDS], words, TN),
                dot(d_to_words[WORDS:], ents, TN),
                dot(d_to_ents[WORDS:], ents, TN),
                dot(d_keys, low, TN),
                dot(d_values, low, TN),
                dot(d_out, context, TN),
            ]
        ).astype(bf16)
        turned = lax.psum_scatter(turned, "wide", scatter_dimension=1, tiled=True)
        turned = lax.psum_scatter(turned, "narrow", scatter_dimension=2, tiled=True)
        att_grad = jnp.swapaxes(turned.astype(f32), 1, 2)
        grad = dot(middle_low, d_inner, TN).astype(bf16)
        grad = lax.psum_scatter(grad, "wide", scatter_dimension=1, tiled=True)
        grad = lax.psum_scatter(grad, "narrow", scatter_dimension=0, tiled=True)
        exp_grad = grad.astype(f32)
        grad = dot(d_ffn, activated, TN).astype(bf16)
        grad = lax.psum_scatter(grad, "wide", scatter_dimension=0, tiled=True)
        grad = lax.psum_scatter(grad, "narrow", scatter_dimension=1, tiled=True)
        red_grad = grad.astype(f32).T

    att_first, att_second, att_update = adapt(
        attention_weight, att_grad, moment_attention, square_attention, matrix_decay
    )
    exp_first, exp_second, exp_update = adapt(
        expand_weight, exp_grad, moment_expand, square_expand, matrix_decay
    )
    red_first, red_second, red_update = adapt(
        reduce_weight, red_grad, moment_reduce, square_reduce, matrix_decay
    )
    update_local = jnp.concatenate(
        [
            jnp.sum(att_update * att_update, axis=(1, 2)),
            jnp.sum(exp_update * exp_update)[None],
            jnp.sum(red_update * red_update)[None],
        ]
    )
    update_total = sum_all(update_local)
    nrm_first, nrm_second, nrm_update = adapt(
        norm_params, norm_grads, moment_norms, square_norms, 0.0
    )
    weight_norm = jnp.sqrt(
        jnp.concatenate([weight_total, jnp.sum(norm_params * norm_params, axis=1)])
    )
    update_norm = jnp.sqrt(
        jnp.concatenate([update_total, jnp.sum(nrm_update * nrm_update, axis=1)])
    )
    trust = weight_norm / update_norm
    new_attention = attention_weight - learn_rate * trust[0:7, None, None] * att_update
    new_expand = expand_weight - learn_rate * trust[7] * exp_update
    new_reduce = reduce_weight - learn_rate * trust[8] * red_update
    new_norms = norm_params - learn_rate * trust[9:13, None] * nrm_update
    trust_stats = jnp.stack([jnp.log(weight_norm), jnp.log(update_norm), jnp.log(trust)], 1)
    return (
        word_out[None],
        ent_out[None],
        word_grad[None],
        ent_grad[None],
        new_attention,
        new_expand,
        new_reduce,
        new_norms,
        att_first,
        exp_first,
        red_first,
        nrm_first,
        att_second,
        exp_second,
        red_second,
        nrm_second,
        trust_stats,
    )


def solution(mesh):
    fast = mesh.shape["wide"] == 8 and mesh.shape["narrow"] == 4
    rows = P(("wide", "narrow"), None, None)
    matrix = P("narrow", "wide")
    stack = P(None, "narrow", "wide")
    weights = (stack, matrix, matrix, P())
    return jax.shard_map(
        functools.partial(shards, fast),
        mesh=mesh,
        in_specs=(rows, rows, P(("wide", "narrow"), None)) + weights * 3 + (rows, rows),
        out_specs=(rows,) * 4 + weights * 3 + (P(),),
        check_vma=False,
    )
```

time: 844 us -> 450 us (0.53)
  waiting for transfers between devices: 428 us -> 164 us
  matrix products: 171 us -> 0 us
  Pallas kernels: 0 us -> 132 us
  local copies, waits for them, and re-layouts: 133 us -> 13.9 us
  starting transfers between devices: 0.49 us -> 46.8 us
  other arithmetic: 49.2 us -> 31.9 us
  between operations: 16.8 us -> 3.34 us
  blocking collectives: 39.7 us -> 50.8 us
    all_gather x6 -> x0, waiting for transfers between devices: 195 us -> none  [the longest x1 60.1 us: shards(): lax.all_gather(attention_weight.astype(bf16), 'wide', axis=2, tiled=True)]
    ppermute x0 -> x63, waiting for transfers between devices: none -> 159 us  [flip(): return lax.ppermute(value, axis, [(i, i ^ bit) for i in range(size)])]
    reduce_scatter x4 -> x0, waiting for transfers between devices: 150 us -> none  [the longest x1 150 us: shards(): lax.psum_scatter(local_grads[0].astype(jnp.bfloat16), 'wide', scatter_dim...]
    dot_general x39 -> x0, matrix products: 148 us -> none  [the longest x5 38.2 us: dense(): return jnp.dot(left, right, preferred_element_type=jnp.float32)]
    pallas_call x0 -> x11, Pallas kernels: none -> 132 us  [the longest x1 25.7 us: feed(): pl.pallas_call(functools.partial(feed_kernel, fast), grid=(4,), in_specs=...]
    unnamed x162 -> x89, local copies, waits for them, and re-layouts: 98.3 us -> 10.5 us
    unnamed x14 -> x0, waiting for transfers between devices: 83 us -> none
    all_gather x0 -> x1, blocking collectives: none -> 50.8 us  [shards(): lax.all_gather(early, ('wide', 'narrow'), axis=0, tiled=False)]
  transfers between devices with their start and end apart: 12 -> 64, of which waited for: 7 -> 30; matrix products, arithmetic and copies ran while one was open for 35% -> 8% of each run, Pallas kernels for 0% -> 21%
where the time goes in v1:
time: 450 us; the launch traced here: 443 us
  waiting for transfers between devices  164 us (36%)
  Pallas kernels  132 us (29%)
  blocking collectives  50.8 us (11%)
  starting transfers between devices  46.8 us (10%)
  other arithmetic  31.9 us (7%)
  local copies, waits for them, and re-layouts  13.9 us (3%)
    ppermute x63, waiting for transfers between devices, flip(): return lax.ppermute(value, axis, [(i, i ^ bit) for i in range(size)])  159 us
    all_gather x1, blocking collectives, shards(): lax.all_gather(early, ('wide', 'narrow'), axis=0, tiled=False)  50.8 us
    ppermute x63, starting transfers between devices, flip(): return lax.ppermute(value, axis, [(i, i ^ bit) for i in range(size)])  44.3 us
    pallas_call x1, Pallas kernels, feed(): pl.pallas_call(functools.partial(feed_kernel, fast), grid=(4,), in_specs=...  25.7 us
    pallas_call x1, Pallas kernels, feed_back(): pl.pallas_call(feed_back_kernel, grid=(4,), in_specs=[VMEM, part, part, c...  20.6 us
    pallas_call x1, Pallas kernels, attend_back(): pl.pallas_call(attend_back_kernel, grid=(HEADS // 2,), in_specs=[SMEM] +...  17.3 us
    pallas_call x1, Pallas kernels, attend(): pl.pallas_call(attend_kernel, grid=(HEADS // 2,), in_specs=[SMEM, pair, p...  12.1 us
    convert_element_type x9, other arithmetic, plus(): return (kept[at].astype(f32) + got[at].astype(f32)).astype(bf16)  11.6 us
  transfers between devices with their start and end apart: 64, of which 30 were waited for; matrix products, arithmetic and copies ran while one was open for 8% of the time, Pallas kernels for 21%

profile of v1, /device:TPU:0, one launch (start us, length us, event | category | flops | bytes accessed | tf_op | source)
XLA Modules:
  0.0 442.7 jit_solution(17946024895515026036)
XLA Ops:
  8.3 3.7 collective-permute-start.31
  16.4 12.1 %collective-permute-done.31 = bf16[192,384]{1,0:T(8,128)(2,1)S(1)} collective-permute-done((bf16[192,384]{1,0:T(8,128)(2,1)S(1)}, bf16[192,384]{1,0:T(8,128)(2,1)S(1)}, u32[]{:S(2)}, u32[]{:S(2)}) %collective-permute-start.31) | collective-permute-done | bytes 147488 | tf_op jit(solution)/shard_map/ppermute | solution.py:676
  29.2 7.9 %collective-permute-done.1 = bf16[96,384]{1,0:T(8,128)(2,1)S(1)} collective-permute-done((bf16[96,384]{1,0:T(8,128)(2,1)S(1)}, bf16[96,384]{1,0:T(8,128)(2,1)S(1)}, u32[]{:S(2)}, u32[]{:S(2)}) %collective-permute-start.1) | collective-permute-done | bytes 73760 | tf_op jit(solution)/shard_map/ppermute | solution.py:676
  40.3 6.3 %collective-permute-done.2 = bf16[2,96,384]{2,1,0:T(8,128)(2,1)S(1)} collective-permute-done((bf16[2,96,384]{2,1,0:T(8,128)(2,1)S(1)}, bf16[2,96,384]{2,1,0:T(8,128)(2,1)S(1)}, u32[]{:S(2)}, u32[]{:S(2)}) %collective-permute-start.2) | collective-permute-done | bytes 147488 | tf_op jit(solution)/shard_map/ppermute | solution.py:676
  71.3 5.6 %collective-permute-done.17 = bf16[2,2,96,384]{3,2,1,0:T(8,128)(2,1)S(1)} collective-permute-done((bf16[2,2,96,384]{3,2,1,0:T(8,128)(2,1)S(1)}, bf16[2,2,96,384]{3,2,1,0:T(8,128)(2,1)S(1)}, u32[]{:S(2)}, u32[]{:S(2)}) %collective-permute-start.17) | collective-permute-done | bytes 294944 | tf_op jit(solution)/shard_map/ppermute | solution.py:676
  85.3 4.6 %collective-permute-done.23 = bf16[2,2,144,384]{3,2,1,0:T(8,128)(2,1)S(1)} collective-permute-done((bf16[2,2,144,384]{3,2,1,0:T(8,128)(2,1)S(1)}, bf16[2,2,144,384]{3,2,1,0:T(8,128)(2,1)S(1)}, u32[]{:S(2)}, u32[]{:S(2)}) %collective-permute-start.23) | collective-permute-done | bytes 442400 | tf_op jit(solution)/shard_map/ppermute | solution.py:676
  95.0 7.7 %collective-permute-done.38.refs_13_ = bf16[2,2,2,96,384]{4,3,2,1,0:T(8,128)(2,1)} collective-permute-done((bf16[2,2,2,96,384]{4,3,2,1,0:T(8,128)(2,1)S(1)}, bf16[2,2,2,96,384]{4,3,2,1,0:T(8,128)(2,1)}, u32[]{:S(2)}, u32[]{:S(2)}) %collective-permute-start.38) | collective-permute-done | bytes 589856 | tf_op jit(solution)/shard_map/ppermute | solution.py:676
  105.2 7.3 %collective-permute-done.18 = bf16[2,2,2,96,384]{4,3,2,1,0:T(8,128)(2,1)S(1)} collective-permute-done((bf16[2,2,2,96,384]{4,3,2,1,0:T(8,128)(2,1)S(1)}, bf16[2,2,2,96,384]{4,3,2,1,0:T(8,128)(2,1)S(1)}, u32[]{:S(2)}, u32[]{:S(2)}) %collective-permute-start.18) | collective-permute-done | bytes 589856 | tf_op jit(solution)/shard_map/ppermute | solution.py:676
  114.0 3.7 collective-permute-done.14
  118.3 6.9 %collective-permute-done.28.refs_5_ = bf16[2,2,2,96,384]{4,3,2,1,0:T(8,128)(2,1)} collective-permute-done((bf16[2,2,2,96,384]{4,3,2,1,0:T(8,128)(2,1)S(1)}, bf16[2,2,2,96,384]{4,3,2,1,0:T(8,128)(2,1)}, u32[]{:S(2)}, u32[]{:S(2)}) %collective-permute-start.28) | collective-permute-done | bytes 589856 | tf_op jit(solution)/shard_map/ppermute | solution.py:676
  125.2 6.5 %collective-permute-done.24.refs_1_ = bf16[2,2,2,144,384]{4,3,2,1,0:T(8,128)(2,1)} collective-permute-done((bf16[2,2,2,144,384]{4,3,2,1,0:T(8,128)(2,1)S(1)}, bf16[2,2,2,144,384]{4,3,2,1,0:T(8,128)(2,1)}, u32[]{:S(2)}, u32[]{:S(2)}) %collective-permute-start.24) | collective-permute-done | bytes 884768 | tf_op jit(solution)/shard_map/ppermute | solution.py:676
  134.5 5.8 %project_kv.1 = (bf16[640,768]{1,0:T(8,128)(2,1)}, bf16[640,768]{1,0:T(8,128)(2,1)}, bf16[640,768]{1,0:T(8,128)(2,1)}, bf16[2,768,768]{2,1,0:T(8,128)(2,1)}) custom-call(f32[512,768]{1,0:T(8,128)} %bitcast.399, f32[128,768]{1,0:T(8,128)} %bitcast.403, bf16[2,2,2,1,48,384]{5,4,3,2,1,0:T(8,128)(2,1)} %get-tuple-element.250.refs_0_, ...), custom_call_target="tpu_custom_call" | custom-call | flops 1509949440 | bytes 8000000 | tf_op jit(solution)/shard_map/project_kv/pallas_call | solution.py:156
  140.4 8.2 %project_q.1 = (bf16[640,768]{1,0:T(8,128)(2,1)}, bf16[640,768]{1,0:T(8,128)(2,1)}, bf16[4,768,768]{2,1,0:T(8,128)(2,1)}) custom-call(bf16[640,768]{1,0:T(8,128)(2,1)} %get-tuple-element.65.low, bf16[2,2,2,2,48,384]{5,4,3,2,1,0:T(8,128)(2,1)} %pad_maximum_fusion.1.refs_0_, bf16[2,2,2,2,48,384]{5,4,3,2,1,0:T(8,128)(2,1)} %bitcast.378, ...), custom_call_target="tpu_custom_call" | custom-call | flops 1509949440 | bytes 8000000 | tf_op jit(solution)/shard_map/project_q/pallas_call | solution.py:191
  148.6 12.1 %attend.1 = (bf16[640,768]{1,0:T(8,128)(2,1)}, f32[640,768]{1,0:T(8,128)}, f32[6,2,640]{2,1,0:T(2,128)}) custom-call(s32[2]{0:T(128)} %bitcast.413, bf16[640,768]{1,0:T(8,128)(2,1)} %get-tuple-element.66.to_words, bf16[640,768]{1,0:T(8,128)(2,1)} %get-tuple-element.67.to_ents, bf16[640,768]{1,0:T(8,128)(2,1)} %get-tuple-element.68.keys, ...), custom_call_target="tpu_custom_call" | custom-call | flops 2516582400 | bytes 12000000 | tf_op jit(solution)/shard_map/attend/pallas_call | solution.py:245
  160.8 25.7 %feed.1 = (f32[512,768]{1,0:T(8,128)}, f32[128,768]{1,0:T(8,128)}, bf16[640,768]{1,0:T(8,128)(2,1)}, bf16[640,3072]{1,0:T(8,128)(2,1)}, f32[640,3072]{1,0:T(8,12...) custom-call(f32[512,768]{1,0:T(8,128)} %bitcast.400, ...), custom_call_target="tpu_custom_call" | custom-call | flops 6794772480 | bytes 40000000 | tf_op jit(solution)/shard_map/feed/pallas_call | solution.py:381
  186.5 8.3 %grad_red.1 = (bf16[2,2,2,2,2,48,768]{6,5,4,3,2,1,0:T(8,128)(2,1)}, bf16[2,2,2,2,2,48,768]{6,5,4,3,2,1,0:T(8,128)(2,1)}) custom-call(bf16[640,768]{1,0:T(8,128)(2,1)} %get-tuple-element.75.d_ffn, bf16[640,3072]{1,0:T(8,128)(2,1)} %get-tuple-element.106.activated), custom_call_target="tpu_custom_call" | custom-call | flops 3019898880 | bytes 10000000 | tf_op jit(solution)/shard_map/grad_red/pallas_call | solution.py:549
  195.0 20.6 %feed_back.1 = (bf16[640,3072]{1,0:T(8,128)(2,1)}, f32[640,768]{1,0:T(8,128)}, bf16[640,768]{1,0:T(8,128)(2,1)}, bf16[640,768]{1,0:T(8,128)(2,1)}, f32[6,2,640]{2,1,0:T(2,128)}, /*index=5*/f32[2,768]{1,0:T(2,128)}) custom-call(bf16[640,768]{1,0:T(8,128)(2,1)} %get-tuple-element.75.d_ffn, bf16[4,768,768]{2,1,0:T(8,128)(2,1)} %get-tuple-element.76.red_all, ...), custom_call_target="tpu_custom_call" | custom-call | flops 6794772480 | bytes 30000000 | tf_op jit(solution)/shard_map/feed_back/pallas_call | solution.py:467
  215.6 10.9 %grad_exp.1 = (bf16[2,2,2,2,2,120,384]{6,5,4,3,2,1,0:T(8,128)(2,1)}, bf16[2,2,2,2,2,120,384]{6,5,4,3,2,1,0:T(8,128)(2,1)}) custom-call(bf16[640,768]{1,0:T(8,128)(2,1)} %get-tuple-element.101.middle_low, bf16[640,3072]{1,0:T(8,128)(2,1)} %get-tuple-element.102.d_inner, bf16[640,768]{1,0:T(8,128)(2,1)} %get-tuple-element.103.d_out, ...), custom_call_target="tpu_custom_call" | custom-call | flops 3774873600 | bytes 12000000 | tf_op jit(solution)/shard_map/grad_exp/pallas_call | solution.py:610
  226.9 17.3 %attend_back.1 = (bf16[640,768]{1,0:T(8,128)(2,1)}, bf16[640,768]{1,0:T(8,128)(2,1)}, bf16[640,768]{1,0:T(8,128)(2,1)}, bf16[640,768]{1,0:T(8,128)(2,1)}) custom-call(s32[2]{0:T(128)} %bitcast.414, bf16[640,768]{1,0:T(8,128)(2,1)} %get-tuple-element.66.to_words, bf16[640,768]{1,0:T(8,128)(2,1)} %get-tuple-element.67.to_ents, ...), custom_call_target="tpu_custom_call" | custom-call | flops 5033164800 | bytes 12000000 | tf_op jit(solution)/shard_map/attend_back/pallas_call | solution.py:520
  244.2 10.5 %grad_att.1 = (bf16[2,2,2,2,2,144,384]{6,5,4,3,2,1,0:T(8,128)(2,1)}, bf16[2,2,2,2,2,144,384]{6,5,4,3,2,1,0:T(8,128)(2,1)}) custom-call(bf16[640,768]{1,0:T(8,128)(2,1)} %get-tuple-element.65.low, bf16[640,768]{1,0:T(8,128)(2,1)} %get-tuple-element.88.d_to_words, bf16[640,768]{1,0:T(8,128)(2,1)} %get-tuple-element.89.d_to_ents, ...), custom_call_target="tpu_custom_call" | custom-call | flops 3019898880 | bytes 12000000 | tf_op jit(solution)/shard_map/grad_att/pallas_call | solution.py:640
  259.9 3.4 add_convert_fusion.11
  264.9 50.8 %all-gather.1 = f32[32,5,768]{2,1,0:T(8,128)S(1)} all-gather(f32[1,5,768]{2,1,0:T(8,128)S(1)} %maximum_bitcast_fusion.2), channel_id=2, replica_groups=mesh['wide'=8,'narrow'=4] {'wide','narrow'}, dimensions={0}, use_global_device_ids=true | all-gather | bytes 506880 | tf_op jit(solution)/shard_map/all_gather | solution.py:855
  316.7 9.2 %grad_hidden.1 = (f32[512,768]{1,0:T(8,128)}, f32[128,768]{1,0:T(8,128)}) custom-call(f32[640,768]{1,0:T(8,128)} %get-tuple-element.84.d_first, bf16[640,768]{1,0:T(8,128)(2,1)} %get-tuple-element.88.d_to_words, bf16[640,768]{1,0:T(8,128)(2,1)} %get-tuple-element.89.d_to_ents, bf16[640,768]{1,0:T(8,128)(2,1)} %get-tuple-element.90.d_keys, ...), custom_call_target="tpu_custom_call" | custom-call | flops 3019898880 | bytes 16000000 | tf_op jit(solution)/shard_map/grad_hidden/pallas_call | solution.py:663
  339.4 4.1 collective-permute-done.60
  347.7 3.8 collective-permute-done.61
  351.7 7.6 %collective-permute-done.49 = bf16[2,2,2,120,384]{4,3,2,1,0:T(8,128)(2,1)S(1)} collective-permute-done((bf16[2,2,2,120,384]{4,3,2,1,0:T(8,128)(2,1)S(1)}, bf16[2,2,2,120,384]{4,3,2,1,0:T(8,128)(2,1)S(1)}, u32[]{:S(2)}, u32[]{:S(2)}) %collective-permute-start.49) | collective-permute-done | bytes 737312 | tf_op jit(solution)/shard_map/ppermute | solution.py:676
  361.4 20.6 %collective-permute-done.50 = bf16[2,2,120,384]{3,2,1,0:T(8,128)(2,1)S(1)} collective-permute-done((bf16[2,2,120,384]{3,2,1,0:T(8,128)(2,1)S(1)}, bf16[2,2,120,384]{3,2,1,0:T(8,128)(2,1)S(1)}, u32[]{:S(2)}, u32[]{:S(2)}) %collective-permute-start.50) | collective-permute-done | bytes 368672 | tf_op jit(solution)/shard_map/ppermute | solution.py:676
  385.5 7.4 %collective-permute-done.53 = bf16[2,2,120,384]{3,2,1,0:T(8,128)(2,1)S(1)} collective-permute-done((bf16[2,2,120,384]{3,2,1,0:T(8,128)(2,1)S(1)}, bf16[2,2,120,384]{3,2,1,0:T(8,128)(2,1)S(1)}, u32[]{:S(2)}, u32[]{:S(2)}) %collective-permute-start.53) | collective-permute-done | bytes 368672 | tf_op jit(solution)/shard_map/ppermute | solution.py:676
  397.7 3.9 collective-permute-done.54
  401.7 7.4 %collective-permute-done.46 = bf16[2,2,144,384]{3,2,1,0:T(8,128)(2,1)S(1)} collective-permute-done((bf16[2,2,144,384]{3,2,1,0:T(8,128)(2,1)S(1)}, bf16[2,2,144,384]{3,2,1,0:T(8,128)(2,1)S(1)}, u32[]{:S(2)}, u32[]{:S(2)}) %collective-permute-start.46) | collective-permute-done | bytes 442400 | tf_op jit(solution)/shard_map/ppermute | solution.py:676
  409.4 10.8 %collective-permute-done.47 = bf16[2,144,384]{2,1,0:T(8,128)(2,1)S(1)} collective-permute-done((bf16[2,144,384]{2,1,0:T(8,128)(2,1)S(1)}, bf16[2,144,384]{2,1,0:T(8,128)(2,1)S(1)}, u32[]{:S(2)}, u32[]{:S(2)}) %collective-permute-start.47) | collective-permute-done | bytes 221216 | tf_op jit(solution)/shard_map/ppermute | solution.py:676
  429.9 4.8 %all-to-all-done = f32[32,1,9]{2,1,0:T(1,128)S(1)} async-done(((f32[32,1,9]{2,1,0:T(1,128)}), f32[32,1,9]{2,1,0:T(1,128)S(1)}, u32[]{:S(2)}, u32[]{:S(2)}) %all-to-all-start) | async-done | bytes 1184 | tf_op jit(solution)/shard_map/all_to_all | solution.py:733
  (293 shorter events, 114.0 us)
Async XLA Ops:
  8.3 20.2 %collective-permute-start.31 = (bf16[192,384]{1,0:T(8,128)(2,1)S(1)}, bf16[192,384]{1,0:T(8,128)(2,1)S(1)}, u32[]{:S(2)}, u32[]{:S(2)}) collective-permute-start(bf16[192,384]{1,0:T(8,128)(2,1)S(1)} %get-tuple-element.268), channel_id=1, source_target_pairs={{0,16},{4,20},{8,24},{12,28},{16,0},{20,4},{24,8},{28,12},{1,17},{... | collective-permute-start | bytes 442376 | tf_op jit(solution)/shard_map/ppermute | solution.py:676
  13.2 26.2 %collective-permute-start.21 = (bf16[240,384]{1,0:T(8,128)(2,1)S(1)}, bf16[240,384]{1,0:T(8,128)(2,1)S(1)}, u32[]{:S(2)}, u32[]{:S(2)}) collective-permute-start(bf16[240,384]{1,0:T(8,128)(2,1)S(1)} %get-tuple-element.266), channel_id=1, source_target_pairs={{0,16},{4,20},{8,24},{12,28},{16,0},{20,4},{24,8},{28,12},{1,17},{... | collective-permute-start | bytes 552968 | tf_op jit(solution)/shard_map/ppermute | solution.py:676
  13.3 24.5 %collective-permute-start.11 = (bf16[192,384]{1,0:T(8,128)(2,1)S(1)}, bf16[192,384]{1,0:T(8,128)(2,1)S(1)}, u32[]{:S(2)}, u32[]{:S(2)}) collective-permute-start(bf16[192,384]{1,0:T(8,128)(2,1)S(1)} %get-tuple-element.274), channel_id=1, source_target_pairs={{0,16},{4,20},{8,24},{12,28},{16,0},{20,4},{24,8},{28,12},{1,17},{... | collective-permute-start | bytes 442376 | tf_op jit(solution)/shard_map/ppermute | solution.py:676
  16.3 20.8 %collective-permute-start.1 = (bf16[96,384]{1,0:T(8,128)(2,1)S(1)}, bf16[96,384]{1,0:T(8,128)(2,1)S(1)}, u32[]{:S(2)}, u32[]{:S(2)}) collective-permute-start(bf16[96,384]{1,0:T(8,128)(2,1)S(1)} %get-tuple-element.284), channel_id=1, source_target_pairs={{0,16},{4,20},{8,24},{12,28},{16,0},{20,4},{24,8},{28,12},{1,17},{... | collective-permute-start | bytes 221192 | tf_op jit(solution)/shard_map/ppermute | solution.py:676
  28.5 21.3 %collective-permute-start.32 = (bf16[2,192,384]{2,1,0:T(8,128)(2,1)S(1)}, bf16[2,192,384]{2,1,0:T(8,128)(2,1)S(1)}, u32[]{:S(2)}, u32[]{:S(2)}) collective-permute-start(bf16[2,192,384]{2,1,0:T(8,128)(2,1)S(1)} %pad_maximum_fusion.12), channel_id=1, source_target_pairs={{0,8},{4,12},{8,0},{12,4},{16,24},{20,28},{24,16},{28,20},{1,9},{5... | collective-permute-start | bytes 884744 | tf_op jit(solution)/shard_map/ppermute | solution.py:676
  37.9 19.4 %collective-permute-start.12 = (bf16[2,192,384]{2,1,0:T(8,128)(2,1)S(1)}, bf16[2,192,384]{2,1,0:T(8,128)(2,1)S(1)}, u32[]{:S(2)}, u32[]{:S(2)}) collective-permute-start(bf16[2,192,384]{2,1,0:T(8,128)(2,1)S(1)} %pad_maximum_fusion.11), channel_id=1, source_target_pairs={{0,8},{4,12},{8,0},{12,4},{16,24},{20,28},{24,16},{28,20},{1,9},{5... | collective-permute-start | bytes 884744 | tf_op jit(solution)/shard_map/ppermute | solution.py:676
  39.5 21.2 %collective-permute-start.22 = (bf16[2,240,384]{2,1,0:T(8,128)(2,1)S(1)}, bf16[2,240,384]{2,1,0:T(8,128)(2,1)S(1)}, u32[]{:S(2)}, u32[]{:S(2)}) collective-permute-start(bf16[2,240,384]{2,1,0:T(8,128)(2,1)S(1)} %pad_maximum_fusion.8), channel_id=1, source_target_pairs={{0,8},{4,12},{8,0},{12,4},{16,24},{20,28},{24,16},{28,20},{1,9},{5... | collective-permute-start | bytes 1105928 | tf_op jit(solution)/shard_map/ppermute | solution.py:676
  78.5 16.5 %collective-permute-start.34 = (bf16[2,2,2,96,384]{4,3,2,1,0:T(8,128)(2,1)S(1)}, bf16[2,2,2,96,384]{4,3,2,1,0:T(8,128)(2,1)}, u32[]{:S(2)}, u32[]{:S(2)}) collective-permute-start(bf16[2,2,2,96,384]{4,3,2,1,0:T(8,128)(2,1)S(1)} %pad_maximum_fusion.6.refs_8_), channel_id=1, source_target_pairs={{0,4},{4,0},{8,12},{12,8},{16,20},{20,16},{24,28},{28,24},{1,5},{5... | collective-permute-start | bytes 1769480 | tf_op jit(solution)/shard_map/ppermute | solution.py:676
  83.2 19.5 %collective-permute-start.38 = (bf16[2,2,2,96,384]{4,3,2,1,0:T(8,128)(2,1)S(1)}, bf16[2,2,2,96,384]{4,3,2,1,0:T(8,128)(2,1)}, u32[]{:S(2)}, u32[]{:S(2)}) collective-permute-start(bf16[2,2,2,96,384]{4,3,2,1,0:T(8,128)(2,1)S(1)} %pad_maximum_fusion.7.refs_12_), channel_id=1, source_target_pairs={{0,2},{1,3},{2,0},{3,1},{4,6},{5,7},{6,4},{7,5},{8,10},{9,11},{10,... | collective-permute-start | bytes 1769480 | tf_op jit(solution)/shard_map/ppermute | solution.py:676
  84.7 19.6 %collective-permute-start.35 = (bf16[2,2,2,96,384]{4,3,2,1,0:T(8,128)(2,1)S(1)}, bf16[2,2,2,96,384]{4,3,2,1,0:T(8,128)(2,1)S(1)}, u32[]{:S(2)}, u32[]{:S(2)}) collective-permute-start(bf16[2,2,2,96,384]{4,3,2,1,0:T(8,128)(2,1)S(1)} %pad_maximum_fusion.6.refs_8_), channel_id=1, source_target_pairs={{0,1},{1,0},{2,3},{3,2},{4,5},{5,4},{6,7},{7,6},{8,9},{9,8},{10,11... | collective-permute-start | bytes 1769480 | tf_op jit(solution)/shard_map/ppermute | solution.py:676
  84.8 19.7 %collective-permute-start.39 = (bf16[2,2,2,96,384]{4,3,2,1,0:T(8,128)(2,1)S(1)}, bf16[2,2,2,96,384]{4,3,2,1,0:T(8,128)(2,1)S(1)}, u32[]{:S(2)}, u32[]{:S(2)}) collective-permute-start(bf16[2,2,2,96,384]{4,3,2,1,0:T(8,128)(2,1)S(1)} %pad_maximum_fusion.7.refs_12_), channel_id=1, source_target_pairs={{0,1},{1,0},{2,3},{3,2},{4,5},{5,4},{6,7},{7,6},{8,9},{9,8},{10,11... | collective-permute-start | bytes 1769480 | tf_op jit(solution)/shard_map/ppermute | solution.py:676
  90.0 22.5 %collective-permute-start.18 = (bf16[2,2,2,96,384]{4,3,2,1,0:T(8,128)(2,1)S(1)}, bf16[2,2,2,96,384]{4,3,2,1,0:T(8,128)(2,1)S(1)}, u32[]{:S(2)}, u32[]{:S(2)}) collective-permute-start(bf16[2,2,2,96,384]{4,3,2,1,0:T(8,128)(2,1)S(1)} %pad_maximum_fusion.4), channel_id=1, source_target_pairs={{0,2},{1,3},{2,0},{3,1},{4,6},{5,7},{6,4},{7,5},{8,10},{9,11},{10,... | collective-permute-start | bytes 1769480 | tf_op jit(solution)/shard_map/ppermute | solution.py:676
  95.0 19.0 %collective-permute-start.19 = (bf16[2,2,2,96,384]{4,3,2,1,0:T(8,128)(2,1)S(1)}, bf16[2,2,2,96,384]{4,3,2,1,0:T(8,128)(2,1)S(1)}, u32[]{:S(2)}, u32[]{:S(2)}) collective-permute-start(bf16[2,2,2,96,384]{4,3,2,1,0:T(8,128)(2,1)S(1)} %pad_maximum_fusion.4), channel_id=1, source_target_pairs={{0,1},{1,0},{2,3},{3,2},{4,5},{5,4},{6,7},{7,6},{8,9},{9,8},{10,11... | collective-permute-start | bytes 1769480 | tf_op jit(solution)/shard_map/ppermute | solution.py:676
  104.5 27.2 %collective-permute-start.24 = (bf16[2,2,2,144,384]{4,3,2,1,0:T(8,128)(2,1)S(1)}, bf16[2,2,2,144,384]{4,3,2,1,0:T(8,128)(2,1)}, u32[]{:S(2)}, u32[]{:S(2)}) collective-permute-start(bf16[2,2,2,144,384]{4,3,2,1,0:T(8,128)(2,1)S(1)} %pad_maximum_fusion.refs_0_), channel_id=1, source_target_pairs={{0,4},{4,0},{8,12},{12,8},{16,20},{20,16},{24,28},{28,24},{1,5},{5... | collective-permute-start | bytes 2654216 | tf_op jit(solution)/shard_map/ppermute | solution.py:676
  114.0 18.5 %collective-permute-start.29 = (bf16[2,2,2,96,384]{4,3,2,1,0:T(8,128)(2,1)S(1)}, bf16[2,2,2,96,384]{4,3,2,1,0:T(8,128)(2,1)S(1)}, u32[]{:S(2)}, u32[]{:S(2)}) collective-permute-start(bf16[2,2,2,96,384]{4,3,2,1,0:T(8,128)(2,1)S(1)} %pad_maximum_fusion.5.refs_4_), channel_id=1, source_target_pairs={{0,1},{1,0},{2,3},{3,2},{4,5},{5,4},{6,7},{7,6},{8,9},{9,8},{10,11... | collective-permute-start | bytes 1769480 | tf_op jit(solution)/shard_map/ppermute | solution.py:676
  117.8 15.4 %collective-permute-start.16 = (bf16[2,2,2,96,384]{4,3,2,1,0:T(8,128)(2,1)S(1)}, bf16[2,2,2,96,384]{4,3,2,1,0:T(8,128)(2,1)S(1)}, u32[]{:S(2)}, u32[]{:S(2)}) collective-permute-start(bf16[2,2,2,96,384]{4,3,2,1,0:T(8,128)(2,1)S(1)} %collective-permute-done.14), channel_id=1, source_target_pairs={{0,1},{1,0},{2,3},{3,2},{4,5},{5,4},{6,7},{7,6},{8,9},{9,8},{10,11... | collective-permute-start | bytes 1769480 | tf_op jit(solution)/shard_map/ppermute | solution.py:676
  125.2 35.6 %collective-permute-start.25 = (bf16[2,2,2,144,384]{4,3,2,1,0:T(8,128)(2,1)S(1)}, bf16[2,2,2,144,384]{4,3,2,1,0:T(8,128)(2,1)}, u32[]{:S(2)}, u32[]{:S(2)}) collective-permute-start(bf16[2,2,2,144,384]{4,3,2,1,0:T(8,128)(2,1)S(1)} %pad_maximum_fusion.refs_0_), channel_id=1, source_target_pairs={{0,1},{1,0},{2,3},{3,2},{4,5},{5,4},{6,7},{7,6},{8,9},{9,8},{10,11... | collective-permute-start | bytes 2654216 | tf_op jit(solution)/shard_map/ppermute | solution.py:676
  131.7 29.1 %collective-permute-start.26 = (bf16[2,2,2,144,384]{4,3,2,1,0:T(8,128)(2,1)}, bf16[2,2,2,144,384]{4,3,2,1,0:T(8,128)(2,1)}, u32[]{:S(2)}, u32[]{:S(2)}) collective-permute-start(bf16[2,2,2,144,384]{4,3,2,1,0:T(8,128)(2,1)} %collective-permute-done.24.refs_1_), channel_id=1, source_target_pairs={{0,1},{1,0},{2,3},{3,2},{4,5},{5,4},{6,7},{7,6},{8,9},{9,8},{10,11... | collective-permute-start | bytes 2654216 | tf_op jit(solution)/shard_map/ppermute | solution.py:676
  132.6 28.2 %collective-permute-start.36 = (bf16[2,2,2,96,384]{4,3,2,1,0:T(8,128)(2,1)}, bf16[2,2,2,96,384]{4,3,2,1,0:T(8,128)(2,1)}, u32[]{:S(2)}, u32[]{:S(2)}) collective-permute-start(bf16[2,2,2,96,384]{4,3,2,1,0:T(8,128)(2,1)} %collective-permute-done.34.refs_9_), channel_id=1, source_target_pairs={{0,1},{1,0},{2,3},{3,2},{4,5},{5,4},{6,7},{7,6},{8,9},{9,8},{10,11... | collective-permute-start | bytes 1769480 | tf_op jit(solution)/shard_map/ppermute | solution.py:676
  133.1 27.7 %collective-permute-start.40 = (bf16[2,2,2,96,384]{4,3,2,1,0:T(8,128)(2,1)}, bf16[2,2,2,96,384]{4,3,2,1,0:T(8,128)(2,1)}, u32[]{:S(2)}, u32[]{:S(2)}) collective-permute-start(bf16[2,2,2,96,384]{4,3,2,1,0:T(8,128)(2,1)} %collective-permute-done.38.refs_13_), channel_id=1, source_target_pairs={{0,1},{1,0},{2,3},{3,2},{4,5},{5,4},{6,7},{7,6},{8,9},{9,8},{10,11... | collective-permute-start | bytes 1769480 | tf_op jit(solution)/shard_map/ppermute | solution.py:676
  133.2 27.6 %collective-permute-start.30 = (bf16[2,2,2,96,384]{4,3,2,1,0:T(8,128)(2,1)}, bf16[2,2,2,96,384]{4,3,2,1,0:T(8,128)(2,1)}, u32[]{:S(2)}, u32[]{:S(2)}) collective-permute-start(bf16[2,2,2,96,384]{4,3,2,1,0:T(8,128)(2,1)} %collective-permute-done.28.refs_5_), channel_id=1, source_target_pairs={{0,1},{1,0},{2,3},{3,2},{4,5},{5,4},{6,7},{7,6},{8,9},{9,8},{10,11... | collective-permute-start | bytes 1769480 | tf_op jit(solution)/shard_map/ppermute | solution.py:676
  194.9 65.0 %collective-permute-start.56 = (bf16[2,2,2,2,2,48,768]{6,5,4,3,2,1,0:T(8,128)(2,1)}, bf16[2,2,2,2,2,48,768]{6,5,4,3,2,1,0:T(8,128)(2,1)}, u32[]{:S(2)}, u32[]{:S(2)}) collective-permute-start(bf16[2,2,2,2,2,48,768]{6,5,4,3,2,1,0:T(8,128)(2,1)} %get-tuple-element.108), channel_id=1, source_target_pairs={{0,1},{1,0},{2,3},{3,2},{4,5},{5,4},{6,7},{7,6},{8,9},{9,8},{10,11... | collective-permute-start | bytes 7077896 | tf_op jit(solution)/shard_map/ppermute | solution.py:676
  226.5 107.0 %collective-permute-start.48 = (bf16[2,2,2,2,2,120,384]{6,5,4,3,2,1,0:T(8,128)(2,1)}, bf16[2,2,2,2,2,120,384]{6,5,4,3,2,1,0:T(8,128)(2,1)}, u32[]{:S(2)}, u32[]{:S(2)}) collective-permute-start(bf16[2,2,2,2,2,120,384]{6,5,4,3,2,1,0:T(8,128)(2,1)} %get-tuple-element.105), channel_id=1, source_target_pairs={{0,1},{1,0},{2,3},{3,2},{4,5},{5,4},{6,7},{7,6},{8,9},{9,8},{10,11... | collective-permute-start | bytes 8847368 | tf_op jit(solution)/shard_map/ppermute | solution.py:676
  254.7 90.0 %collective-permute-start.41 = (bf16[2,2,2,2,2,144,384]{6,5,4,3,2,1,0:T(8,128)(2,1)}, bf16[2,2,2,2,2,144,384]{6,5,4,3,2,1,0:T(8,128)(2,1)}, u32[]{:S(2)}, u32[]{:S(2)}) collective-permute-start(bf16[2,2,2,2,2,144,384]{6,5,4,3,2,1,0:T(8,128)(2,1)} %get-tuple-element.100), channel_id=1, source_target_pairs={{0,1},{1,0},{2,3},{3,2},{4,5},{5,4},{6,7},{7,6},{8,9},{9,8},{10,11... | collective-permute-start | bytes 10616840 | tf_op jit(solution)/shard_map/ppermute | solution.py:676
  263.3 62.5 %collective-permute-start.57 = (bf16[2,2,2,48,768]{4,3,2,1,0:T(8,128)(2,1)}, bf16[2,2,2,48,768]{4,3,2,1,0:T(8,128)(2,1)}, u32[]{:S(2)}, u32[]{:S(2)}) collective-permute-start(bf16[2,2,2,48,768]{4,3,2,1,0:T(8,128)(2,1)} %get-tuple-element.218), channel_id=1, source_target_pairs={{0,2},{1,3},{2,0},{3,1},{4,6},{5,7},{6,4},{7,5},{8,10},{9,11},{10,... | collective-permute-start | bytes 1769480 | tf_op jit(solution)/shard_map/ppermute | solution.py:676
  315.8 16.5 %collective-permute-start.59 = (bf16[2,2,2,48,768]{4,3,2,1,0:T(8,128)(2,1)}, bf16[2,2,2,48,768]{4,3,2,1,0:T(8,128)(2,1)}, u32[]{:S(2)}, u32[]{:S(2)}) collective-permute-start(bf16[2,2,2,48,768]{4,3,2,1,0:T(8,128)(2,1)} %get-tuple-element.216), channel_id=1, source_target_pairs={{0,4},{4,0},{8,12},{12,8},{16,20},{20,16},{24,28},{28,24},{1,5},{5... | collective-permute-start | bytes 1769480 | tf_op jit(solution)/shard_map/ppermute | solution.py:676
  336.2 23.0 %collective-permute-start.49 = (bf16[2,2,2,120,384]{4,3,2,1,0:T(8,128)(2,1)S(1)}, bf16[2,2,2,120,384]{4,3,2,1,0:T(8,128)(2,1)S(1)}, u32[]{:S(2)}, u32[]{:S(2)}) collective-permute-start(bf16[2,2,2,120,384]{4,3,2,1,0:T(8,128)(2,1)S(1)} %get-tuple-element.214), channel_id=1, source_target_pairs={{0,2},{1,3},{2,0},{3,1},{4,6},{5,7},{6,4},{7,5},{8,10},{9,11},{10,... | collective-permute-start | bytes 2211848 | tf_op jit(solution)/shard_map/ppermute | solution.py:676
  338.3 21.1 %collective-permute-start.51 = (bf16[2,2,2,120,384]{4,3,2,1,0:T(8,128)(2,1)S(1)}, bf16[2,2,2,120,384]{4,3,2,1,0:T(8,128)(2,1)S(1)}, u32[]{:S(2)}, u32[]{:S(2)}) collective-permute-start(bf16[2,2,2,120,384]{4,3,2,1,0:T(8,128)(2,1)S(1)} %get-tuple-element.212), channel_id=1, source_target_pairs={{0,4},{4,0},{8,12},{12,8},{16,20},{20,16},{24,28},{28,24},{1,5},{5... | collective-permute-start | bytes 2211848 | tf_op jit(solution)/shard_map/ppermute | solution.py:676
  347.5 36.8 %collective-permute-start.42 = (bf16[2,2,2,144,384]{4,3,2,1,0:T(8,128)(2,1)S(1)}, bf16[2,2,2,144,384]{4,3,2,1,0:T(8,128)(2,1)S(1)}, u32[]{:S(2)}, u32[]{:S(2)}) collective-permute-start(bf16[2,2,2,144,384]{4,3,2,1,0:T(8,128)(2,1)S(1)} %get-tuple-element.210), channel_id=1, source_target_pairs={{0,2},{1,3},{2,0},{3,1},{4,6},{5,7},{6,4},{7,5},{8,10},{9,11},{10,... | collective-permute-start | bytes 2654216 | tf_op jit(solution)/shard_map/ppermute | solution.py:676
  347.6 37.4 %collective-permute-start.44 = (bf16[2,2,2,144,384]{4,3,2,1,0:T(8,128)(2,1)S(1)}, bf16[2,2,2,144,384]{4,3,2,1,0:T(8,128)(2,1)S(1)}, u32[]{:S(2)}, u32[]{:S(2)}) collective-permute-start(bf16[2,2,2,144,384]{4,3,2,1,0:T(8,128)(2,1)S(1)} %get-tuple-element.208), channel_id=1, source_target_pairs={{0,4},{4,0},{8,12},{12,8},{16,20},{20,16},{24,28},{28,24},{1,5},{5... | collective-permute-start | bytes 2654216 | tf_op jit(solution)/shard_map/ppermute | solution.py:676
  359.4 22.6 %collective-permute-start.50 = (bf16[2,2,120,384]{3,2,1,0:T(8,128)(2,1)S(1)}, bf16[2,2,120,384]{3,2,1,0:T(8,128)(2,1)S(1)}, u32[]{:S(2)}, u32[]{:S(2)}) collective-permute-start(bf16[2,2,120,384]{3,2,1,0:T(8,128)(2,1)S(1)} %fusion.40), channel_id=1, source_target_pairs={{0,4},{4,0},{8,12},{12,8},{16,20},{20,16},{24,28},{28,24},{1,5},{5... | collective-permute-start | bytes 1105928 | tf_op jit(solution)/shard_map/ppermute | solution.py:676
  359.5 24.5 %collective-permute-start.52 = (bf16[2,2,120,384]{3,2,1,0:T(8,128)(2,1)S(1)}, bf16[2,2,120,384]{3,2,1,0:T(8,128)(2,1)S(1)}, u32[]{:S(2)}, u32[]{:S(2)}) collective-permute-start(bf16[2,2,120,384]{3,2,1,0:T(8,128)(2,1)S(1)} %fusion.43), channel_id=1, source_target_pairs={{0,2},{1,3},{2,0},{3,1},{4,6},{5,7},{6,4},{7,5},{8,10},{9,11},{10,... | collective-permute-start | bytes 1105928 | tf_op jit(solution)/shard_map/ppermute | solution.py:676
  (73 other events, 978.0 us)

commit v2 on v1

v2 whole, which is shorter than its diff:
```python
import functools

import jax
import jax.numpy as jnp
from jax import lax
from jax.experimental import pallas as pl
from jax.experimental.pallas import tpu as pltpu
from jax.sharding import PartitionSpec as P

D = 768
FF = 3072
HEADS = 12
HEAD = 64
WORDS = 512
ENTS = 128
ROWS = WORDS + ENTS
STEP = 7

eps_norm = 1e-05
adam_eps = 1e-06
matrix_decay = 0.01
learn_rate = 0.5
masked_score = -1e30

f32 = jnp.float32
bf16 = jnp.bfloat16
NN = (((1,), (0,)), ((), ()))
NT = (((1,), (1,)), ((), ()))
TN = (((0,), (0,)), ((), ()))
VMEM = pl.BlockSpec(memory_space=pltpu.VMEM)
SMEM = pl.BlockSpec(memory_space=pltpu.SMEM)
ANY = pl.BlockSpec(memory_space=pl.ANY)
COST_RATE = 4e9
PARAMS = pltpu.CompilerParams(vmem_limit_bytes=60 * 2**20)


def dot(left, right, dims):
    return lax.dot_general(left, right, dims, preferred_element_type=f32)


def shape(dims, dtype):
    return jax.ShapeDtypeStruct(dims, dtype)


def tokens(values):
    return [v for v in values if v is not None]


def cost(us, rate=COST_RATE):
    return pl.CostEstimate(flops=int(us * rate), bytes_accessed=0, transcendentals=0)


def away_blocks():
    for core in range(2):
        for outer in range(2):
            for lead in range(2):
                for low in range(2):
                    for high in range(2):
                        yield core, outer, lead, low, high


def places(wide, narrow, second, block):
    core, outer, lead, low, high = block
    x_away, y_away = (outer, lead) if second else (lead, outer)
    w = wide ^ (high * 4 + low * 2 + y_away)
    n = narrow ^ (x_away * 2 + core)
    return w, n


def piece_of(bufs, block):
    core, outer, lead, low, high = block
    return bufs[core * 2 + outer].at[lead, low, high]


def coords():
    return lax.axis_index("wide"), lax.axis_index("narrow")


def start_attention(bufs, second, target, slots, sem):
    wide, narrow = coords()
    for block in away_blocks():
        w, n = places(wide, narrow, second, block)
        row = pl.multiple_of(w * 96 + (n % 2) * 48, 16)
        lane = pl.multiple_of((n // 2) * 384, 128)
        src = piece_of(bufs, block)
        pltpu.make_async_copy(src, target.at[slots, pl.ds(row, 48), pl.ds(lane, 384)], sem).start()


def drain(ref, sem):
    pltpu.make_async_copy(ref, ref, sem).wait()


def prep_kernel(att, exp, red, keep, send, exp_low, red_low, sums):
    narrow = lax.axis_index("narrow")
    core = narrow % 2
    total = []
    for i in range(7):
        value = att[i]
        total.append(jnp.sum(value * value))
        turned = value.T.astype(bf16)
        halves = turned.reshape(2, 48, 192)

        @pl.when(core == 0)
        def _():
            keep[i] = halves[0]
            send[i] = halves[1]

        @pl.when(core == 1)
        def _():
            keep[i] = halves[1]
            send[i] = halves[0]

    value = exp[...]
    total.append(jnp.sum(value * value))
    exp_low[...] = value.astype(bf16)
    value = red[...]
    total.append(jnp.sum(value * value))
    red_low[...] = value.astype(bf16)
    for i in range(9):
        sums[i] = total[i]


def prep(att, exp, red):
    return pl.pallas_call(
        prep_kernel,
        in_specs=[VMEM] * 3,
        out_specs=[VMEM] * 4 + [SMEM],
        out_shape=[
            shape((7, 48, 192), bf16),
            shape((7, 48, 192), bf16),
            shape((192, 384), bf16),
            shape((96, D), bf16),
            shape((9,), f32),
        ],
        compiler_params=PARAMS,
        name="prep",
    )(att, exp, red)


def pick_rows(source, mine, other):
    core = lax.axis_index("narrow") % 2
    for c in range(2):

        @pl.when(core == c)
        def _():
            for target, at in ((mine, c * 192), (other, 192 - c * 192)):
                target[:, :192] = source[:, at : at + 192]
                target[:, 192:] = source[:, at + 384 : at + 576]


def pick_tiles(source, mine, other):
    core = lax.axis_index("narrow") % 2
    for c in range(2):

        @pl.when(core == c)
        def _():
            for target, at in ((mine, c * 192), (other, 192 - c * 192)):
                target[:, :128] = source[:, at : at + 128]
                target[:, 128:256] = source[:, at + 384 : at + 512]
                target[:, 256:320] = source[:, at + 128 : at + 192]
                target[:, 320:] = source[:, at + 512 : at + 576]


def project_kv_kernel(fast, n_after, word, ent, *refs):
    if fast:
        first, second, refs = refs[:4], refs[4:8], refs[8:]
    else:
        whole, refs = refs[0], refs[1:]
    low, keys, values, mine, other, saved, target, sem, sem_save = refs[n_after:]
    if fast:
        start_attention(first, False, target, pl.ds(0, 1), sem)
        start_attention(second, True, target, pl.ds(1, 1), sem)
    else:
        pltpu.make_async_copy(whole.at[pl.ds(4, 2)], target, sem).start()
    low[:WORDS] = word[...].astype(bf16)
    low[WORDS:] = ent[...].astype(bf16)
    pick_tiles(low, mine, other)
    drain(target, sem)
    save = pltpu.make_async_copy(target, saved, sem_save)
    save.start()
    keys[...] = dot(low[...], target[0], NT).astype(bf16)
    values[...] = dot(low[...], target[1], NT).astype(bf16)
    save.wait()


def project_kv(fast, word, ent, pieces, after=()):
    after = tokens(after)
    return pl.pallas_call(
        functools.partial(project_kv_kernel, fast, len(after)),
        in_specs=[VMEM, VMEM] + [ANY] * (len(pieces) + len(after)),
        out_specs=[VMEM] * 5 + [ANY],
        out_shape=[shape((ROWS, D), bf16)] * 3
        + [shape((ROWS, D // 2), bf16)] * 2
        + [shape((2, D, D), bf16)],
        scratch_shapes=[
            pltpu.VMEM((2, D, D), bf16),
            pltpu.SemaphoreType.DMA,
            pltpu.SemaphoreType.DMA,
        ],
        compiler_params=PARAMS,
        cost_estimate=cost(6, 4e8),
        name="project_kv",
    )(word, ent, *pieces, *after)


def project_q_kernel(fast, n_after, low, *refs):
    if fast:
        first, second, refs = refs[:4], refs[4:8], refs[8:]
    else:
        whole, refs = refs[0], refs[1:]
    to_words, to_ents, saved, target, sem, sem_save = refs[n_after:]
    if fast:
        start_attention(first, False, target, pl.ds(0, 2), sem)
        start_attention(second, True, target, pl.ds(2, 2), sem)
    else:
        for slot, k in enumerate((0, 2, 1, 3)):
            pltpu.make_async_copy(whole.at[k], target.at[slot], sem).start()
    drain(target, sem)
    save = pltpu.make_async_copy(target, saved, sem_save)
    save.start()
    scale = HEAD ** (-0.5)
    word = low[:WORDS]
    ent = low[WORDS:]
    to_words[:WORDS] = (dot(word, target[0], NT) * scale).astype(bf16)
    to_words[WORDS:] = (dot(ent, target[1], NT) * scale).astype(bf16)
    to_ents[:WORDS] = (dot(word, target[2], NT) * scale).astype(bf16)
    to_ents[WORDS:] = (dot(ent, target[3], NT) * scale).astype(bf16)
    save.wait()


def project_q(fast, low, pieces, after=()):
    after = tokens(after)
    return pl.pallas_call(
        functools.partial(project_q_kernel, fast, len(after)),
        in_specs=[VMEM] + [ANY] * (len(pieces) + len(after)),
        out_specs=[VMEM] * 2 + [ANY],
        out_shape=[shape((ROWS, D), bf16)] * 2 + [shape((4, D, D), bf16)],
        scratch_shapes=[
            pltpu.VMEM((4, D, D), bf16),
            pltpu.SemaphoreType.DMA,
            pltpu.SemaphoreType.DMA,
        ],
        compiler_params=PARAMS,
        cost_estimate=cost(7, 4e8),
        name="project_q",
    )(low, *pieces, *after)


def head_masks(counts):
    lane = lax.broadcasted_iota(jnp.int32, (ROWS, 128), 1)
    row = lax.broadcasted_iota(jnp.int32, (ROWS, 128), 0)
    edge = jnp.where(row < WORDS, counts[0], counts[1] + WORDS)
    bias = jnp.where(row < edge, 0.0, masked_score)
    out = []
    for h in range(2):
        own = jnp.where((lane < HEAD) if h == 0 else (lane >= HEAD), 1.0, 0.0).astype(bf16)
        mark = jnp.where(lane == (HEAD if h == 0 else 0), 1.0, 0.0)
        rest = (1.0 - mark).astype(bf16)
        tag = (bias * mark).astype(bf16)
        out.append((own, mark.astype(bf16), rest, tag))
    return out


def scores_of(masks, keys, to_words, to_ents):
    own, mark, rest, tag = masks
    tagged = keys * own + tag
    upper = dot(tagged[:WORDS], to_words * rest + mark, NT)
    lower = dot(tagged[WORDS:], to_ents * rest + mark, NT)
    return jnp.concatenate([upper, lower], 0)


def attend_kernel(n_after, counts, to_words, to_ents, keys, values, *refs):
    context, exact, lse = refs[n_after:]
    masks = head_masks(counts)
    outs = []
    for h in range(2):
        scores = scores_of(masks[h], keys[...], to_words[...], to_ents[...])
        top = jnp.max(scores, axis=0, keepdims=True)
        expd = jnp.exp(scores - top)
        total = jnp.sum(expd, axis=0, keepdims=True)
        lse[h : h + 1, :] = top + jnp.log(total)
        mixed = dot(values[:, h * HEAD : (h + 1) * HEAD], expd.astype(bf16), TN)
        outs.append(mixed * (1.0 / total))
    joined = jnp.concatenate(outs, 0).T
    exact[...] = joined
    context[...] = joined.astype(bf16)


def attend(counts, to_words, to_ents, keys, values, after=()):
    after = tokens(after)
    pair = pl.BlockSpec((ROWS, 128), lambda i: (0, i))
    stat = pl.BlockSpec((None, 2, ROWS), lambda i: (i, 0, 0))
    return pl.pallas_call(
        functools.partial(attend_kernel, len(after)),
        grid=(HEADS // 2,),
        in_specs=[SMEM, pair, pair, pair, pair] + [ANY] * len(after),
        out_specs=[pair, pair, stat],
        out_shape=[
            shape((ROWS, D), bf16),
            shape((ROWS, D), f32),
            shape((HEADS // 2, 2, ROWS), f32),
        ],
        compiler_params=PARAMS,
        cost_estimate=cost(12, 4e8),
        name="attend",
    )(counts, to_words, to_ents, keys, values, *after)


def normed(value):
    center = value - jnp.mean(value, axis=-1, keepdims=True)
    spread = jnp.mean(center * center, axis=-1, keepdims=True)
    inverse = lax.rsqrt(spread + eps_norm)
    return center * inverse, inverse


def normed_back(unit, inverse, cotangent):
    mean = jnp.mean(cotangent, axis=-1, keepdims=True)
    inner = jnp.mean(cotangent * unit, axis=-1, keepdims=True)
    return inverse * (cotangent - mean - unit * inner)


def column_sum(value):
    return jnp.sum(value, axis=0, keepdims=True)


def feed_in_kernel(fast, n_after, word, ent, context, norms, *refs):
    if fast:
        bufs, refs = (refs[0:4], refs[4:8]), refs[8:]
    else:
        bufs, refs = refs[0:2], refs[2:]
    (
        middle,
        middle_low,
        activated,
        slope,
        unit_one,
        inverse_one,
        middle_mine,
        middle_other,
        context_mine,
        context_other,
        out_saved,
        exp_saved,
        out_all,
        exp_all,
        sem_out,
        sem_exp,
        sem_save,
    ) = refs[n_after:]
    step = pl.program_id(0)
    save_out = pltpu.make_async_copy(out_all, out_saved, sem_save.at[0])
    save_exp = pltpu.make_async_copy(exp_all, exp_saved, sem_save.at[1])

    @pl.when(step == 0)
    def _():
        if fast:
            start_feed_in(bufs, out_all, exp_all, sem_out, sem_exp)
        else:
            pltpu.make_async_copy(bufs[0].at[6], out_all, sem_out).start()
            for j in range(4):
                cols = pl.ds(j * D, D)
                pltpu.make_async_copy(bufs[1].at[:, cols], exp_all.at[j], sem_exp).start()
        drain(out_all, sem_out)
        save_out.start()
        hidden = jnp.concatenate([word[...], ent[...]], 0)
        unit, inverse = normed(hidden + dot(context[...], out_all[...], NT))
        value = unit * norms[0:1, :] + norms[1:2, :]
        unit_one[...] = unit
        inverse_one[...] = inverse
        middle_low[...] = value.astype(bf16)
        middle[...] = value
        pick_rows(middle_low, middle_mine, middle_other)
        pick_tiles(context, context_mine, context_other)
        drain(exp_all, sem_exp)
        save_exp.start()

    inner = dot(middle_low[...], exp_all[step], NN)
    share = 0.5 + 0.5 * lax.erf(inner * 0.7071067811865476)
    bell = jnp.exp(-0.5 * inner * inner) * 0.3989422804014327
    slope[...] = (share + inner * bell).astype(bf16)
    activated[...] = (inner * share).astype(bf16)

    @pl.when(step == 3)
    def _():
        save_out.wait()
        save_exp.wait()


def start_feed_in(bufs, out_all, exp_all, sem_out, sem_exp):
    wide, narrow = coords()
    for block in away_blocks():
        w, n = places(wide, narrow, False, block)
        row = pl.multiple_of(w * 96 + (n % 2) * 48, 16)
        lane = pl.multiple_of((n // 2) * 384, 128)
        src = piece_of(bufs[0], block).at[pl.ds(96, 48)]
        pltpu.make_async_copy(src, out_all.at[pl.ds(row, 48), pl.ds(lane, 384)], sem_out).start()
    for half in range(2):
        for block in away_blocks():
            w, n = places(wide, narrow, half == 1, block)
            src = piece_of(bufs[half], block)
            if half == 0:
                src = src.at[pl.ds(0, 96)]
            row = pl.multiple_of(n * 192 + half * 96, 16)
            lane = pl.multiple_of((w % 2) * 384, 128)
            dst = exp_all.at[w // 2, pl.ds(row, 96), pl.ds(lane, 384)]
            pltpu.make_async_copy(src, dst, sem_exp).start()


def feed_in(fast, word, ent, context, norms, pieces, after=()):
    after = tokens(after)
    column = pl.BlockSpec((ROWS, D), lambda i: (0, i))
    return pl.pallas_call(
        functools.partial(feed_in_kernel, fast, len(after)),
        grid=(4,),
        in_specs=[VMEM] * 4 + [ANY] * (len(pieces) + len(after)),
        out_specs=[VMEM] * 2 + [column, column] + [VMEM] * 6 + [ANY] * 2,
        out_shape=[
            shape((ROWS, D), f32),
            shape((ROWS, D), bf16),
            shape((ROWS, FF), bf16),
            shape((ROWS, FF), bf16),
            shape((ROWS, D), f32),
            shape((ROWS, 1), f32),
            shape((ROWS, D // 2), bf16),
            shape((ROWS, D // 2), bf16),
            shape((ROWS, D // 2), bf16),
            shape((ROWS, D // 2), bf16),
            shape((D, D), bf16),
            shape((4, D, D), bf16),
        ],
        scratch_shapes=[
            pltpu.VMEM((D, D), bf16),
            pltpu.VMEM((4, D, D), bf16),
            pltpu.SemaphoreType.DMA,
            pltpu.SemaphoreType.DMA,
            pltpu.SemaphoreType.DMA((2,)),
        ],
        compiler_params=PARAMS,
        cost_estimate=cost(15),
        name="feed_in",
    )(word, ent, context, norms, *pieces, *after)


def feed_out_kernel(fast, n_after, activated, middle, norms, word_cot, ent_cot, *refs):
    if fast:
        bufs, refs = (refs[0:4], refs[4:8]), refs[8:]
    else:
        bufs, refs = refs[0:1], refs[1:]
    (
        word_out,
        ent_out,
        d_second,
        d_ffn,
        grads_two,
        red_saved,
        total,
        red_all,
        sem_red,
        sem_save,
    ) = refs[n_after:]
    step = pl.program_id(0)
    save = pltpu.make_async_copy(red_all, red_saved, sem_save)

    @pl.when(step == 0)
    def _():
        if fast:
            start_feed_out(bufs, red_all, sem_red)
        else:
            for j in range(4):
                cols = pl.ds(j * D, D)
                pltpu.make_async_copy(bufs[0].at[:, cols], red_all.at[j], sem_red).start()
        total[...] = middle[...]
        drain(red_all, sem_red)
        save.start()

    total[...] += dot(activated[...], red_all[step], NT)

    @pl.when(step == 3)
    def _():
        unit, inverse = normed(total[...])
        result = unit * norms[2:3, :] + norms[3:4, :]
        word_out[...] = result[:WORDS]
        ent_out[...] = result[WORDS:]
        cot = jnp.concatenate([word_cot[...], ent_cot[...]], 0)
        grads_two[0:1, :] = column_sum(cot * unit)
        grads_two[1:2, :] = column_sum(cot)
        back = normed_back(unit, inverse, cot * norms[2:3, :])
        d_second[...] = back
        d_ffn[...] = back.astype(bf16)
        save.wait()


def start_feed_out(bufs, red_all, sem_red):
    wide, narrow = coords()
    for half in range(2):
        for block in away_blocks():
            w, n = places(wide, narrow, half == 1, block)
            src = piece_of(bufs[half], block)
            row = pl.multiple_of(w * 96 + half * 48, 16)
            pltpu.make_async_copy(src, red_all.at[n, pl.ds(row, 48)], sem_red).start()


def feed_out(fast, activated, middle, norms, word_cot, ent_cot, pieces, after=()):
    after = tokens(after)
    column = pl.BlockSpec((ROWS, D), lambda i: (0, i))
    return pl.pallas_call(
        functools.partial(feed_out_kernel, fast, len(after)),
        grid=(4,),
        in_specs=[column] + [VMEM] * 4 + [ANY] * (len(pieces) + len(after)),
        out_specs=[VMEM] * 5 + [ANY],
        out_shape=[
            shape((WORDS, D), f32),
            shape((ENTS, D), f32),
            shape((ROWS, D), f32),
            shape((ROWS, D), bf16),
            shape((2, D), f32),
            shape((4, D, D), bf16),
        ],
        scratch_shapes=[
            pltpu.VMEM((ROWS, D), f32),
            pltpu.VMEM((4, D, D), bf16),
            pltpu.SemaphoreType.DMA,
            pltpu.SemaphoreType.DMA,
        ],
        compiler_params=PARAMS,
        cost_estimate=cost(13),
        name="feed_out",
    )(activated, middle, norms, word_cot, ent_cot, *pieces, *after)


def feed_back_one_kernel(n_after, d_ffn, red_all, exp_all, slope, d_second, *refs):
    d_inner, total = refs[n_after:]
    step = pl.program_id(0)
    back = (dot(d_ffn[...], red_all[...], NN) * slope[...].astype(f32)).astype(bf16)
    d_inner[...] = back

    @pl.when(step == 0)
    def _():
        total[...] = d_second[...]

    total[...] += dot(back, exp_all[...], NT)


def feed_back_one(first, d_ffn, red_all, exp_all, slope, d_second, after=()):
    after = tokens(after)
    wide = pl.BlockSpec((ROWS, D), lambda i: (0, i + first))
    column = pl.BlockSpec((ROWS, D), lambda i: (0, i))
    part = pl.BlockSpec((None, D, D), lambda i: (i + first, 0, 0))
    return pl.pallas_call(
        functools.partial(feed_back_one_kernel, len(after)),
        grid=(2,),
        in_specs=[VMEM, part, part, wide, VMEM] + [ANY] * len(after),
        out_specs=[column, VMEM],
        out_shape=[shape((ROWS, FF // 2), bf16), shape((ROWS, D), f32)],
        compiler_params=PARAMS,
        cost_estimate=cost(10),
        name="feed_back_one",
    )(d_ffn, red_all, exp_all, slope, d_second, *after)


def feed_back_two_kernel(
    n_after, d_ffn, red_all, exp_all, slope, d_second, unit_one, inverse_one, norms, out_all, exact, *refs
):
    d_inner, d_first, d_out, d_context, row_inner, grads_one, total = refs[n_after:]
    step = pl.program_id(0)
    back = (dot(d_ffn[...], red_all[...], NN) * slope[...].astype(f32)).astype(bf16)
    d_inner[...] = back

    @pl.when(step == 0)
    def _():
        total[...] = d_second[...]

    total[...] += dot(back, exp_all[...], NT)

    @pl.when(step == 1)
    def _():
        d_middle = total[...]
        unit = unit_one[...]
        grads_one[0:1, :] = column_sum(d_middle * unit)
        grads_one[1:2, :] = column_sum(d_middle)
        first = normed_back(unit, inverse_one[...], d_middle * norms[0:1, :])
        d_first[...] = first
        d_out[...] = first.astype(bf16)
        context = dot(first.astype(bf16), out_all[...], NN).astype(bf16)
        d_context[...] = context
        product = context.astype(f32) * exact[...]
        head = lax.broadcasted_iota(jnp.int32, (16, D), 1) // HEAD
        pick = jnp.where(head == lax.broadcasted_iota(jnp.int32, (16, D), 0), 1.0, 0.0).astype(bf16)
        high = product.astype(bf16)
        low = (product - high.astype(f32)).astype(bf16)
        sums = dot(pick, high, NT) + dot(pick, low, NT)
        for i in range(HEADS // 2):
            row_inner[i] = sums[2 * i : 2 * i + 2]


def feed_back_two(
    first, d_ffn, red_all, exp_all, slope, d_second, unit_one, inverse_one, norms, out_all, exact, after=()
):
    after = tokens(after)
    wide = pl.BlockSpec((ROWS, D), lambda i: (0, i + first))
    column = pl.BlockSpec((ROWS, D), lambda i: (0, i))
    part = pl.BlockSpec((None, D, D), lambda i: (i + first, 0, 0))
    return pl.pallas_call(
        functools.partial(feed_back_two_kernel, len(after)),
        grid=(2,),
        in_specs=[VMEM, part, part, wide] + [VMEM] * 6 + [ANY] * len(after),
        out_specs=[column] + [VMEM] * 5,
        out_shape=[
            shape((ROWS, FF // 2), bf16),
            shape((ROWS, D), f32),
            shape((ROWS, D), bf16),
            shape((ROWS, D), bf16),
            shape((HEADS // 2, 2, ROWS), f32),
            shape((2, D), f32),
        ],
        scratch_shapes=[pltpu.VMEM((ROWS, D), f32)],
        compiler_params=PARAMS,
        cost_estimate=cost(15),
        name="feed_back_two",
    )(d_ffn, red_all, exp_all, slope, d_second, unit_one, inverse_one, norms, out_all, exact, *after)


def attend_back_kernel(
    n_after, counts, to_words, to_ents, keys, values, d_context, lse, row_inner, *refs
):
    d_to_words, d_to_ents, d_keys, d_values = refs[n_after:]
    masks = head_masks(counts)
    scale = HEAD ** (-0.5)
    one, two, three, four = [], [], [], []
    for h in range(2):
        cols = slice(h * HEAD, (h + 1) * HEAD)
        scores = scores_of(masks[h], keys[...], to_words[...], to_ents[...])
        probs = jnp.exp(scores - lse[h : h + 1, :])
        d_probs = dot(values[...] * masks[h][0], d_context[...], NT)
        d_scores = (probs * (d_probs - row_inner[h : h + 1, :])).astype(bf16)
        one.append(dot(keys[:WORDS, cols], d_scores[:WORDS], TN))
        two.append(dot(keys[WORDS:, cols], d_scores[WORDS:], TN))
        three.append(
            jnp.concatenate(
                [
                    dot(d_scores[:WORDS], to_words[:, cols], NN),
                    dot(d_scores[WORDS:], to_ents[:, cols], NN),
                ],
                0,
            )
        )
        four.append(dot(probs.astype(bf16), d_context[:, cols], NN))
    d_to_words[...] = (jnp.concatenate(one, 0).T * scale).astype(bf16)
    d_to_ents[...] = (jnp.concatenate(two, 0).T * scale).astype(bf16)
    d_keys[...] = jnp.concatenate(three, 1).astype(bf16)
    d_values[...] = jnp.concatenate(four, 1).astype(bf16)


def attend_back(first, counts, to_words, to_ents, keys, values, d_context, lse, row_inner, after=()):
    after = tokens(after)
    pair = pl.BlockSpec((ROWS, 128), lambda i: (0, i + first))
    column = pl.BlockSpec((ROWS, 128), lambda i: (0, i))
    stat = pl.BlockSpec((None, 2, ROWS), lambda i: (i + first, 0, 0))
    return pl.pallas_call(
        functools.partial(attend_back_kernel, len(after)),
        grid=(HEADS // 4,),
        in_specs=[SMEM] + [pair] * 5 + [stat] * 2 + [ANY] * len(after),
        out_specs=[column] * 4,
        out_shape=[shape((ROWS, D // 2), bf16)] * 4,
        compiler_params=PARAMS,
        cost_estimate=cost(10),
        name="attend_back",
    )(counts, to_words, to_ents, keys, values, d_context, lse, row_inner, *after)


def relative():
    for x in range(2):
        for y in range(2):
            for low in range(2):
                for high in range(2):
                    yield x, y, low, high


def emit(mine, got, outs, half, first, rest, rows, value):
    if not mine:
        outs[0][(half, first) + rest + (rows,)] = value.astype(bf16)
        return
    value = (value + got[(half, first) + rest + (rows,)].astype(f32)).astype(bf16)
    if first:
        outs[half][rest + (rows,)] = value
    else:
        outs[2][(half,) + rest + (rows,)] = value


def grad_call(kernel, name, mine, operands, got, dims, extra, after):
    after = tokens(after)
    zs, rows, lanes = dims
    if mine:
        outs = [shape((2,) + zs + (rows, lanes), bf16)] * 2
        outs += [shape((2, 2) + zs + (rows, lanes), bf16)]
        operands = list(operands) + [got]
    else:
        outs = [shape((2, 2, 2) + zs + (rows, lanes), bf16)]
    return pl.pallas_call(
        functools.partial(kernel, mine, len(after), len(outs)),
        in_specs=[VMEM] * len(operands) + [ANY] * len(after),
        out_specs=[VMEM] * len(outs),
        out_shape=outs,
        scratch_shapes=extra,
        compiler_params=PARAMS,
        cost_estimate=cost(7),
        name=name,
    )(*operands, *after)


def split_refs(mine, n_after, n_outs, refs):
    got, refs = (refs[0], refs[1:]) if mine else (None, refs)
    refs = refs[n_after:]
    return got, refs[:n_outs], refs[n_outs:]


def grad_red_kernel(mine, n_after, n_outs, d_ffn, activated, *refs):
    got, outs, (whole,) = split_refs(mine, n_after, n_outs, refs)
    wide, narrow = coords()
    core = 0 if mine else 1
    for x in range(2):
        n = narrow ^ (x * 2 + core)
        lanes = pl.ds(pl.multiple_of(n * D, D), D)
        whole[...] = dot(d_ffn[...], activated[:, lanes], TN)
        for y in range(2):
            for low in range(2):
                for high in range(2):
                    w = wide ^ (high * 4 + low * 2 + y)
                    for half in range(2):
                        rows = pl.ds(pl.multiple_of(w * 96 + half * 48, 16), 48)
                        first, second = (x, y) if half == 0 else (y, x)
                        emit(
                            mine, got, outs, half, first, (second, low, high), slice(0, 48), whole[rows, :]
                        )


def grad_red(mine, d_ffn, activated, got=None, after=()):
    return grad_call(
        grad_red_kernel,
        "grad_red",
        mine,
        (d_ffn, activated),
        got,
        ((2, 2), 48, D),
        [pltpu.VMEM((D, D), f32)],
        after,
    )


def grad_exp_kernel(mine, n_after, n_outs, middle, d_inner_one, d_inner_two, d_out, context, *refs):
    got, outs, (whole, turned) = split_refs(mine, n_after, n_outs, refs)
    wide, narrow = coords()
    for z in range(4):
        d_inner = d_inner_one if z < 2 else d_inner_two
        whole[z] = dot(middle[...], d_inner[:, (z % 2) * D : (z % 2 + 1) * D], TN)
    for x, y, low, high in relative():
        z = (wide // 2) ^ (high * 2 + low)
        lanes = pl.ds(pl.multiple_of(((wide % 2) ^ y) * 384, 128), 384)
        for half in range(2):
            rows = pl.ds(pl.multiple_of((narrow // 2 ^ x) * 192 + half * 96, 16), 96)
            first, second = (x, y) if half == 0 else (y, x)
            emit(
                mine, got, outs, half, first, (second, low, high), slice(0, 96), whole[z, rows, lanes]
            )
    turned[...] = dot(d_out[...], context[...], TN)
    for y in range(2):
        for low in range(2):
            for high in range(2):
                w = wide ^ (high * 4 + low * 2 + y)
                blocks = packed(turned, w * 96, narrow)
                for x in range(2):
                    for half in range(2):
                        first, second = (x, y) if half == 0 else (y, x)
                        value = blocks[x][half * 16 : half * 16 + 32]
                        emit(
                            mine, got, outs, half, first, (second, low, high), slice(96, 128), value
                        )


def packed(turned, start, narrow):
    upper = pl.ds(pl.multiple_of(start, 16), 48)
    lower = pl.ds(pl.multiple_of(start + 48, 16), 48)
    tail_upper = turned[upper, 256:]
    tail_lower = turned[lower, 256:]
    tails = (
        jnp.concatenate([tail_upper[:, :64], tail_lower[:, :64]], 1),
        jnp.concatenate([tail_upper[:, 64:], tail_lower[:, 64:]], 1),
    )
    x_own = narrow // 2
    out = []
    for x in range(2):
        lanes = pl.ds(pl.multiple_of((x_own ^ x) * 128, 128), 128)
        tail = jnp.where(x_own == x, tails[0], tails[1])
        out.append(jnp.concatenate([turned[upper, lanes], turned[lower, lanes], tail], 1))
    return out


def unpacked(block):
    upper = jnp.concatenate([block[..., :128], block[..., 256:320]], -1)
    lower = jnp.concatenate([block[..., 128:256], block[..., 320:]], -1)
    return jnp.concatenate([upper, lower], -2)


def grad_exp(mine, middle, d_inner_one, d_inner_two, d_out, context, got=None, after=()):
    return grad_call(
        grad_exp_kernel,
        "grad_exp",
        mine,
        (middle, d_inner_one, d_inner_two, d_out, context),
        got,
        ((2, 2), 128, 384),
        [pltpu.VMEM((4, 384, D), f32), pltpu.VMEM((D, 384), f32)],
        after,
    )


def grad_att_kernel(part, mine, n_after, n_outs, picked, d_to_words, d_to_ents, d_keys, d_values, *refs):
    got, outs, (turned,) = split_refs(mine, n_after, n_outs, refs)
    wide, narrow = coords()
    work = (
        (d_keys, slice(0, ROWS), 0, 0),
        (d_to_words, slice(0, WORDS), 0, 1),
        (d_to_words, slice(WORDS, ROWS), 0, 2),
        (d_values, slice(0, ROWS), 1, 0),
        (d_to_ents, slice(0, WORDS), 1, 1),
        (d_to_ents, slice(WORDS, ROWS), 1, 2),
    )
    for ref, rows, half, at in work:
        turned[...] = dot(ref[rows, :], picked[rows, :], TN)
        for y in range(2):
            for low in range(2):
                w = (wide % 4) ^ (low * 2 + y)
                blocks = packed(turned, w * 96, narrow)
                for x in range(2):
                    first, second = (x, y) if half == 0 else (y, x)
                    where = slice(at * 48, at * 48 + 48)
                    emit(mine, got, outs, half, first, (second, low), where, blocks[x])


def grad_att(part, mine, picked, grads, got=None, after=()):
    return grad_call(
        functools.partial(grad_att_kernel, part),
        "grad_att",
        mine,
        (picked,) + tuple(grads),
        got,
        ((2,), 144, 384),
        [pltpu.VMEM((D // 2, 384), f32)],
        after,
    )


def grad_hidden_kernel(n_after, d_first, *refs):
    grads, (kv, q), (word, ent) = refs[:8], refs[8:10], refs[10 + n_after :]
    d_to_words, d_to_ents, d_keys, d_values = [
        jnp.concatenate([grads[i][...], grads[4 + i][...]], 1) for i in range(4)
    ]
    shared = d_first[...] + dot(d_keys, kv[0], NN) + dot(d_values, kv[1], NN)
    word[...] = (
        shared[:WORDS] + dot(d_to_words[:WORDS], q[0], NN) + dot(d_to_ents[:WORDS], q[2], NN)
    )
    ent[...] = (
        shared[WORDS:] + dot(d_to_words[WORDS:], q[1], NN) + dot(d_to_ents[WORDS:], q[3], NN)
    )


def grad_hidden(d_first, grads, kv, q, after=()):
    after = tokens(after)
    return pl.pallas_call(
        functools.partial(grad_hidden_kernel, len(after)),
        in_specs=[VMEM] * 11 + [ANY] * len(after),
        out_specs=[VMEM] * 2,
        out_shape=[shape((WORDS, D), f32), shape((ENTS, D), f32)],
        compiler_params=PARAMS,
        cost_estimate=cost(9),
        name="grad_hidden",
    )(d_first, *grads, kv, q, *after)


def flip(axis, bit, value):
    size = lax.axis_size(axis)
    return lax.ppermute(value, axis, [(i, i ^ bit) for i in range(size)])


def over(name, value):
    axis, bit = {
        "core": ("narrow", 1),
        "x": ("narrow", 2),
        "y": ("wide", 1),
        "low": ("wide", 2),
        "high": ("wide", 4),
    }[name]
    return flip(axis, bit, value)


class Links:
    def __init__(self):
        self.past = {}

    def send(self, name, value):
        kind = "z" if name in ("low", "high") else name
        past = self.past.setdefault(kind, [])
        if len(past) > 1:
            value, unused = lax.optimization_barrier((value, past[-2]))
        got = over(name, value)
        past.append(got)
        return got


def later(values, token):
    return lax.optimization_barrier((tuple(values), token))[0]


def gather_high(links, first, second):
    both = jnp.concatenate([first, second], 0)
    return both, links.send("high", both)


def gather_low(links, cut, both):
    both = jnp.stack(both, 0)
    got = links.send("low", both)
    left = jnp.stack([both[:, :cut], got[:, :cut]], 0)
    right = jnp.stack([both[:, cut:], got[:, cut:]], 0)
    return left, right


def gather_near(links, left, right):
    got_left = links.send("x", left)
    got_right = links.send("y", right)
    left = jnp.stack([left, got_left], 0)
    right = jnp.stack([right, got_right], 0)
    return left, right


def gather_far(links, left, right):
    return gather_core(left, right, links.send("y", left), links.send("x", right))


def gather_core(left, right, left_far, right_far, token=None):
    left_core = over("core", left)
    right_core = over("core", right)
    if token is not None:
        left_far, right_far = later((left_far, right_far), token)
    return (
        left,
        left_far,
        left_core,
        over("core", left_far),
        right,
        right_far,
        right_core,
        over("core", right_far),
    )


def plus(kept, got):
    return (kept.astype(f32) + got.astype(f32)).astype(bf16)


class Sum:
    def __init__(self, send_left, send_right, keep):
        self.keep = keep
        self.got = over("x", send_left), over("y", send_right)

    def wait(self, token):
        self.got = later(self.got, token) if isinstance(self.got, tuple) else later((self.got,), token)[0]
        return self

    def second(self):
        left, right = self.got
        keep = self.keep
        self.got = (
            over("y", plus(keep[0, 1], left[1])),
            over("x", plus(keep[1, 1], right[1])),
        )
        self.keep = plus(keep[0, 0], left[0]), plus(keep[1, 0], right[0])
        return self.got

    def third(self):
        left, right = self.got
        keep = jnp.stack([plus(self.keep[0], left), plus(self.keep[1], right)], 1)
        self.keep = keep[0]
        self.got = over("low", keep[1])
        return self.got

    def low(self):
        return plus(self.keep, self.got)

    def fourth(self):
        keep = self.low()
        self.keep = keep[:, 0]
        self.got = over("high", keep[:, 1])
        return self.got

    def result(self):
        return self.keep.astype(f32) + self.got.astype(f32)


def sum_all(value):
    size = lax.axis_size("wide") * lax.axis_size("narrow")
    spread = jnp.broadcast_to(value[None], (size,) + value.shape)
    got = lax.all_to_all(spread, ("wide", "narrow"), 0, 0, tiled=False)
    return jnp.sum(got, axis=0)


def adapt(weight, grad, first, second, decay):
    first = 0.5 * first + 0.5 * grad
    second = 0.5 * second + 0.5 * grad * grad
    fix_first = 1.0 - 0.5**STEP
    fix_second = 1.0 - 0.5**STEP
    update = first / fix_first / (jnp.sqrt(second / fix_second) + adam_eps) + decay * weight
    return (first, second, update)


def shards(
    fast,
    word_states,
    entity_states,
    seq_counts,
    attention_weight,
    expand_weight,
    reduce_weight,
    norm_params,
    moment_attention,
    moment_expand,
    moment_reduce,
    moment_norms,
    square_attention,
    square_expand,
    square_reduce,
    square_norms,
    word_cotangent,
    entity_cotangent,
):
    word, ent, counts = word_states[0], entity_states[0], seq_counts[0]
    core = lax.axis_index("narrow") % 2
    high = lax.axis_index("wide") // 4
    if fast:
        keep, send, exp_low, red_low, weight_local = prep(
            attention_weight, expand_weight, reduce_weight.T
        )
        got = over("core", send)
        rows = jnp.where(
            core == 0, jnp.concatenate([keep, got], 2), jnp.concatenate([got, keep], 2)
        )
        links = Links()
        kv = gather_high(links, rows[4], rows[5])
        query = gather_high(
            links,
            jnp.concatenate([rows[0], rows[2]], 0),
            jnp.concatenate([rows[1], rows[3]], 0),
        )
        kv = gather_low(links, 48, kv)
        query = gather_low(links, 96, query)
        kv = gather_near(links, *kv)
        kv_pieces = gather_far(links, *kv)
        query = gather_near(links, *query)
        query_pieces = gather_far(links, *query)
        one = gather_high(links, jnp.concatenate([exp_low[:96], rows[6]], 0), exp_low[96:])
        kv_pieces = [v.reshape(v.shape[:3] + (1, 48, 384)) for v in kv_pieces]
        query_pieces = [v.reshape(v.shape[:3] + (2, 48, 384)) for v in query_pieces]
    else:
        weight_local = jnp.concatenate(
            [
                jnp.sum(attention_weight * attention_weight, axis=(1, 2)),
                jnp.sum(expand_weight * expand_weight)[None],
                jnp.sum(reduce_weight * reduce_weight)[None],
            ]
        )
        turned = jnp.swapaxes(attention_weight.astype(bf16), 1, 2)
        turned = lax.all_gather(turned, "wide", axis=1, tiled=True)
        turned = lax.all_gather(turned, "narrow", axis=2, tiled=True)
        exp_all = lax.all_gather(expand_weight.astype(bf16), "wide", axis=1, tiled=True)
        exp_all = lax.all_gather(exp_all, "narrow", axis=0, tiled=True)
        red_all = lax.all_gather(reduce_weight.astype(bf16).T, "wide", axis=0, tiled=True)
        red_all = lax.all_gather(red_all, "narrow", axis=1, tiled=True)
        kv_pieces = query_pieces = [turned]
        one_pieces = [turned, exp_all]
        two_pieces = [red_all]
        one = two = (None, None)

    low, keys, values, low_mine, low_other, kv_all = project_kv(fast, word, ent, kv_pieces)
    if fast:
        one = gather_low(links, 144, later(one, keys))
        two = gather_high(links, *later((red_low[:48], red_low[48:]), keys))
        one = gather_near(links, *one)
        one_pieces = gather_far(links, *one)
    to_words, to_ents, q_all = project_q(fast, low, query_pieces)
    context, exact, lse = attend(counts, to_words, to_ents, keys, values, after=one)
    if fast:
        two = gather_low(links, 48, later(two, to_words))
        two = gather_near(links, *later(two, context))
        two_far = links.send("y", two[0]), links.send("x", two[1])
    (
        middle,
        middle_low,
        activated,
        slope,
        unit_one,
        inverse_one,
        middle_mine,
        middle_other,
        context_mine,
        context_other,
        out_all,
        exp_all,
    ) = feed_in(fast, word, ent, context, norm_params, one_pieces, after=two)
    if fast:
        two_pieces = gather_core(*two, *two_far, token=activated)
    word_out, ent_out, d_second, d_ffn, grads_two, red_all = feed_out(
        fast, activated, middle, norm_params, word_cotangent[0], entity_cotangent[0], two_pieces
    )
    got = red = exp = att_one = att_two = None
    if fast:
        got = over("core", grad_red(False, d_ffn, activated)[0])
    d_inner_one, partial = feed_back_one(0, d_ffn, red_all, exp_all, slope, d_second)
    if fast:
        red = Sum(*grad_red(True, d_ffn, activated, got, after=(partial,)))
    d_inner_two, d_first, d_out, d_context, row_inner, grads_one = feed_back_two(
        2,
        d_ffn,
        red_all,
        exp_all,
        slope,
        partial,
        unit_one,
        inverse_one,
        norm_params,
        out_all,
        exact,
        after=(red.keep,) if fast else (),
    )
    early = jnp.concatenate([grads_one, grads_two], 0)
    early = jnp.concatenate([early, jnp.pad(weight_local, (0, D - 9))[None]], 0)
    early = jnp.pad(early, ((0, 11), (0, 0)))
    early = lax.all_gather(early, ("wide", "narrow"))
    exp_args = (d_inner_one, d_inner_two, d_out)
    att_args = (counts, to_words, to_ents, keys, values, d_context, lse, row_inner)
    if fast:
        sent = grad_exp(False, middle_other, *exp_args, context_other)[0]
        got = over("core", sent)
        red.wait(sent).second()
    grads = attend_back(0, *att_args, after=(red.keep + (sent,)) if fast else ())
    if fast:
        exp = Sum(*grad_exp(True, middle_mine, *exp_args, context_mine, got, after=(grads[0],)))
        red.wait(exp.keep).third()
        sent = grad_att(0, False, low_other, grads, after=(exp.keep, red.keep))[0]
        got = over("core", sent)
    more = attend_back(3, *att_args, after=(sent, red.keep) if fast else ())
    if fast:
        exp.wait(more[0]).second()
        red.wait(more[0]).fourth()
        att_one = Sum(*grad_att(0, True, low_mine, grads, got, after=exp.keep + (more[0], red.keep)))
        sent = grad_att(1, False, low_other, more, after=(att_one.keep,))[0]
        got = over("core", sent)
        exp.wait(sent).third()
        att_two = Sum(*grad_att(1, True, low_mine, more, got, after=(sent,)))
    word_grad, ent_grad = grad_hidden(
        d_first, grads + more, kv_all, q_all, after=(att_two.keep,) if fast else ()
    )
    early = jnp.sum(later((early,), word_grad)[0], axis=0)
    norm_grads = early[:4]
    weight_total = early[4, :9]

    if fast:
        att_one.wait(att_two.keep).second()
        exp.wait(word_grad).fourth()
        att_two.wait(word_grad).second()
        att_one.wait(word_grad).third()
        att_two.third()
        red_sum = red.result()
        exp_sum = exp.result()
        first, second = att_one.low(), att_two.low()
        got = over("high", jnp.where(high == 0, second, first))
        att_sum = jnp.where(high == 0, first, second).astype(f32) + got.astype(f32)
        out_rows = jnp.concatenate([exp_sum[0, 96:], exp_sum[1, 112:]], 0)
        turned = jnp.stack(
            [
                att_sum[0, 48:96],
                att_sum[1, 48:96],
                att_sum[0, 96:],
                att_sum[1, 96:],
                att_sum[0, :48],
                att_sum[1, :48],
                out_rows,
            ]
        )
        att_grad = jnp.swapaxes(unpacked(turned), 1, 2)
        exp_grad = jnp.concatenate([exp_sum[0, :96], exp_sum[1, :96]], 0)
        red_grad = jnp.concatenate([red_sum[0], red_sum[1]], 0)
    else:
        d_to_words, d_to_ents, d_keys, d_values = [
            jnp.concatenate([a, b], 1) for a, b in zip(grads, more)
        ]
        d_inner = jnp.concatenate([d_inner_one, d_inner_two], 1)
        words, ents = low[:WORDS], low[WORDS:]
        turned = jnp.stack(
            [
                dot(d_to_words[:WORDS], words, TN),
                dot(d_to_ents[:WORDS], words, TN),
                dot(d_to_words[WORDS:], ents, TN),
                dot(d_to_ents[WORDS:], ents, TN),
                dot(d_keys, low, TN),
                dot(d_values, low, TN),
                dot(d_out, context, TN),
            ]
        ).astype(bf16)
        turned = lax.psum_scatter(turned, "wide", scatter_dimension=1, tiled=True)
        turned = lax.psum_scatter(turned, "narrow", scatter_dimension=2, tiled=True)
        att_grad = jnp.swapaxes(turned.astype(f32), 1, 2)
        grad = dot(middle_low, d_inner, TN).astype(bf16)
        grad = lax.psum_scatter(grad, "wide", scatter_dimension=1, tiled=True)
        grad = lax.psum_scatter(grad, "narrow", scatter_dimension=0, tiled=True)
        exp_grad = grad.astype(f32)
        grad = dot(d_ffn, activated, TN).astype(bf16)
        grad = lax.psum_scatter(grad, "wide", scatter_dimension=0, tiled=True)
        grad = lax.psum_scatter(grad, "narrow", scatter_dimension=1, tiled=True)
        red_grad = grad.astype(f32)

    att_first, att_second, att_update = adapt(
        attention_weight, att_grad, moment_attention, square_attention, matrix_decay
    )
    exp_first, exp_second, exp_update = adapt(
        expand_weight, exp_grad, moment_expand, square_expand, matrix_decay
    )
    red_first, red_second, red_update = adapt(
        reduce_weight.T, red_grad, moment_reduce.T, square_reduce.T, matrix_decay
    )
    update_local = jnp.concatenate(
        [
            jnp.sum(att_update * att_update, axis=(1, 2)),
            jnp.sum(exp_update * exp_update)[None],
            jnp.sum(red_update * red_update)[None],
        ]
    )
    update_total = sum_all(update_local)
    nrm_first, nrm_second, nrm_update = adapt(
        norm_params, norm_grads, moment_norms, square_norms, 0.0
    )
    weight_norm = jnp.sqrt(
        jnp.concatenate([weight_total, jnp.sum(norm_params * norm_params, axis=1)])
    )
    update_norm = jnp.sqrt(
        jnp.concatenate([update_total, jnp.sum(nrm_update * nrm_update, axis=1)])
    )
    trust = weight_norm / update_norm
    new_attention = attention_weight - learn_rate * trust[0:7, None, None] * att_update
    new_expand = expand_weight - learn_rate * trust[7] * exp_update
    new_reduce = reduce_weight - learn_rate * trust[8] * red_update.T
    new_norms = norm_params - learn_rate * trust[9:13, None] * nrm_update
    trust_stats = jnp.stack([jnp.log(weight_norm), jnp.log(update_norm), jnp.log(trust)], 1)
    return (
        word_out[None],
        ent_out[None],
        word_grad[None],
        ent_grad[None],
        new_attention,
        new_expand,
        new_reduce,
        new_norms,
        att_first,
        exp_first,
        red_first.T,
        nrm_first,
        att_second,
        exp_second,
        red_second.T,
        nrm_second,
        trust_stats,
    )


def solution(mesh):
    fast = mesh.shape["wide"] == 8 and mesh.shape["narrow"] == 4
    rows = P(("wide", "narrow"), None, None)
    matrix = P("narrow", "wide")
    stack = P(None, "narrow", "wide")
    weights = (stack, matrix, matrix, P())
    return jax.shard_map(
        functools.partial(shards, fast),
        mesh=mesh,
        in_specs=(rows, rows, P(("wide", "narrow"), None)) + weights * 3 + (rows, rows),
        out_specs=(rows,) * 4 + weights * 3 + (P(),),
        check_vma=False,
    )
```

time: 450 us -> 410 us (0.911)
  waiting for transfers between devices: 164 us -> 108 us
  blocking collectives: 50.8 us -> 0 us
  Pallas kernels: 132 us -> 160 us
  starting transfers between devices: 46.8 us -> 68.1 us
  between operations: 3.34 us -> 17 us
    ppermute x63 -> x68, waiting for transfers between devices: 159 us -> 93.5 us  [flip(): return lax.ppermute(value, axis, [(i, i ^ bit) for i in range(size)])]
    all_gather x1 -> x0, blocking collectives: 50.8 us -> none  [shards(): lax.all_gather(early, ('wide', 'narrow'), axis=0, tiled=False)]
    pallas_call x10 -> x18, Pallas kernels: 129 us -> 157 us  [the longest x8 47.6 us: grad_call(): pl.pallas_call(functools.partial(kernel, mine, len(after), len(outs)), in...]
    ppermute x63 -> x68, starting transfers between devices: 44.3 us -> 65.5 us  [flip(): return lax.ppermute(value, axis, [(i, i ^ bit) for i in range(size)])]
    all_gather x0 -> x1, waiting for transfers between devices: none -> 10.1 us  [shards(): early = lax.all_gather(early, ('wide', 'narrow'))]
    convert_element_type x12 -> x6, other arithmetic: 11.9 us -> 7.7 us  [plus(): return (kept.astype(f32) + got.astype(f32)).astype(bf16)]
    another operation x39 -> x35, other arithmetic: 7.44 us -> 9.36 us  [the longest x7 4.1 us: third(): keep = jnp.stack([plus(self.keep[0], left), plus(self.keep[1], right)], 1)]
    unnamed x89 -> x103, local copies, waits for them, and re-layouts: 10.5 us -> 10.4 us
  transfers between devices with their start and end apart: 64 -> 70, of which waited for: 30 -> 27; matrix products, arithmetic and copies ran while one was open for 8% -> 8% of each run, Pallas kernels for 21% -> 30%
where the time goes in v2:
time: 410 us; the launch traced here: 402 us
  Pallas kernels  160 us (39%)
  waiting for transfers between devices  108 us (26%)
  starting transfers between devices  68.1 us (17%)
  other arithmetic  34.6 us (8%)
  between operations  17 us (4%)
  local copies, waits for them, and re-layouts  14.4 us (4%)
    ppermute x68, waiting for transfers between devices, flip(): return lax.ppermute(value, axis, [(i, i ^ bit) for i in range(size)])  93.5 us
    ppermute x68, starting transfers between devices, flip(): return lax.ppermute(value, axis, [(i, i ^ bit) for i in range(size)])  65.5 us
    pallas_call x8, Pallas kernels, grad_call(): pl.pallas_call(functools.partial(kernel, mine, len(after), len(outs)), in...  47.6 us
    pallas_call x2, Pallas kernels, attend_back(): pl.pallas_call(functools.partial(attend_back_kernel, len(after)), grid=(H...  19.7 us
    pallas_call x1, Pallas kernels, feed_in(): pl.pallas_call(functools.partial(feed_in_kernel, fast, len(after)), grid=...  16.1 us
    pallas_call x1, Pallas kernels, feed_back_two(): pl.pallas_call(functools.partial(feed_back_two_kernel, len(after)), grid=...  14.9 us
    pallas_call x1, Pallas kernels, feed_out(): pl.pallas_call(functools.partial(feed_out_kernel, fast, len(after)), grid...  13.3 us
    pallas_call x1, Pallas kernels, attend(): pl.pallas_call(functools.partial(attend_kernel, len(after)), grid=(HEADS...  12.5 us
  transfers between devices with their start and end apart: 70, of which 27 were waited for; matrix products, arithmetic and copies ran while one was open for 8% of the time, Pallas kernels for 30%

profile of v2, /device:TPU:0, one launch (start us, length us, event | category | flops | bytes accessed | tf_op | source)
XLA Modules:
  0.0 402.2 jit_solution(17565276125334005731)
XLA Ops:
  17.6 4.4 %collective-permute-done.1 = bf16[96,384]{1,0:T(8,128)(2,1)S(1)} collective-permute-done((bf16[96,384]{1,0:T(8,128)(2,1)S(1)}, bf16[96,384]{1,0:T(8,128)(2,1)S(1)}, u32[]{:S(2)}, u32[]{:S(2)}) %collective-permute-start.1) | collective-permute-done | bytes 73760 | tf_op jit(solution)/shard_map/ppermute | solution.py:882
  45.4 4.0 %collective-permute-done.4 = bf16[2,2,2,48,384]{4,3,2,1,0:T(8,128)(2,1)S(1)} collective-permute-done((bf16[2,2,2,48,384]{4,3,2,1,0:T(8,128)(2,1)S(1)}, bf16[2,2,2,48,384]{4,3,2,1,0:T(8,128)(2,1)S(1)}, u32[]{:S(2)}, u32[]{:S(2)}) %collective-permute-start.4) | collective-permute-done | bytes 294944 | tf_op jit(solution)/shard_map/ppermute | solution.py:882
  57.8 6.7 %project_kv.1 = (bf16[640,768]{1,0:T(8,128)(2,1)}, bf16[640,768]{1,0:T(8,128)(2,1)}, bf16[640,768]{1,0:T(8,128)(2,1)}, bf16[640,384]{1,0:T(8,128)(2,1)}, bf16[64...) custom-call(f32[512,768]{1,0:T(8,128)} %bitcast.377, f32[128,768]{1,0:T(8,128)} %bitcast.386, ...), custom_call_target="tpu_custom_call" | custom-call | flops 2400000000 | tf_op jit(solution)/shard_map/project_kv/pallas_call | solution.py:188
  69.7 6.2 %collective-permute-done.22 = bf16[2,240,384]{2,1,0:T(8,128)(2,1)S(1)} collective-permute-done((bf16[2,240,384]{2,1,0:T(8,128)(2,1)S(1)}, bf16[2,240,384]{2,1,0:T(8,128)(2,1)S(1)}, u32[]{:S(2)}, u32[]{:S(2)}) %collective-permute-start.22) | collective-permute-done | bytes 368672 | tf_op jit(solution)/shard_map/ppermute | solution.py:882
  78.3 5.0 %collective-permute-done.14 = bf16[2,2,2,96,384]{4,3,2,1,0:T(8,128)(2,1)S(1)} collective-permute-done((bf16[2,2,2,96,384]{4,3,2,1,0:T(8,128)(2,1)S(1)}, bf16[2,2,2,96,384]{4,3,2,1,0:T(8,128)(2,1)S(1)}, u32[]{:S(2)}, u32[]{:S(2)}) %collective-permute-start.14) | collective-permute-done | bytes 589856 | tf_op jit(solution)/shard_map/ppermute | solution.py:882
  83.4 5.9 %collective-permute-done.24 = bf16[2,2,96,384]{3,2,1,0:T(8,128)(2,1)S(1)} collective-permute-done((bf16[2,2,96,384]{3,2,1,0:T(8,128)(2,1)S(1)}, bf16[2,2,96,384]{3,2,1,0:T(8,128)(2,1)S(1)}, u32[]{:S(2)}, u32[]{:S(2)}) %collective-permute-start.24) | collective-permute-done | bytes 294944 | tf_op jit(solution)/shard_map/ppermute | solution.py:882
  95.3 7.2 %project_q.1 = (bf16[640,768]{1,0:T(8,128)(2,1)}, bf16[640,768]{1,0:T(8,128)(2,1)}, bf16[4,768,768]{2,1,0:T(8,128)(2,1)}) custom-call(bf16[640,768]{1,0:T(8,128)(2,1)} %get-tuple-element.129.low, bf16[2,2,2,2,48,384]{5,4,3,2,1,0:T(8,128)(2,1)} %pad_maximum_fusion.1.refs_0_, bf16[2,2,2,2,48,384]{5,4,3,2,1,0:T(8,128)(2,1)} %bitcast.383, ...), custom_call_target="tpu_custom_call" | custom-call | flops 2800000000 | tf_op jit(solution)/shard_map/project_q/pallas_call | solution.py:233
  103.1 12.5 %attend.1 = (bf16[640,768]{1,0:T(8,128)(2,1)}, f32[640,768]{1,0:T(8,128)}, f32[6,2,640]{2,1,0:T(2,128)}) custom-call(s32[2]{0:T(128)} %bitcast.395, bf16[640,768]{1,0:T(8,128)(2,1)} %get-tuple-element.135.to_words, bf16[640,768]{1,0:T(8,128)(2,1)} %get-tuple-element.136.to_ents, bf16[640,768]{1,0:T(8,128)(2,1)} %get-tuple-element.137.keys, ...), custom_call_target="tpu_custom_call" | custom-call | flops 4800000000 | tf_op jit(solution)/shard_map/attend/pallas_call | solution.py:293
  117.6 7.7 %collective-permute-done.34 = bf16[2,2,48,768]{3,2,1,0:T(8,128)(2,1)S(1)} collective-permute-done((bf16[2,2,48,768]{3,2,1,0:T(8,128)(2,1)S(1)}, bf16[2,2,48,768]{3,2,1,0:T(8,128)(2,1)S(1)}, u32[]{:S(2)}, u32[]{:S(2)}) %collective-permute-start.34) | collective-permute-done | bytes 294944 | tf_op jit(solution)/shard_map/ppermute | solution.py:882
  126.5 7.5 %collective-permute-done.33 = bf16[2,2,48,768]{3,2,1,0:T(8,128)(2,1)S(1)} collective-permute-done((bf16[2,2,48,768]{3,2,1,0:T(8,128)(2,1)S(1)}, bf16[2,2,48,768]{3,2,1,0:T(8,128)(2,1)S(1)}, u32[]{:S(2)}, u32[]{:S(2)}) %collective-permute-start.33) | collective-permute-done | bytes 294944 | tf_op jit(solution)/shard_map/ppermute | solution.py:882
  137.5 16.1 %feed_in.1 = (f32[640,768]{1,0:T(8,128)}, bf16[640,768]{1,0:T(8,128)(2,1)}, bf16[640,3072]{1,0:T(8,128)(2,1)}, bf16[640,3072]{1,0:T(8,128)(2,1)}, f32[640,768]{1...) custom-call(f32[512,768]{1,0:T(8,128)} %bitcast.378, ...), custom_call_target="tpu_custom_call" | custom-call | flops 60000002048 | tf_op jit(solution)/shard_map/feed_in/pallas_call | solution.py:412
  157.3 13.3 %feed_out.1 = (f32[512,768]{1,0:T(8,128)}, f32[128,768]{1,0:T(8,128)}, f32[640,768]{1,0:T(8,128)}, bf16[640,768]{1,0:T(8,128)(2,1)}, f32[2,768]{1,0:T(2,128)}, /*index=5*/bf16[4,768,768]{2,1,0:T(8,128)(2,1)}) custom-call(bf16[640,3072]{1,0:T(8,128)(2,1)} %get-tuple-element.160.activated, f32[640,768]{1,0:T(8,128)} %get-tuple-element.161.middle, ...), custom_call_target="tpu_custom_call" | custom-call | flops 51999997952 | tf_op jit(solution)/shard_map/feed_out/pallas_call | solution.py:506
  170.6 6.0 %grad_red.2 = bf16[2,2,2,2,2,48,768]{6,5,4,3,2,1,0:T(8,128)(2,1)} custom-call(bf16[640,768]{1,0:T(8,128)(2,1)} %get-tuple-element.168.d_ffn, bf16[640,3072]{1,0:T(8,128)(2,1)} %get-tuple-element.160.activated), custom_call_target="tpu_custom_call" | custom-call | flops 28000000000 | tf_op jit(solution)/shard_map/grad_red/pallas_call | solution.py:699
  176.8 9.5 %feed_back_one.1 = (bf16[640,1536]{1,0:T(8,128)(2,1)}, f32[640,768]{1,0:T(8,128)}) custom-call(bf16[640,768]{1,0:T(8,128)(2,1)} %get-tuple-element.168.d_ffn, bf16[4,768,768]{2,1,0:T(8,128)(2,1)} %get-tuple-element.169.red_all, bf16[4,768,768]{2,1,0:T(8,128)(2,1)} %get-tuple-element.170.exp_all, bf16[640,3072]{1,0:T(8,128)(2,1)} %get-tuple-element.171.slope, ...), custom_call_target="tpu_custom_call" | custom-call | flops 40000000000 | tf_op jit(solution)/shard_map/feed_back_one/pallas_call | solution.py:549
  187.6 6.9 %grad_red.3 = (bf16[2,2,2,48,768]{4,3,2,1,0:T(8,128)(2,1)}, bf16[2,2,2,48,768]{4,3,2,1,0:T(8,128)(2,1)}, bf16[2,2,2,2,48,768]{5,4,3,2,1,0:T(8,128)(2,1)}) custom-call(bf16[640,768]{1,0:T(8,128)(2,1)} %get-tuple-element.168.d_ffn, bf16[640,3072]{1,0:T(8,128)(2,1)} %get-tuple-element.160.activated, bf16[2,2,2,2,2,48,768]{6,5,4,3,2,1,0:T(8,128)(2,1)} %copy-done.28, ...), custom_call_target="tpu_custom_call" | custom-call | flops 28000000000 | tf_op jit(solution)/shard_map/grad_red/pallas_call | solution.py:699
  196.5 14.9 %feed_back_two.1 = (bf16[640,1536]{1,0:T(8,128)(2,1)}, f32[640,768]{1,0:T(8,128)}, bf16[640,768]{1,0:T(8,128)(2,1)}, bf16[640,768]{1,0:T(8,128)(2,1)}, f32[6,2,640]{2,1,0:T(2,128)}, /*index=5*/f32[2,768]{1,0:T(2,128)}) custom-call(bf16[640,768]{1,0:T(8,128)(2,1)} %get-tuple-element.168.d_ffn, bf16[4,768,768]{2,1,0:T(8,128)(2,1)} %get-tuple-element.169.red_all, ...), custom_call_target="tpu_custom_call" | custom-call | flops 60000002048 | tf_op jit(solution)/shard_map/feed_back_two/pallas_call | solution.py:603
  211.4 7.3 %grad_exp.2.refs_2_ = bf16[2,2,2,2,2,128,384]{6,5,4,3,2,1,0:T(8,128)(2,1)} custom-call(bf16[640,384]{1,0:T(8,128)(2,1)} %get-tuple-element.185.middle, bf16[640,1536]{1,0:T(8,128)(2,1)} %get-tuple-element.186.d_inner_one, bf16[640,1536]{1,0:T(8,128)(2,1)} %get-tuple-element.187.d_inner_two, bf16[640,768]{1,0:T(8,128)(2,1)} %get-tuple-element.188.d_out, ...), custom_call_target="tpu_custom_call" | custom-call | flops 28000000000 | tf_op jit(solution)/shard_map/grad_exp/pallas_call | solution.py:699
  221.9 9.8 %attend_back.2 = (bf16[640,384]{1,0:T(8,128)(2,1)}, bf16[640,384]{1,0:T(8,128)(2,1)}, bf16[640,384]{1,0:T(8,128)(2,1)}, bf16[640,384]{1,0:T(8,128)(2,1)}) custom-call(s32[2]{0:T(128)} %bitcast.396, bf16[640,768]{1,0:T(8,128)(2,1)} %get-tuple-element.135.to_words, bf16[640,768]{1,0:T(8,128)(2,1)} %get-tuple-element.136.to_ents, ...), custom_call_target="tpu_custom_call" | custom-call | flops 40000000000 | tf_op jit(solution)/shard_map/attend_back/pallas_call | solution.py:659
  231.7 8.3 %grad_exp.3 = (bf16[2,2,2,128,384]{4,3,2,1,0:T(8,128)(2,1)}, bf16[2,2,2,128,384]{4,3,2,1,0:T(8,128)(2,1)}, bf16[2,2,2,2,128,384]{5,4,3,2,1,0:T(8,128)(2,1)}) custom-call(bf16[640,384]{1,0:T(8,128)(2,1)} %get-tuple-element.197.middle, bf16[640,1536]{1,0:T(8,128)(2,1)} %get-tuple-element.186.d_inner_one, bf16[640,1536]{1,0:T(8,128)(2,1)} %get-tuple-element.187.d_inner_two, ...), custom_call_target="tpu_custom_call" | custom-call | flops 28000000000 | tf_op jit(solution)/shard_map/grad_exp/pallas_call | solution.py:699
  244.5 4.5 %grad_att.4.refs_0_ = bf16[2,2,2,2,144,384]{5,4,3,2,1,0:T(8,128)(2,1)} custom-call(bf16[640,384]{1,0:T(8,128)(2,1)} %get-tuple-element.196.picked, bf16[640,384]{1,0:T(8,128)(2,1)} %get-tuple-element.192.refs_1_.d_to_words.refs_0_, bf16[640,384]{1,0:T(8,128)(2,1)} %get-tuple-element.193.d_to_ents.refs_1_, ...), custom_call_target="tpu_custom_call" | custom-call | flops 28000000000 | tf_op jit(solution)/shard_map/grad_att/pallas_call | solution.py:699
  249.0 9.9 %attend_back.3 = (bf16[640,384]{1,0:T(8,128)(2,1)}, bf16[640,384]{1,0:T(8,128)(2,1)}, bf16[640,384]{1,0:T(8,128)(2,1)}, bf16[640,384]{1,0:T(8,128)(2,1)}) custom-call(s32[2]{0:T(128)} %bitcast.397, bf16[640,768]{1,0:T(8,128)(2,1)} %get-tuple-element.135.to_words, bf16[640,768]{1,0:T(8,128)(2,1)} %get-tuple-element.136.to_ents, ...), custom_call_target="tpu_custom_call" | custom-call | flops 40000000000 | tf_op jit(solution)/shard_map/attend_back/pallas_call | solution.py:659
  264.6 5.0 %grad_att.5 = (bf16[2,2,144,384]{3,2,1,0:T(8,128)(2,1)}, bf16[2,2,144,384]{3,2,1,0:T(8,128)(2,1)}, bf16[2,2,2,144,384]{4,3,2,1,0:T(8,128)(2,1)}) custom-call(bf16[640,384]{1,0:T(8,128)(2,1)} %get-tuple-element.208.picked, bf16[640,384]{1,0:T(8,128)(2,1)} %get-tuple-element.192.refs_1_.d_to_words.refs_0_, ...), custom_call_target="tpu_custom_call" | custom-call | flops 28000000000 | tf_op jit(solution)/shard_map/grad_att/pallas_call | solution.py:699
  269.6 4.5 %grad_att.6.refs_1_ = bf16[2,2,2,2,144,384]{5,4,3,2,1,0:T(8,128)(2,1)} custom-call(bf16[640,384]{1,0:T(8,128)(2,1)} %get-tuple-element.196.picked, bf16[640,384]{1,0:T(8,128)(2,1)} %get-tuple-element.202.refs_3_.d_to_words.refs_4_, bf16[640,384]{1,0:T(8,128)(2,1)} %get-tuple-element.203.d_to_ents.refs_5_, ...), custom_call_target="tpu_custom_call" | custom-call | flops 28000000000 | tf_op jit(solution)/shard_map/grad_att/pallas_call | solution.py:699
  280.1 5.2 %collective-permute-done.67 = bf16[2,48,768]{2,1,0:T(8,128)(2,1)} collective-permute-done((bf16[2,48,768]{2,1,0:T(8,128)(2,1)}, bf16[2,48,768]{2,1,0:T(8,128)(2,1)}, u32[]{:S(2)}, u32[]{:S(2)}) %collective-permute-start.67) | collective-permute-done | bytes 147488 | tf_op jit(solution)/shard_map/ppermute | solution.py:882
  293.1 5.4 %collective-permute-done.63 = bf16[2,2,128,384]{3,2,1,0:T(8,128)(2,1)S(1)} collective-permute-done((bf16[2,2,128,384]{3,2,1,0:T(8,128)(2,1)}, bf16[2,2,128,384]{3,2,1,0:T(8,128)(2,1)S(1)}, u32[]{:S(2)}, u32[]{:S(2)}) %collective-permute-start.63) | collective-permute-done | bytes 393248 | tf_op jit(solution)/shard_map/ppermute | solution.py:882
  300.5 5.1 %grad_att.7 = (bf16[2,2,144,384]{3,2,1,0:T(8,128)(2,1)}, bf16[2,2,144,384]{3,2,1,0:T(8,128)(2,1)}, bf16[2,2,2,144,384]{4,3,2,1,0:T(8,128)(2,1)}) custom-call(bf16[640,384]{1,0:T(8,128)(2,1)} %get-tuple-element.208.picked, bf16[640,384]{1,0:T(8,128)(2,1)} %get-tuple-element.202.refs_3_.d_to_words.refs_4_, ...), custom_call_target="tpu_custom_call" | custom-call | flops 28000000000 | tf_op jit(solution)/shard_map/grad_att/pallas_call | solution.py:699
  314.2 9.1 %grad_hidden.1 = (f32[512,768]{1,0:T(8,128)}, f32[128,768]{1,0:T(8,128)}) custom-call(f32[640,768]{1,0:T(8,128)} %get-tuple-element.179.d_first, bf16[640,384]{1,0:T(8,128)(2,1)} %get-tuple-element.192.refs_1_.d_to_words.refs_0_, bf16[640,384]{1,0:T(8,128)(2,1)} %get-tuple-element.193.d_to_ents.refs_1_, bf16[640,384]{1,0:T(8,128)(2,1)} %get-tuple-element.194.d_keys.refs_2_, ...), custom_call_target="tpu_custom_call" | custom-call | flops 35999997952 | tf_op jit(solution)/shard_map/grad_hidden/pallas_call | solution.py:869
  325.0 10.1 %all-gather.3.cloned.1.call-done = f32[512,768]{1,0:T(8,128)} async-done(((f32[16,768]{1,0:T(8,128)}), f32[512,768]{1,0:T(8,128)}) %all-gather.3.cloned.1.call-update) | async-done | bytes 1572880 | tf_op jit(solution)/shard_map/all_gather | solution.py:1136
  339.9 6.2 %collective-permute-done.59 = bf16[2,144,384]{2,1,0:T(8,128)(2,1)S(1)} collective-permute-done((bf16[2,144,384]{2,1,0:T(8,128)(2,1)S(1)}, bf16[2,144,384]{2,1,0:T(8,128)(2,1)S(1)}, u32[]{:S(2)}, u32[]{:S(2)}) %collective-permute-start.59) | collective-permute-done | bytes 221216 | tf_op jit(solution)/shard_map/ppermute | solution.py:882
  357.7 4.8 %collective-permute-done.61 = bf16[2,144,384]{2,1,0:T(8,128)(2,1)S(1)} collective-permute-done((bf16[2,144,384]{2,1,0:T(8,128)(2,1)S(1)}, bf16[2,144,384]{2,1,0:T(8,128)(2,1)S(1)}, u32[]{:S(2)}, u32[]{:S(2)}) %collective-permute-start.61) | collective-permute-done | bytes 221216 | tf_op jit(solution)/shard_map/ppermute | solution.py:882
  365.6 8.6 %collective-permute-done.62 = bf16[2,144,384]{2,1,0:T(8,128)(2,1)S(1)} collective-permute-done((bf16[2,144,384]{2,1,0:T(8,128)(2,1)S(1)}, bf16[2,144,384]{2,1,0:T(8,128)(2,1)S(1)}, u32[]{:S(2)}, u32[]{:S(2)}) %collective-permute-start.62) | collective-permute-done | bytes 221216 | tf_op jit(solution)/shard_map/ppermute | solution.py:882
  382.5 4.8 %all-to-all-done = f32[32,1,9]{2,1,0:T(1,128)S(1)} async-done(((f32[32,1,9]{2,1,0:T(1,128)}), f32[32,1,9]{2,1,0:T(1,128)S(1)}, u32[]{:S(2)}, u32[]{:S(2)}) %all-to-all-start) | async-done | bytes 1184 | tf_op jit(solution)/shard_map/all_to_all | solution.py:1002
  (325 shorter events, 142.9 us)
Async XLA Ops:
  7.2 327.8 %all-gather.3.cloned.1.call-start = ((), (), s32[]{:S(2)}) async-start(), calls=%async_computation.1 | async-start | bytes 1622016 | tf_op jit(solution)/shard_map/all_gather | solution.py:1136
  28.1 13.7 %collective-permute-start.12 = (bf16[2,192,384]{2,1,0:T(8,128)(2,1)S(1)}, bf16[2,192,384]{2,1,0:T(8,128)(2,1)S(1)}, u32[]{:S(2)}, u32[]{:S(2)}) collective-permute-start(bf16[2,192,384]{2,1,0:T(8,128)(2,1)S(1)} %pad_maximum_fusion.12), channel_id=1, source_target_pairs={{0,8},{4,12},{8,0},{12,4},{16,24},{20,28},{24,16},{28,20},{1,9},{5... | collective-permute-start | bytes 884744 | tf_op jit(solution)/shard_map/ppermute | solution.py:882
  55.8 35.4 %collective-permute-start.19 = (bf16[2,2,2,96,384]{4,3,2,1,0:T(8,128)(2,1)S(1)}, bf16[2,2,2,96,384]{4,3,2,1,0:T(8,128)(2,1)S(1)}, u32[]{:S(2)}, u32[]{:S(2)}) collective-permute-start(bf16[2,2,2,96,384]{4,3,2,1,0:T(8,128)(2,1)S(1)} %pad_maximum_fusion.4), channel_id=1, source_target_pairs={{0,1},{1,0},{2,3},{3,2},{4,5},{5,4},{6,7},{7,6},{8,9},{9,8},{10,11... | collective-permute-start | bytes 1769480 | tf_op jit(solution)/shard_map/ppermute | solution.py:882
  55.9 21.8 %collective-permute-start.18 = (bf16[2,2,2,96,384]{4,3,2,1,0:T(8,128)(2,1)S(1)}, bf16[2,2,2,96,384]{4,3,2,1,0:T(8,128)(2,1)S(1)}, u32[]{:S(2)}, u32[]{:S(2)}) collective-permute-start(bf16[2,2,2,96,384]{4,3,2,1,0:T(8,128)(2,1)S(1)} %pad_maximum_fusion.4), channel_id=1, source_target_pairs={{0,2},{1,3},{2,0},{3,1},{4,6},{5,7},{6,4},{7,5},{8,10},{9,11},{10,... | collective-permute-start | bytes 1769480 | tf_op jit(solution)/shard_map/ppermute | solution.py:882
  67.1 25.1 %collective-permute-start.15 = (bf16[2,2,2,96,384]{4,3,2,1,0:T(8,128)(2,1)S(1)}, bf16[2,2,2,96,384]{4,3,2,1,0:T(8,128)(2,1)S(1)}, u32[]{:S(2)}, u32[]{:S(2)}) collective-permute-start(bf16[2,2,2,96,384]{4,3,2,1,0:T(8,128)(2,1)S(1)} %pad_maximum_fusion.2), channel_id=1, source_target_pairs={{0,1},{1,0},{2,3},{3,2},{4,5},{5,4},{6,7},{7,6},{8,9},{9,8},{10,11... | collective-permute-start | bytes 1769480 | tf_op jit(solution)/shard_map/ppermute | solution.py:882
  67.2 16.2 %collective-permute-start.14 = (bf16[2,2,2,96,384]{4,3,2,1,0:T(8,128)(2,1)S(1)}, bf16[2,2,2,96,384]{4,3,2,1,0:T(8,128)(2,1)S(1)}, u32[]{:S(2)}, u32[]{:S(2)}) collective-permute-start(bf16[2,2,2,96,384]{4,3,2,1,0:T(8,128)(2,1)S(1)} %pad_maximum_fusion.2), channel_id=1, source_target_pairs={{0,4},{4,0},{8,12},{12,8},{16,20},{20,16},{24,28},{28,24},{1,5},{5... | collective-permute-start | bytes 1769480 | tf_op jit(solution)/shard_map/ppermute | solution.py:882
  91.2 26.1 %collective-permute-start.28 = (bf16[2,2,2,96,384]{4,3,2,1,0:T(8,128)(2,1)}, bf16[2,2,2,96,384]{4,3,2,1,0:T(8,128)(2,1)}, u32[]{:S(2)}, u32[]{:S(2)}) collective-permute-start(bf16[2,2,2,96,384]{4,3,2,1,0:T(8,128)(2,1)} %pad_maximum_fusion.5.refs_1_.refs_4_), channel_id=1, source_target_pairs={{0,2},{1,3},{2,0},{3,1},{4,6},{5,7},{6,4},{7,5},{8,10},{9,11},{10,... | collective-permute-start | bytes 1769480 | tf_op jit(solution)/shard_map/ppermute | solution.py:882
  92.1 42.5 %collective-permute-start.26 = (bf16[2,2,2,144,384]{4,3,2,1,0:T(8,128)(2,1)S(1)}, bf16[2,2,2,144,384]{4,3,2,1,0:T(8,128)(2,1)S(1)}, u32[]{:S(2)}, u32[]{:S(2)}) collective-permute-start(bf16[2,2,2,144,384]{4,3,2,1,0:T(8,128)(2,1)S(1)} %pad_maximum_fusion.refs_0_), channel_id=1, source_target_pairs={{0,1},{1,0},{2,3},{3,2},{4,5},{5,4},{6,7},{7,6},{8,9},{9,8},{10,11... | collective-permute-start | bytes 2654216 | tf_op jit(solution)/shard_map/ppermute | solution.py:882
  93.0 22.7 %collective-permute-start.25 = (bf16[2,2,2,144,384]{4,3,2,1,0:T(8,128)(2,1)S(1)}, bf16[2,2,2,144,384]{4,3,2,1,0:T(8,128)(2,1)S(1)}, u32[]{:S(2)}, u32[]{:S(2)}) collective-permute-start(bf16[2,2,2,144,384]{4,3,2,1,0:T(8,128)(2,1)S(1)} %pad_maximum_fusion.refs_0_), channel_id=1, source_target_pairs={{0,4},{4,0},{8,12},{12,8},{16,20},{20,16},{24,28},{28,24},{1,5},{5... | collective-permute-start | bytes 2654216 | tf_op jit(solution)/shard_map/ppermute | solution.py:882
  115.6 21.8 %collective-permute-start.27 = (bf16[2,2,2,144,384]{4,3,2,1,0:T(8,128)(2,1)S(1)}, bf16[2,2,2,144,384]{4,3,2,1,0:T(8,128)(2,1)}, u32[]{:S(2)}, u32[]{:S(2)}) collective-permute-start(bf16[2,2,2,144,384]{4,3,2,1,0:T(8,128)(2,1)S(1)} %collective-permute-done.25.refs_1_), channel_id=1, source_target_pairs={{0,1},{1,0},{2,3},{3,2},{4,5},{5,4},{6,7},{7,6},{8,9},{9,8},{10,11... | collective-permute-start | bytes 2654216 | tf_op jit(solution)/shard_map/ppermute | solution.py:882
  117.1 16.9 %collective-permute-start.29 = (bf16[2,2,2,96,384]{4,3,2,1,0:T(8,128)(2,1)}, bf16[2,2,2,96,384]{4,3,2,1,0:T(8,128)(2,1)S(1)}, u32[]{:S(2)}, u32[]{:S(2)}) collective-permute-start(bf16[2,2,2,96,384]{4,3,2,1,0:T(8,128)(2,1)} %pad_maximum_fusion.5.refs_1_.refs_4_), channel_id=1, source_target_pairs={{0,1},{1,0},{2,3},{3,2},{4,5},{5,4},{6,7},{7,6},{8,9},{9,8},{10,11... | collective-permute-start | bytes 1769480 | tf_op jit(solution)/shard_map/ppermute | solution.py:882
  117.3 18.4 %collective-permute-start.30 = (bf16[2,2,2,96,384]{4,3,2,1,0:T(8,128)(2,1)}, bf16[2,2,2,96,384]{4,3,2,1,0:T(8,128)(2,1)S(1)}, u32[]{:S(2)}, u32[]{:S(2)}) collective-permute-start(bf16[2,2,2,96,384]{4,3,2,1,0:T(8,128)(2,1)} %collective-permute-done.28.refs_5_), channel_id=1, source_target_pairs={{0,1},{1,0},{2,3},{3,2},{4,5},{5,4},{6,7},{7,6},{8,9},{9,8},{10,11... | collective-permute-start | bytes 1769480 | tf_op jit(solution)/shard_map/ppermute | solution.py:882
  133.9 20.2 %collective-permute-start.39 = (bf16[2,2,2,48,768]{4,3,2,1,0:T(8,128)(2,1)S(1)}, bf16[2,2,2,48,768]{4,3,2,1,0:T(8,128)(2,1)}, u32[]{:S(2)}, u32[]{:S(2)}) collective-permute-start(bf16[2,2,2,48,768]{4,3,2,1,0:T(8,128)(2,1)S(1)} %pad_maximum_fusion.7.refs_9_.refs_4_), channel_id=1, source_target_pairs={{0,1},{1,0},{2,3},{3,2},{4,5},{5,4},{6,7},{7,6},{8,9},{9,8},{10,11... | collective-permute-start | bytes 1769480 | tf_op jit(solution)/shard_map/ppermute | solution.py:882
  134.0 20.1 %collective-permute-start.37 = (bf16[2,2,2,48,768]{4,3,2,1,0:T(8,128)(2,1)S(1)}, bf16[2,2,2,48,768]{4,3,2,1,0:T(8,128)(2,1)}, u32[]{:S(2)}, u32[]{:S(2)}) collective-permute-start(bf16[2,2,2,48,768]{4,3,2,1,0:T(8,128)(2,1)S(1)} %pad_maximum_fusion.6.refs_8_.refs_0_), channel_id=1, source_target_pairs={{0,1},{1,0},{2,3},{3,2},{4,5},{5,4},{6,7},{7,6},{8,9},{9,8},{10,11... | collective-permute-start | bytes 1769480 | tf_op jit(solution)/shard_map/ppermute | solution.py:882
  134.6 18.9 %collective-permute-start.36 = (bf16[2,2,2,48,768]{4,3,2,1,0:T(8,128)(2,1)S(1)}, bf16[2,2,2,48,768]{4,3,2,1,0:T(8,128)(2,1)S(1)}, u32[]{:S(2)}, u32[]{:S(2)}) collective-permute-start(bf16[2,2,2,48,768]{4,3,2,1,0:T(8,128)(2,1)S(1)} %pad_maximum_fusion.7.refs_9_.refs_4_), channel_id=1, source_target_pairs={{0,2},{1,3},{2,0},{3,1},{4,6},{5,7},{6,4},{7,5},{8,10},{9,11},{10,... | collective-permute-start | bytes 1769480 | tf_op jit(solution)/shard_map/ppermute | solution.py:882
  136.5 17.1 %collective-permute-start.35 = (bf16[2,2,2,48,768]{4,3,2,1,0:T(8,128)(2,1)S(1)}, bf16[2,2,2,48,768]{4,3,2,1,0:T(8,128)(2,1)}, u32[]{:S(2)}, u32[]{:S(2)}) collective-permute-start(bf16[2,2,2,48,768]{4,3,2,1,0:T(8,128)(2,1)S(1)} %pad_maximum_fusion.6.refs_8_.refs_0_), channel_id=1, source_target_pairs={{0,4},{4,0},{8,12},{12,8},{16,20},{20,16},{24,28},{28,24},{1,5},{5... | collective-permute-start | bytes 1769480 | tf_op jit(solution)/shard_map/ppermute | solution.py:882
  194.5 24.2 %collective-permute-start.42 = (bf16[2,2,2,48,768]{4,3,2,1,0:T(8,128)(2,1)}, bf16[2,2,2,48,768]{4,3,2,1,0:T(8,128)(2,1)S(1)}, u32[]{:S(2)}, u32[]{:S(2)}) collective-permute-start(bf16[2,2,2,48,768]{4,3,2,1,0:T(8,128)(2,1)} %get-tuple-element.183), channel_id=1, source_target_pairs={{0,2},{1,3},{2,0},{3,1},{4,6},{5,7},{6,4},{7,5},{8,10},{9,11},{10,... | collective-permute-start | bytes 1769480 | tf_op jit(solution)/shard_map/ppermute | solution.py:882
  195.7 23.0 %collective-permute-start.43 = (bf16[2,2,2,48,768]{4,3,2,1,0:T(8,128)(2,1)}, bf16[2,2,2,48,768]{4,3,2,1,0:T(8,128)(2,1)S(1)}, u32[]{:S(2)}, u32[]{:S(2)}) collective-permute-start(bf16[2,2,2,48,768]{4,3,2,1,0:T(8,128)(2,1)} %get-tuple-element.184), channel_id=1, source_target_pairs={{0,4},{4,0},{8,12},{12,8},{16,20},{20,16},{24,28},{28,24},{1,5},{5... | collective-permute-start | bytes 1769480 | tf_op jit(solution)/shard_map/ppermute | solution.py:882
  219.9 20.2 %collective-permute-start.45 = (bf16[2,2,48,768]{3,2,1,0:T(8,128)(2,1)S(1)}, bf16[2,2,48,768]{3,2,1,0:T(8,128)(2,1)S(1)}, u32[]{:S(2)}, u32[]{:S(2)}) collective-permute-start(bf16[2,2,48,768]{3,2,1,0:T(8,128)(2,1)S(1)} %get-tuple-element.326), channel_id=1, source_target_pairs={{0,4},{4,0},{8,12},{12,8},{16,20},{20,16},{24,28},{28,24},{1,5},{5... | collective-permute-start | bytes 884744 | tf_op jit(solution)/shard_map/ppermute | solution.py:882
  221.1 19.0 %collective-permute-start.46 = (bf16[2,2,48,768]{3,2,1,0:T(8,128)(2,1)S(1)}, bf16[2,2,48,768]{3,2,1,0:T(8,128)(2,1)S(1)}, u32[]{:S(2)}, u32[]{:S(2)}) collective-permute-start(bf16[2,2,48,768]{3,2,1,0:T(8,128)(2,1)S(1)} %get-tuple-element.319), channel_id=1, source_target_pairs={{0,2},{1,3},{2,0},{3,1},{4,6},{5,7},{6,4},{7,5},{8,10},{9,11},{10,... | collective-permute-start | bytes 884744 | tf_op jit(solution)/shard_map/ppermute | solution.py:882
  241.1 17.9 %collective-permute-start.50 = (bf16[2,2,48,768]{3,2,0,1:T(8,128)(2,1)S(1)}, bf16[2,2,48,768]{3,2,0,1:T(8,128)(2,1)S(1)}, u32[]{:S(2)}, u32[]{:S(2)}) collective-permute-start(bf16[2,2,48,768]{3,2,0,1:T(8,128)(2,1)S(1)} %get-tuple-element.335), channel_id=1, source_target_pairs={{0,8},{4,12},{8,0},{12,4},{16,24},{20,28},{24,16},{28,20},{1,9},{5... | collective-permute-start | bytes 884744 | tf_op jit(solution)/shard_map/ppermute | solution.py:882
  242.5 19.3 %collective-permute-start.48 = (bf16[2,2,2,128,384]{4,3,2,1,0:T(8,128)(2,1)}, bf16[2,2,2,128,384]{4,3,2,1,0:T(8,128)(2,1)S(1)}, u32[]{:S(2)}, u32[]{:S(2)}) collective-permute-start(bf16[2,2,2,128,384]{4,3,2,1,0:T(8,128)(2,1)} %get-tuple-element.209), channel_id=1, source_target_pairs={{0,2},{1,3},{2,0},{3,1},{4,6},{5,7},{6,4},{7,5},{8,10},{9,11},{10,... | collective-permute-start | bytes 2359304 | tf_op jit(solution)/shard_map/ppermute | solution.py:882
  243.1 19.1 %collective-permute-start.49 = (bf16[2,2,2,128,384]{4,3,2,1,0:T(8,128)(2,1)}, bf16[2,2,2,128,384]{4,3,2,1,0:T(8,128)(2,1)}, u32[]{:S(2)}, u32[]{:S(2)}) collective-permute-start(bf16[2,2,2,128,384]{4,3,2,1,0:T(8,128)(2,1)} %get-tuple-element.210), channel_id=1, source_target_pairs={{0,4},{4,0},{8,12},{12,8},{16,20},{20,16},{24,28},{28,24},{1,5},{5... | collective-permute-start | bytes 2359304 | tf_op jit(solution)/shard_map/ppermute | solution.py:882
  249.0 15.6 %collective-permute-start.47 = (bf16[2,2,2,2,144,384]{5,4,3,2,1,0:T(8,128)(2,1)}, bf16[2,2,2,2,144,384]{5,4,3,2,1,0:T(8,128)(2,1)}, u32[]{:S(2)}, u32[]{:S(2)}) collective-permute-start(bf16[2,2,2,2,144,384]{5,4,3,2,1,0:T(8,128)(2,1)} %grad_att.4.refs_0_), channel_id=1, source_target_pairs={{0,1},{1,0},{2,3},{3,2},{4,5},{5,4},{6,7},{7,6},{8,9},{9,8},{10,11... | collective-permute-start | bytes 5308424 | tf_op jit(solution)/shard_map/ppermute | solution.py:882
  274.2 26.3 %collective-permute-start.51 = (bf16[2,2,2,2,144,384]{5,4,3,2,1,0:T(8,128)(2,1)}, bf16[2,2,2,2,144,384]{5,4,3,2,1,0:T(8,128)(2,1)}, u32[]{:S(2)}, u32[]{:S(2)}) collective-permute-start(bf16[2,2,2,2,144,384]{5,4,3,2,1,0:T(8,128)(2,1)} %grad_att.6.refs_1_), channel_id=1, source_target_pairs={{0,1},{1,0},{2,3},{3,2},{4,5},{5,4},{6,7},{7,6},{8,9},{9,8},{10,11... | collective-permute-start | bytes 5308424 | tf_op jit(solution)/shard_map/ppermute | solution.py:882
  291.2 19.0 %collective-permute-start.52 = (bf16[2,2,144,384]{3,2,1,0:T(8,128)(2,1)}, bf16[2,2,144,384]{3,2,1,0:T(8,128)(2,1)}, u32[]{:S(2)}, u32[]{:S(2)}) collective-permute-start(bf16[2,2,144,384]{3,2,1,0:T(8,128)(2,1)} %get-tuple-element.222), channel_id=1, source_target_pairs={{0,2},{1,3},{2,0},{3,1},{4,6},{5,7},{6,4},{7,5},{8,10},{9,11},{10,... | collective-permute-start | bytes 1327112 | tf_op jit(solution)/shard_map/ppermute | solution.py:882
  292.0 18.2 %collective-permute-start.53 = (bf16[2,2,144,384]{3,2,1,0:T(8,128)(2,1)}, bf16[2,2,144,384]{3,2,1,0:T(8,128)(2,1)}, u32[]{:S(2)}, u32[]{:S(2)}) collective-permute-start(bf16[2,2,144,384]{3,2,1,0:T(8,128)(2,1)} %get-tuple-element.223), channel_id=1, source_target_pairs={{0,4},{4,0},{8,12},{12,8},{16,20},{20,16},{24,28},{28,24},{1,5},{5... | collective-permute-start | bytes 1327112 | tf_op jit(solution)/shard_map/ppermute | solution.py:882
  300.3 23.1 %collective-permute-start.65 = (bf16[2,2,128,384]{3,2,0,1:T(8,128)(2,1)}, bf16[2,2,128,384]{3,2,0,1:T(8,128)(2,1)}, u32[]{:S(2)}, u32[]{:S(2)}) collective-permute-start(bf16[2,2,128,384]{3,2,0,1:T(8,128)(2,1)} %fusion.24), channel_id=1, source_target_pairs={{0,8},{4,12},{8,0},{12,4},{16,24},{20,28},{24,16},{28,20},{1,9},{5... | collective-permute-start | bytes 1179656 | tf_op jit(solution)/shard_map/ppermute | solution.py:882
  305.6 31.8 %collective-permute-start.57 = (bf16[2,2,144,384]{3,2,1,0:T(8,128)(2,1)}, bf16[2,2,144,384]{3,2,1,0:T(8,128)(2,1)}, u32[]{:S(2)}, u32[]{:S(2)}) collective-permute-start(bf16[2,2,144,384]{3,2,1,0:T(8,128)(2,1)} %get-tuple-element.228), channel_id=1, source_target_pairs={{0,2},{1,3},{2,0},{3,1},{4,6},{5,7},{6,4},{7,5},{8,10},{9,11},{10,... | collective-permute-start | bytes 1327112 | tf_op jit(solution)/shard_map/ppermute | solution.py:882
  306.6 30.8 %collective-permute-start.58 = (bf16[2,2,144,384]{3,2,1,0:T(8,128)(2,1)}, bf16[2,2,144,384]{3,2,1,0:T(8,128)(2,1)}, u32[]{:S(2)}, u32[]{:S(2)}) collective-permute-start(bf16[2,2,144,384]{3,2,1,0:T(8,128)(2,1)} %get-tuple-element.229), channel_id=1, source_target_pairs={{0,4},{4,0},{8,12},{12,8},{16,20},{20,16},{24,28},{28,24},{1,5},{5... | collective-permute-start | bytes 1327112 | tf_op jit(solution)/shard_map/ppermute | solution.py:882
  312.2 27.7 %collective-permute-start.54 = (bf16[2,144,384]{2,1,0:T(8,128)(2,1)}, bf16[2,144,384]{2,1,0:T(8,128)(2,1)S(1)}, u32[]{:S(2)}, u32[]{:S(2)}) collective-permute-start(bf16[2,144,384]{2,1,0:T(8,128)(2,1)} %get-tuple-element.332), channel_id=1, source_target_pairs={{0,4},{4,0},{8,12},{12,8},{16,20},{20,16},{24,28},{28,24},{1,5},{5... | collective-permute-start | bytes 663560 | tf_op jit(solution)/shard_map/ppermute | solution.py:882
  313.3 26.7 %collective-permute-start.55 = (bf16[2,144,384]{2,1,0:T(8,128)(2,1)}, bf16[2,144,384]{2,1,0:T(8,128)(2,1)S(1)}, u32[]{:S(2)}, u32[]{:S(2)}) collective-permute-start(bf16[2,144,384]{2,1,0:T(8,128)(2,1)} %get-tuple-element.331), channel_id=1, source_target_pairs={{0,2},{1,3},{2,0},{3,1},{4,6},{5,7},{6,4},{7,5},{8,10},{9,11},{10,... | collective-permute-start | bytes 663560 | tf_op jit(solution)/shard_map/ppermute | solution.py:882
  (86 other events, 694.3 us)
Sparse Core Ops, SparseCore 0:
  280.2 54.7 all-gather.2
